TPU v7x, 32 devices: a whole 2x2x4 slice. The times are simulated.
32 devices in a mesh: asc: 8 (over y, x, core), desc: 4 (over z).
Axes of the slice: x: 2, y: 2, z: 4, core: 2. Of those that a mesh axis runs over, the one named last changes fastest.
Arguments:
- coef_asc: float32 [1024, 128], P(('asc', 'desc')), may hold values from -0.3 to 0.3
- coef_desc: float32 [1024, 128], P(('asc', 'desc')), may hold values from -0.3 to 0.3
- cross_asc: int32 [2048, 128], P(('asc', 'desc')), may hold values from 0 to 1023, as said below
- cross_desc: int32 [2048, 128], P(('asc', 'desc')), may hold values from 0 to 1023, as said below
- time_asc: float32 [2048, 128], P(('asc', 'desc')), may hold values from 0 to 1
- time_desc: float32 [2048, 128], P(('asc', 'desc')), may hold values from 0 to 1
- height: float32 [2048, 128], P(('asc', 'desc')), may hold values from -18 to 18
- block_fill: int32 [2048], P(('asc', 'desc')), may hold values from 0 to 128, as said below
Outputs:
- adjusted_asc: float32 [1024, 128], P(('asc', 'desc'))
- adjusted_desc: float32 [1024, 128], P(('asc', 'desc'))
Inputs may be any that keep to these rules, and one draw needn't show every extreme that they name: `cross_asc`: every crossover slot stored on a device of asc index p names an ascending arc a with a // 128 == p; slot s of every block names an arc a with (a // 32) % 4 == s % 4. `cross_desc`: every crossover slot stored on a device of desc index q names a descending arc d with (d // 32) % 4 == q; slot s of every block names an arc d with d // 128 == s % 8. `block_fill`: the slots in use stand first in each block; on each device the blocks with a nonzero count stand first and the first block is full; on some device all 64 blocks are in use.
All inputs are finite; a program needn't handle non-finite values.
Results may differ from a plain program's by a relative error of at most 0.0003.
Values sent between devices are 32-bit elements; how exact they have to be, the bound alone decides.
No kernel may reach another device: no remote copies, remote signals or barrier semaphores. Data moves between devices by JAX's collectives and lax.ppermute only.
A program may use at most 64 MiB of HBM per device.

v0:
```python
import jax
import jax.numpy as jnp
from jax import lax
from jax.sharding import PartitionSpec as P

GN_STEPS = 2
CG_STEPS = 3


damping = 2.0
cauchy_square = 2.25


def harmonics(times, term_count):
    half_terms = term_count // 2
    frequency = (lax.iota(jnp.int32, half_terms) + 1).astype(jnp.float32)
    phases = jnp.pi * times[:, None] * frequency[None, :]
    return jnp.concatenate([jnp.cos(phases), jnp.sin(phases)], axis=1)


def one_hot(ids, count):
    return (ids[:, None] == lax.iota(jnp.int32, count)[None, :]).astype(jnp.float32)


def pick_rows(selector, field):
    return jnp.dot(
        selector, field, precision=lax.Precision.HIGHEST, preferred_element_type=jnp.float32
    )


def collect_rows(selector, terms):
    return lax.dot_general(
        selector,
        terms,
        (((0,), (0,)), ((), ())),
        precision=lax.Precision.HIGHEST,
        preferred_element_type=jnp.float32,
    )


def residual_react(modelled, observed, live_mask, previous):
    misfit = live_mask * (observed - modelled)
    weight = live_mask / (1.0 + misfit * misfit / cauchy_square)
    return (weight * misfit, weight, jnp.zeros((), jnp.float32))


def image_react(modelled, observed, live_mask, previous):
    weighted = previous * modelled
    curve_part = jnp.zeros((), jnp.float32)
    return (weighted, previous, curve_part)


def norm_total(value):
    return lax.psum(value, ("asc", "desc"))


def curve_total(value):
    return lax.psum(value, ("asc", "desc"))


def body(coef_asc, coef_desc, cross_asc, cross_desc, time_asc, time_desc, height, block_fill):
    owned_asc, term_count = coef_asc.shape
    owned_desc = coef_desc.shape[0]
    blocks, block_width = cross_asc.shape
    count_asc = lax.axis_size("asc")
    count_desc = lax.axis_size("desc")
    position = lax.broadcasted_iota(jnp.int32, (blocks, block_width), 1)
    live_plain = (position < block_fill[:, None]).astype(jnp.float32)
    cols_asc = block_width // count_desc
    cols_desc = block_width // count_asc
    ids_send_asc = (cross_asc % owned_asc).astype(jnp.float32).reshape(blocks, cols_asc, count_desc)
    got_ids_asc, got_times_asc = (
        lax.all_to_all(ids_send_asc, "desc", split_axis=2, concat_axis=2, tiled=True),
        lax.all_to_all(
            time_asc.reshape(blocks, cols_asc, count_desc),
            "desc",
            split_axis=2,
            concat_axis=2,
            tiled=True,
        ),
    )
    ids_send_desc = (
        (cross_desc % owned_desc).astype(jnp.float32).reshape(blocks, cols_desc, count_asc)
    )
    got_ids_desc, got_times_desc = (
        lax.all_to_all(ids_send_desc, "asc", split_axis=2, concat_axis=2, tiled=True),
        lax.all_to_all(
            time_desc.reshape(blocks, cols_desc, count_asc),
            "asc",
            split_axis=2,
            concat_axis=2,
            tiled=True,
        ),
    )
    select_asc = one_hot(got_ids_asc.reshape(-1).astype(jnp.int32), owned_asc)
    select_desc = one_hot(got_ids_desc.reshape(-1).astype(jnp.int32), owned_desc)
    holder_basis_asc = harmonics(got_times_asc.reshape(-1), term_count)
    holder_basis_desc = harmonics(got_times_desc.reshape(-1), term_count)
    state_asc, state_desc = (coef_asc, coef_desc)
    keep_asc = jnp.float32(1.0)
    keep_desc = jnp.float32(1.0)
    empty_weights = jnp.zeros((blocks, block_width), jnp.float32)

    def crossing(field_asc, field_desc, react, weights):
        value_asc = jnp.sum(holder_basis_asc * pick_rows(select_asc, field_asc), axis=1)
        value_desc = jnp.sum(holder_basis_desc * pick_rows(select_desc, field_desc), axis=1)
        back_asc = lax.all_to_all(
            value_asc.reshape(blocks, cols_asc, count_desc),
            "desc",
            split_axis=2,
            concat_axis=2,
            tiled=True,
        ).reshape(blocks, block_width)
        back_desc = lax.all_to_all(
            value_desc.reshape(blocks, cols_desc, count_asc),
            "asc",
            split_axis=2,
            concat_axis=2,
            tiled=True,
        ).reshape(blocks, block_width)
        weighted, weight, curve_part = react(back_asc - back_desc, height, live_plain, weights)
        out_asc = lax.all_to_all(
            weighted.reshape(blocks, cols_asc, count_desc),
            "desc",
            split_axis=2,
            concat_axis=2,
            tiled=True,
        ).reshape(-1)
        out_desc = lax.all_to_all(
            weighted.reshape(blocks, cols_desc, count_asc),
            "asc",
            split_axis=2,
            concat_axis=2,
            tiled=True,
        ).reshape(-1)
        grad_asc = collect_rows(select_asc, out_asc[:, None] * holder_basis_asc)
        grad_desc = -collect_rows(select_desc, out_desc[:, None] * holder_basis_desc)
        return (grad_asc, grad_desc, curve_part, weight)

    def inner_sum(first, second):
        return keep_asc * jnp.sum(first[0] * second[0]) + keep_desc * jnp.sum(first[1] * second[1])

    for outer_step in range(GN_STEPS):
        grad_asc, grad_desc, unused, weights = crossing(
            state_asc, state_desc, residual_react, empty_weights
        )
        remainder = (grad_asc - damping * state_asc, grad_desc - damping * state_desc)
        direction = remainder
        step_sum = (jnp.zeros_like(state_asc), jnp.zeros_like(state_desc))
        norm_now = norm_total(inner_sum(remainder, remainder))
        for inner_step in range(CG_STEPS):
            image_asc, image_desc, curve_part, kept = crossing(
                direction[0], direction[1], image_react, weights
            )
            image_pair = (image_asc + damping * direction[0], image_desc + damping * direction[1])
            curvature = curve_total(inner_sum(direction, image_pair))
            step_length = norm_now / curvature
            step_sum = (
                step_sum[0] + step_length * direction[0],
                step_sum[1] + step_length * direction[1],
            )
            if inner_step + 1 < CG_STEPS:
                remainder = (
                    remainder[0] - step_length * image_pair[0],
                    remainder[1] - step_length * image_pair[1],
                )
                norm_next = norm_total(inner_sum(remainder, remainder))
                ratio = norm_next / norm_now
                direction = (
                    remainder[0] + ratio * direction[0],
                    remainder[1] + ratio * direction[1],
                )
                norm_now = norm_next
        state_asc = state_asc + step_sum[0]
        state_desc = state_desc + step_sum[1]
    result_asc, result_desc = (state_asc, state_desc)
    return (result_asc, result_desc)


def solution(mesh):
    placed = (
        P(("asc", "desc"), None),
        P(("asc", "desc"), None),
        P(("asc", "desc"), None),
        P(("asc", "desc"), None),
        P(("asc", "desc"), None),
        P(("asc", "desc"), None),
        P(("asc", "desc"), None),
        P(("asc", "desc")),
    )
    return jax.shard_map(
        body,
        mesh=mesh,
        in_specs=placed,
        out_specs=(P(("asc", "desc"), None), P(("asc", "desc"), None)),
        check_vma=False,
    )
```

profile of v0, /device:TPU:0, one launch (start us, length us, event | category | flops | bytes accessed | tf_op | source)
XLA Modules:
  0.0 910.7 jit_solution(15668624906101091482)
XLA Ops:
  2.2 5.2 all-to-all-start.3
  21.2 4.9 all-to-all-start
  43.1 15.6 %multiply_cosine_fusion = (f32[8192,64]{0,1:T(8,128)S(1)}, f32[8192,64]{0,1:T(8,128)S(1)}, f32[8192,64]{0,1:T(8,128)S(1)}, f32[8192,64]{0,1:T(8,128)}) fusion(f32[8192]{0:T(1024)S(1)} %mul.551, f32[64]{0:T(128)S(1)} %add_convert_fusion, f32[8192]{0:T(1024)S(1)} %mul.545), kind=kLoop, calls=%fused_computation.51 | loop fusion | flops 1048576 | bytes 8454400 | tf_op jit(solution)/shard_map/cos | solution.py:18
  97.9 4.8 fusion.70
  121.1 5.1 all-to-all-start.8
  127.0 4.9 all-to-all-done.8
  147.3 5.3 multiply_reduce_fusion.16
  162.2 39.9 %all-reduce.1 = (f32[]{:T(128)}, f32[]{:T(128)}) all-reduce(f32[]{:T(128)S(6)} %add.186, f32[]{:T(128)S(6)} %add.189), channel_id=1, replica_groups=mesh['asc'=8,'desc'=4] {'asc','desc'}, use_global_device_ids=true, to_apply=%region_4.5 | all-reduce | flops 2 | bytes 16 | tf_op jit(solution)/shard_map/psum | solution.py:54
  206.0 40.3 %psum.86 = f32[]{:T(128)} all-reduce(f32[]{:T(128)S(6)} %add.190), channel_id=1, replica_groups=mesh['asc'=8,'desc'=4] {'asc','desc'}, use_global_device_ids=true, to_apply=%region_12.13 | all-reduce | flops 1 | bytes 8 | tf_op jit(solution)/shard_map/psum | solution.py:54
  253.1 5.0 all-to-all-start.13
  268.4 4.9 all-to-all-done.12
  288.6 5.3 multiply_reduce_fusion.12
  302.2 39.8 %psum.87 = f32[]{:T(128)} all-reduce(f32[]{:T(128)S(6)} %add.195), channel_id=1, replica_groups=mesh['asc'=8,'desc'=4] {'asc','desc'}, use_global_device_ids=true, to_apply=%region_17.18 | all-reduce | flops 1 | bytes 8 | tf_op jit(solution)/shard_map/psum | solution.py:58
  345.9 40.6 %psum.88 = f32[]{:T(128)} all-reduce(f32[]{:T(128)S(6)} %add.197), channel_id=1, replica_groups=mesh['asc'=8,'desc'=4] {'asc','desc'}, use_global_device_ids=true, to_apply=%region_20.21 | all-reduce | flops 1 | bytes 8 | tf_op jit(solution)/shard_map/psum | solution.py:54
  408.4 4.9 all-to-all-done.16
  428.7 5.3 fusion.154
  442.4 39.8 %psum.89 = f32[]{:T(128)} all-reduce(f32[]{:T(128)S(6)} %add.202), channel_id=1, replica_groups=mesh['asc'=8,'desc'=4] {'asc','desc'}, use_global_device_ids=true, to_apply=%region_25.26 | all-reduce | flops 1 | bytes 8 | tf_op jit(solution)/shard_map/psum | solution.py:58
  503.5 4.9 all-to-all-done.20
  523.7 4.8 fusion.112
  546.9 5.0 all-to-all-start.24
  552.8 4.9 all-to-all-done.24
  573.1 5.4 multiply_reduce_fusion.6
  588.1 39.9 %all-reduce = (f32[]{:T(128)}, f32[]{:T(128)}) all-reduce(f32[]{:T(128)S(6)} %add.209, f32[]{:T(128)S(6)} %add.212), channel_id=1, replica_groups=mesh['asc'=8,'desc'=4] {'asc','desc'}, use_global_device_ids=true, to_apply=%region_30.31 | all-reduce | flops 2 | bytes 16 | tf_op jit(solution)/shard_map/psum | solution.py:54
  631.6 40.2 %psum.92 = f32[]{:T(128)} all-reduce(f32[]{:T(128)S(6)} %add.213), channel_id=1, replica_groups=mesh['asc'=8,'desc'=4] {'asc','desc'}, use_global_device_ids=true, to_apply=%region_38.39 | all-reduce | flops 1 | bytes 8 | tf_op jit(solution)/shard_map/psum | solution.py:54
  678.6 4.9 all-to-all-start.29
  693.9 4.9 all-to-all-done.28
  714.1 5.4 multiply_reduce_fusion.2
  727.8 39.8 %psum.93 = f32[]{:T(128)} all-reduce(f32[]{:T(128)S(6)} %add.218), channel_id=1, replica_groups=mesh['asc'=8,'desc'=4] {'asc','desc'}, use_global_device_ids=true, to_apply=%region_43.44 | all-reduce | flops 1 | bytes 8 | tf_op jit(solution)/shard_map/psum | solution.py:58
  771.3 40.5 %psum.94 = f32[]{:T(128)} all-reduce(f32[]{:T(128)S(6)} %add.220), channel_id=1, replica_groups=mesh['asc'=8,'desc'=4] {'asc','desc'}, use_global_device_ids=true, to_apply=%region_46.47 | all-reduce | flops 1 | bytes 8 | tf_op jit(solution)/shard_map/psum | solution.py:54
  833.6 4.9 all-to-all-done.32
  854.1 5.4 fusion.148
  867.8 39.8 %psum.95 = f32[]{:T(128)} all-reduce(f32[]{:T(128)S(6)} %add.225), channel_id=1, replica_groups=mesh['asc'=8,'desc'=4] {'asc','desc'}, use_global_device_ids=true, to_apply=%region_51.52 | all-reduce | flops 1 | bytes 8 | tf_op jit(solution)/shard_map/psum | solution.py:58
  (365 shorter events, 358.2 us)
Async XLA Ops:
  2.2 10.0 %all-to-all-start.3 = ((f32[8,1,1024]{2,1,0:T(1,128)}), f32[8,1,1024]{2,1,0:T(1,128)S(1)}, u32[]{:S(2)}, u32[]{:S(2)}) async-start(f32[8,1,1024]{2,1,0:T(1,128)} %reshape.274), calls=%async_computation.3 | async-start | bytes 65536 | tf_op jit(solution)/shard_map/all_to_all | solution.py:87
  12.2 9.0 all-to-all-start.4
  21.2 10.5 %all-to-all-start = ((f32[4,1,2048]{2,1,0:T(1,128)}), f32[4,1,2048]{2,1,0:T(1,128)S(1)}, u32[]{:S(2)}, u32[]{:S(2)}) async-start(f32[4,1,2048]{2,1,0:T(1,128)} %reshape.266), calls=%async_computation | async-start | bytes 65536 | tf_op jit(solution)/shard_map/all_to_all | solution.py:73
  64.1 9.6 %all-to-all-start.5 = ((f32[8,1,1024]{2,1,0:T(1,128)}), f32[8,1,1024]{2,1,0:T(1,128)S(1)}, u32[]{:S(2)}, u32[]{:S(2)}) async-start(f32[8,1,1024]{2,1,0:T(1,128)} %reshape.276), calls=%async_computation.5 | async-start | bytes 65536 | tf_op jit(solution)/shard_map/all_to_all | solution.py:114
  93.3 12.9 %all-to-all-start.6 = ((f32[4,1,2048]{2,1,0:T(1,128)}), f32[4,1,2048]{2,1,0:T(1,128)S(1)}, u32[]{:S(2)}, u32[]{:S(2)}) async-start(f32[4,1,2048]{2,1,0:T(1,128)} %reshape.278), calls=%async_computation.6 | async-start | bytes 65536 | tf_op jit(solution)/shard_map/all_to_all | solution.py:122
  106.2 15.0 %all-to-all-start.9 = ((f32[8,1,1024]{2,1,0:T(1,128)}), f32[8,1,1024]{2,1,0:T(1,128)S(1)}, u32[]{:S(2)}, u32[]{:S(2)}) async-start(f32[8,1,1024]{2,1,0:T(1,128)} %reshape.284), calls=%async_computation.9 | async-start | bytes 65536 | tf_op jit(solution)/shard_map/all_to_all | solution.py:114
  121.1 10.7 %all-to-all-start.8 = ((f32[4,1,2048]{2,1,0:T(1,128)}), f32[4,1,2048]{2,1,0:T(1,128)S(1)}, u32[]{:S(2)}, u32[]{:S(2)}) async-start(f32[4,1,2048]{2,1,0:T(1,128)} %reshape.280), calls=%async_computation.8 | async-start | bytes 65536 | tf_op jit(solution)/shard_map/all_to_all | solution.py:107
  133.5 9.0 all-to-all-start.11
  142.5 10.1 %all-to-all-start.10 = ((f32[4,1,2048]{2,1,0:T(1,128)}), f32[4,1,2048]{2,1,0:T(1,128)S(1)}, u32[]{:S(2)}, u32[]{:S(2)}) async-start(f32[4,1,2048]{2,1,0:T(1,128)} %reshape.286), calls=%async_computation.10 | async-start | bytes 65536 | tf_op jit(solution)/shard_map/all_to_all | solution.py:122
  253.1 11.0 %all-to-all-start.13 = ((f32[8,1,1024]{2,1,0:T(1,128)}), f32[8,1,1024]{2,1,0:T(1,128)S(1)}, u32[]{:S(2)}, u32[]{:S(2)}) async-start(f32[8,1,1024]{2,1,0:T(1,128)} %reshape.292), calls=%async_computation.13 | async-start | bytes 65536 | tf_op jit(solution)/shard_map/all_to_all | solution.py:114
  264.0 9.2 %all-to-all-start.12 = ((f32[4,1,2048]{2,1,0:T(1,128)}), f32[4,1,2048]{2,1,0:T(1,128)S(1)}, u32[]{:S(2)}, u32[]{:S(2)}) async-start(f32[4,1,2048]{2,1,0:T(1,128)} %reshape.290), calls=%async_computation.12 | async-start | bytes 65536 | tf_op jit(solution)/shard_map/all_to_all | solution.py:107
  274.9 9.0 all-to-all-start.15
  284.0 10.0 %all-to-all-start.14 = ((f32[4,1,2048]{2,1,0:T(1,128)}), f32[4,1,2048]{2,1,0:T(1,128)S(1)}, u32[]{:S(2)}, u32[]{:S(2)}) async-start(f32[4,1,2048]{2,1,0:T(1,128)} %reshape.294), calls=%async_computation.14 | async-start | bytes 65536 | tf_op jit(solution)/shard_map/all_to_all | solution.py:122
  393.3 10.7 %all-to-all-start.17 = ((f32[8,1,1024]{2,1,0:T(1,128)}), f32[8,1,1024]{2,1,0:T(1,128)S(1)}, u32[]{:S(2)}, u32[]{:S(2)}) async-start(f32[8,1,1024]{2,1,0:T(1,128)} %reshape.300), calls=%async_computation.17 | async-start | bytes 65536 | tf_op jit(solution)/shard_map/all_to_all | solution.py:114
  404.0 9.3 %all-to-all-start.16 = ((f32[4,1,2048]{2,1,0:T(1,128)}), f32[4,1,2048]{2,1,0:T(1,128)S(1)}, u32[]{:S(2)}, u32[]{:S(2)}) async-start(f32[4,1,2048]{2,1,0:T(1,128)} %reshape.298), calls=%async_computation.16 | async-start | bytes 65536 | tf_op jit(solution)/shard_map/all_to_all | solution.py:107
  414.9 9.0 all-to-all-start.19
  423.9 10.1 %all-to-all-start.18 = ((f32[4,1,2048]{2,1,0:T(1,128)}), f32[4,1,2048]{2,1,0:T(1,128)S(1)}, u32[]{:S(2)}, u32[]{:S(2)}) async-start(f32[4,1,2048]{2,1,0:T(1,128)} %reshape.302), calls=%async_computation.18 | async-start | bytes 65536 | tf_op jit(solution)/shard_map/all_to_all | solution.py:122
  489.1 10.1 %all-to-all-start.21 = ((f32[8,1,1024]{2,1,0:T(1,128)}), f32[8,1,1024]{2,1,0:T(1,128)S(1)}, u32[]{:S(2)}, u32[]{:S(2)}) async-start(f32[8,1,1024]{2,1,0:T(1,128)} %reshape.308), calls=%async_computation.21 | async-start | bytes 65536 | tf_op jit(solution)/shard_map/all_to_all | solution.py:114
  499.1 9.2 %all-to-all-start.20 = ((f32[4,1,2048]{2,1,0:T(1,128)}), f32[4,1,2048]{2,1,0:T(1,128)S(1)}, u32[]{:S(2)}, u32[]{:S(2)}) async-start(f32[4,1,2048]{2,1,0:T(1,128)} %reshape.306), calls=%async_computation.20 | async-start | bytes 65536 | tf_op jit(solution)/shard_map/all_to_all | solution.py:107
  510.0 9.0 all-to-all-start.23
  519.1 12.9 %all-to-all-start.22 = ((f32[4,1,2048]{2,1,0:T(1,128)}), f32[4,1,2048]{2,1,0:T(1,128)S(1)}, u32[]{:S(2)}, u32[]{:S(2)}) async-start(f32[4,1,2048]{2,1,0:T(1,128)} %reshape.310), calls=%async_computation.22 | async-start | bytes 65536 | tf_op jit(solution)/shard_map/all_to_all | solution.py:122
  532.0 14.9 %all-to-all-start.25 = ((f32[8,1,1024]{2,1,0:T(1,128)}), f32[8,1,1024]{2,1,0:T(1,128)S(1)}, u32[]{:S(2)}, u32[]{:S(2)}) async-start(f32[8,1,1024]{2,1,0:T(1,128)} %reshape.316), calls=%async_computation.25 | async-start | bytes 65536 | tf_op jit(solution)/shard_map/all_to_all | solution.py:114
  546.9 10.7 %all-to-all-start.24 = ((f32[4,1,2048]{2,1,0:T(1,128)}), f32[4,1,2048]{2,1,0:T(1,128)S(1)}, u32[]{:S(2)}, u32[]{:S(2)}) async-start(f32[4,1,2048]{2,1,0:T(1,128)} %reshape.312), calls=%async_computation.24 | async-start | bytes 65536 | tf_op jit(solution)/shard_map/all_to_all | solution.py:107
  568.3 10.2 %all-to-all-start.26 = ((f32[4,1,2048]{2,1,0:T(1,128)}), f32[4,1,2048]{2,1,0:T(1,128)S(1)}, u32[]{:S(2)}, u32[]{:S(2)}) async-start(f32[4,1,2048]{2,1,0:T(1,128)} %reshape.318), calls=%async_computation.26 | async-start | bytes 65536 | tf_op jit(solution)/shard_map/all_to_all | solution.py:122
  678.6 10.9 %all-to-all-start.29 = ((f32[8,1,1024]{2,1,0:T(1,128)}), f32[8,1,1024]{2,1,0:T(1,128)S(1)}, u32[]{:S(2)}, u32[]{:S(2)}) async-start(f32[8,1,1024]{2,1,0:T(1,128)} %reshape.324), calls=%async_computation.29 | async-start | bytes 65536 | tf_op jit(solution)/shard_map/all_to_all | solution.py:114
  689.5 9.2 %all-to-all-start.28 = ((f32[4,1,2048]{2,1,0:T(1,128)}), f32[4,1,2048]{2,1,0:T(1,128)S(1)}, u32[]{:S(2)}, u32[]{:S(2)}) async-start(f32[4,1,2048]{2,1,0:T(1,128)} %reshape.322), calls=%async_computation.28 | async-start | bytes 65536 | tf_op jit(solution)/shard_map/all_to_all | solution.py:107
  700.4 9.0 all-to-all-start.31
  709.4 10.0 %all-to-all-start.30 = ((f32[4,1,2048]{2,1,0:T(1,128)}), f32[4,1,2048]{2,1,0:T(1,128)S(1)}, u32[]{:S(2)}, u32[]{:S(2)}) async-start(f32[4,1,2048]{2,1,0:T(1,128)} %reshape.326), calls=%async_computation.30 | async-start | bytes 65536 | tf_op jit(solution)/shard_map/all_to_all | solution.py:122
  818.5 10.7 %all-to-all-start.33 = ((f32[8,1,1024]{2,1,0:T(1,128)}), f32[8,1,1024]{2,1,0:T(1,128)S(1)}, u32[]{:S(2)}, u32[]{:S(2)}) async-start(f32[8,1,1024]{2,1,0:T(1,128)} %reshape.332), calls=%async_computation.33 | async-start | bytes 65536 | tf_op jit(solution)/shard_map/all_to_all | solution.py:114
  829.2 9.2 %all-to-all-start.32 = ((f32[4,1,2048]{2,1,0:T(1,128)}), f32[4,1,2048]{2,1,0:T(1,128)S(1)}, u32[]{:S(2)}, u32[]{:S(2)}) async-start(f32[4,1,2048]{2,1,0:T(1,128)} %reshape.330), calls=%async_computation.32 | async-start | bytes 65536 | tf_op jit(solution)/shard_map/all_to_all | solution.py:107
  840.1 9.0 all-to-all-start.35
  849.1 10.3 %all-to-all-start.34 = ((f32[4,1,2048]{2,1,0:T(1,128)}), f32[4,1,2048]{2,1,0:T(1,128)S(1)}, u32[]{:S(2)}, u32[]{:S(2)}) async-start(f32[4,1,2048]{2,1,0:T(1,128)} %reshape.334), calls=%async_computation.34 | async-start | bytes 65536 | tf_op jit(solution)/shard_map/all_to_all | solution.py:122
  (21 other events, 447.8 us)
where the time goes:
time: 924 us; the launch traced here: 911 us
  blocking collectives  401 us (43%)
  starting transfers between devices  143 us (15%)
  matrix products  131 us (14%)
  waiting for transfers between devices  82.2 us (9%)
  local copies, waits for them, and re-layouts  74.8 us (8%)
  other arithmetic  48.4 us (5%)
  between operations  30.4 us (3%)
    psum x6, blocking collectives, norm_total(): return lax.psum(value, ('asc', 'desc'))  241 us
    psum x4, blocking collectives, curve_total(): return lax.psum(value, ('asc', 'desc'))  159 us
    dot_general x16, matrix products, collect_rows(): lax.dot_general(selector, terms, (((0,), (0,)), ((), ())), precision=lax....  78.1 us
    dot_general x16, matrix products, pick_rows(): jnp.dot(selector, field, precision=lax.Precision.HIGHEST, preferred_eleme...  52.6 us
    all_to_all x8, waiting for transfers between devices, crossing(): lax.all_to_all(value_asc.reshape(blocks, cols_asc, count_desc), 'desc', s...  38.7 us
    all_to_all x8, starting transfers between devices, crossing(): lax.all_to_all(value_desc.reshape(blocks, cols_desc, count_asc), 'asc', s...  34.3 us
    unnamed x111, local copies, waits for them, and re-layouts  34.1 us
    all_to_all x8, starting transfers between devices, crossing(): lax.all_to_all(weighted.reshape(blocks, cols_desc, count_asc), 'asc', spl...  33.5 us
  transfers between devices with their start and end apart: 36, of which 19 were waited for; matrix products, arithmetic and copies ran while one was open for 15% of the time, Pallas kernels for 0%

commit v1 on v0

v1 whole, which is shorter than its diff:
```python
import functools
import math

import jax
import jax.numpy as jnp
from jax import lax
from jax.experimental import pallas as pl
from jax.experimental.pallas import tpu as pltpu
from jax.sharding import PartitionSpec as P

GN_STEPS = 2
damping = 2.0
cauchy_square = 2.25

LANES = 128
STEP_ROWS = 2
UNROLL = 2
SCALE = 1.0 / 128.0
FIELDS = 6
PIVOT_FLOOR = 1e-6
F32 = jnp.float32
BF16 = jnp.bfloat16

COS_TERMS = [(-1.0) ** i * math.pi ** (2 * i) / math.factorial(2 * i) for i in range(8)]
SIN_TERMS = [(-1.0) ** i * math.pi ** (2 * i + 1) / math.factorial(2 * i + 1) for i in range(7)]


def params():
    return pltpu.CompilerParams(vmem_limit_bytes=32 * 1024 * 1024)


def whole(count):
    return [pl.BlockSpec(memory_space=pltpu.VMEM)] * count


def split(x):
    high = x.astype(BF16)
    low = (x - high.astype(F32)).astype(BF16)
    return high, low


def flat(ref, field, chunks):
    return jnp.concatenate([ref[j, field] for j in range(chunks)], axis=0)


def local_id(ids, owned):
    if owned & (owned - 1) == 0:
        return ids & (owned - 1)
    return lax.rem(ids, owned)


def pack_kernel(na, nd, owned_asc, owned_desc, ca, cd, ta, td, height, fill, out, turned):
    blocks, width = ca.shape
    group = width // na
    rows = blocks // na
    fill_row = fill[...]
    row_id = lax.broadcasted_iota(jnp.int32, (blocks, blocks), 0)
    col_id = lax.broadcasted_iota(jnp.int32, (blocks, blocks), 1)
    fill_col = jnp.sum(
        jnp.where(row_id == col_id, fill_row, 0).astype(F32), axis=1, keepdims=True
    )
    lane = lax.broadcasted_iota(jnp.int32, (blocks, width), 1)
    live = (lane.astype(F32) < fill_col).astype(F32)
    fields = [
        local_id(ca[...], owned_asc).astype(F32),
        ta[...],
        local_id(cd[...], owned_desc).astype(F32),
        td[...],
        height[...],
        live,
    ]
    source = lax.broadcasted_iota(jnp.int32, (width, width), 0)
    target = lax.broadcasted_iota(jnp.int32, (width, width), 1)
    owner = target // group
    place = target - owner * group
    order = (source == place * na + owner).astype(F32).astype(BF16)
    for f, x in enumerate(fields):
        high = x.astype(BF16)
        rest = x - high.astype(F32)
        middle = rest.astype(BF16)
        low = (rest - middle.astype(F32)).astype(BF16)
        turned[f] = (
            jnp.dot(high, order, preferred_element_type=F32)
            + jnp.dot(middle, order, preferred_element_type=F32)
        ) + jnp.dot(low, order, preferred_element_type=F32)
    lane_group = lax.broadcasted_iota(jnp.int32, (rows, width), 1) // group
    for f in range(FIELDS):
        parts = [None] * na
        for k in range(na):
            piece = turned[f, pl.ds(k, rows, stride=na), :]
            for r in range(na):
                amount = ((k - r) * group) % width
                moved = pltpu.roll(piece, amount, 1) if amount else piece
                parts[r] = moved if k == 0 else jnp.where(lane_group == k, moved, parts[r])
        for r in range(na):
            out[r % nd, r // nd, f] = parts[r]


def cos_sin_pi(x):
    turns = jnp.floor(x + 0.5)
    f = x - turns
    sign = 1.0 - 2.0 * (turns - 2.0 * jnp.floor(turns * 0.5))
    u = f * f
    c = COS_TERMS[-1]
    for term in COS_TERMS[-2::-1]:
        c = c * u + term
    s = SIN_TERMS[-1]
    for term in SIN_TERMS[-2::-1]:
        s = s * u + term
    return c * sign, s * (f * sign)


def rows_pair(ref, start):
    return jnp.concatenate([ref[pl.ds(start + i, 1), :] for i in range(STEP_ROWS)], axis=1)


def stacked(field):
    high, low = split(field)
    top = jnp.concatenate([high, high], axis=1)
    bottom = jnp.concatenate([low, jnp.zeros_like(low)], axis=1)
    return jnp.concatenate([top, bottom], axis=0)


def forward_step(stack, phi, ids_row, row_iota, owned):
    both = jnp.dot(stack, phi, preferred_element_type=F32)
    value = both[:owned] + both[owned:]
    return jnp.sum(jnp.where(row_iota == ids_row, value, 0.0), axis=0, keepdims=True)


def store_rows(ref, start, value):
    for i in range(STEP_ROWS):
        ref[pl.ds(start + i, 1), :] = value[:, i * LANES : (i + 1) * LANES]


def basis_loop(ids_ref, time_ref, coef, phi_ref, value_ref):
    owned, terms = coef.shape
    half = terms // 2
    steps = phi_ref.shape[0]
    width = phi_ref.shape[2]
    stack = stacked(coef)
    row_iota = lax.broadcasted_iota(jnp.int32, (owned, width), 0).astype(F32)
    fine = (lax.broadcasted_iota(jnp.int32, (8, width), 0) + 1).astype(F32)
    coarse = (lax.broadcasted_iota(jnp.int32, (half // 8, width), 0) * 8).astype(F32)

    def step(n):
        start = n * STEP_ROWS
        times = rows_pair(time_ref, start)
        cos_fine, sin_fine = cos_sin_pi(fine * times)
        cos_coarse, sin_coarse = cos_sin_pi(coarse * times)
        cos_parts, sin_parts = [], []
        for j in range(half // 8):
            cj = cos_coarse[j : j + 1]
            sj = sin_coarse[j : j + 1]
            cos_parts.append(cj * cos_fine - sj * sin_fine)
            sin_parts.append(sj * cos_fine + cj * sin_fine)
        high, low = split(jnp.concatenate(cos_parts + sin_parts, axis=0))
        phi = jnp.concatenate([high, low], axis=0)
        phi_ref[n] = phi
        value = forward_step(stack, phi, rows_pair(ids_ref, start), row_iota, owned)
        store_rows(value_ref, start, value)

    def block(i, carry):
        for u in range(UNROLL):
            step(i * UNROLL + u)
        return carry

    lax.fori_loop(0, steps // UNROLL, block, 0)


def setup_asc_kernel(chunks, packed, coef, phi, value, meta, times):
    meta[0] = flat(packed, 0, chunks)
    times[...] = flat(packed, 1, chunks)
    meta[1] = flat(packed, 4, chunks)
    meta[2] = flat(packed, 5, chunks)
    basis_loop(meta.at[0], times, coef[...], phi, value)


def setup_desc_kernel(chunks, packed, coef, value_asc, phi, meta, send, times, value):
    rows = send.shape[2]
    meta[0] = flat(packed, 2, chunks)
    times[...] = flat(packed, 3, chunks)
    meta[1] = flat(packed, 4, chunks)
    meta[2] = flat(packed, 5, chunks)
    basis_loop(meta.at[0], times, coef[...], phi, value)
    for j in range(chunks):
        send[j, 0] = value_asc[j * rows : (j + 1) * rows, :]
        send[j, 1] = value[j * rows : (j + 1) * rows, :]


def backward_forward(chunks, ids, z_ref, phis, finish, send, value_ref):
    owned = finish.owned
    steps, double, width = phis[0].shape
    terms = double // 2
    row_iota = lax.broadcasted_iota(jnp.int32, (owned, width), 0).astype(F32)

    def gather(role, n):
        start = n * STEP_ROWS
        hit = row_iota == rows_pair(ids[role], start)
        high = jnp.where(hit, rows_pair(z_ref.at[2 * role], start), 0.0).astype(BF16)
        low = jnp.where(hit, rows_pair(z_ref.at[2 * role + 1], start), 0.0).astype(BF16)
        return lax.dot_general(
            jnp.concatenate([high, low], axis=0),
            phis[role][n],
            (((1,), (1,)), ((), ())),
            preferred_element_type=F32,
        )

    def back(i, carry):
        asc, desc = carry
        for u in range(UNROLL):
            asc = asc + gather(0, i * UNROLL + u)
            desc = desc + gather(1, i * UNROLL + u)
        return asc, desc

    zero = jnp.zeros((2 * owned, double), F32)
    sums = lax.fori_loop(0, steps // UNROLL, back, (zero, zero))
    grads = [g[:owned, :terms] + (g[:owned, terms:] + g[owned:, :terms]) for g in sums]
    fields = finish(grads[0], -grads[1])
    stacks = [stacked(f) for f in fields]

    def ahead(i, carry):
        for u in range(UNROLL):
            n = i * UNROLL + u
            start = n * STEP_ROWS
            for role in range(2):
                value = forward_step(
                    stacks[role], phis[role][n], rows_pair(ids[role], start), row_iota, owned
                )
                store_rows(value_ref.at[role], start, value)
        return carry

    lax.fori_loop(0, steps // UNROLL, ahead, 0)
    rows = send.shape[2]
    for j in range(chunks):
        for role in range(2):
            send[j, role] = value_ref[role, j * rows : (j + 1) * rows, :]


class Finish:
    def __init__(self, owned, call):
        self.owned = owned
        self.call = call

    def __call__(self, asc, desc):
        return self.call(asc, desc)


def store_split(z_ref, role, z):
    high = z.astype(BF16).astype(F32)
    z_ref[2 * role] = high
    z_ref[2 * role + 1] = z - high


def cross_values(chunks, got, sent, role):
    if role == 0:
        return flat(sent, 0, chunks) - flat(got, 1, chunks)
    return flat(got, 0, chunks) - flat(sent, 1, chunks)


def weigh(model, meta, role, weights, z_ref):
    height, live = meta[1], meta[2]
    misfit = jnp.where(live > 0.0, height - model, 0.0)
    weight = live / (1.0 + misfit * misfit / cauchy_square)
    weights[role] = weight
    store_split(z_ref, role, weight * misfit)


def first_kernel(
    chunks, got, sent, meta_a, meta_d, phi_a, phi_d, state_a, state_d,
    model, weights, basis, send, z_ref, value_ref,
):
    for role, meta in enumerate((meta_a, meta_d)):
        values = cross_values(chunks, got, sent, role)
        model[role] = values
        weigh(values, meta, role, weights, z_ref)

    def finish(asc, desc):
        new = (asc - damping * state_a[...], desc - damping * state_d[...])
        basis[0], basis[1] = new
        return new

    backward_forward(
        chunks, (meta_a.at[0], meta_d.at[0]), z_ref, (phi_a, phi_d),
        Finish(state_a.shape[0], finish), send, value_ref,
    )


def image_kernel(
    chunks, got, sent, meta_a, meta_d, phi_a, phi_d, weights, before,
    crossed, basis, send, z_ref, value_ref,
):
    for role, meta in enumerate((meta_a, meta_d)):
        values = cross_values(chunks, got, sent, role)
        crossed[role] = values
        store_split(z_ref, role, weights[role] * values)

    def finish(asc, desc):
        new = (
            SCALE * (asc + damping * before[0]),
            SCALE * (desc + damping * before[1]),
        )
        basis[0], basis[1] = new
        return new

    backward_forward(
        chunks, (meta_a.at[0], meta_d.at[0]), z_ref, (phi_a, phi_d),
        Finish(before.shape[1], finish), send, value_ref,
    )


def total(x):
    return jnp.sum(jnp.sum(x, axis=0, keepdims=True), axis=1, keepdims=True)


PAIRS = [(0, 0), (0, 1), (0, 2), (1, 1), (1, 2), (2, 2)]


def gram_kernel(
    chunks, got, sent, weights, crossed_0, crossed_1, basis_0, basis_1, basis_2,
    crossed_2, scalars,
):
    for role in range(2):
        crossed_2[role] = cross_values(chunks, got, sent, role)
    weight = weights[0]
    values = [crossed_0[0], crossed_1[0], crossed_2[0]]
    bases = [basis_0, basis_1, basis_2]
    lane = lax.broadcasted_iota(jnp.int32, (1, LANES), 1)
    line = jnp.zeros((1, LANES), F32)
    for place, (i, j) in enumerate(PAIRS):
        dots = total(bases[i][0] * bases[j][0] + bases[i][1] * bases[j][1])
        curve = total(weight * values[i] * values[j]) + damping * dots
        line = jnp.where(lane == place, curve, line)
        if i == 0:
            line = jnp.where(lane == len(PAIRS) + j, dots, line)
    for d in range(scalars.shape[0]):
        scalars[d] = jnp.broadcast_to(line, scalars.shape[1:])


def solve(scalars):
    summed = scalars[0]
    for d in range(1, scalars.shape[0]):
        summed = summed + scalars[d]
    line = summed[0:1]
    lane = lax.broadcasted_iota(jnp.int32, (1, LANES), 1)

    def pick(place):
        return jnp.sum(jnp.where(lane == place, line, 0.0), axis=1, keepdims=True)

    g = {pair: pick(place) for place, pair in enumerate(PAIRS)}
    right = [pick(len(PAIRS) + i) for i in range(3)]
    s = [
        jnp.where(g[i, i] > 0.0, lax.rsqrt(jnp.maximum(g[i, i], 1e-37)), 0.0) for i in range(3)
    ]
    l10 = g[0, 1] * s[0] * s[1]
    l20 = g[0, 2] * s[0] * s[2]
    g21 = g[1, 2] * s[1] * s[2]
    c = [right[i] * s[i] for i in range(3)]

    def inverse(pivot):
        good = pivot > PIVOT_FLOOR
        return jnp.where(good, 1.0 / jnp.where(good, pivot, 1.0), 0.0)

    inv1 = inverse(1.0 - l10 * l10)
    t21 = g21 - l20 * l10
    l21 = t21 * inv1
    inv2 = inverse(1.0 - l20 * l20 - l21 * t21)
    u1 = c[1] - l10 * c[0]
    u2 = c[2] - l20 * c[0] - l21 * u1
    x2 = u2 * inv2
    x1 = u1 * inv1 - l21 * x2
    x0 = c[0] - l10 * x1 - l20 * x2
    return [x0 * s[0], x1 * s[1], x2 * s[2]]


def combine(y, parts):
    return y[0] * parts[0] + (y[1] * parts[1] + y[2] * parts[2])


def next_kernel(
    chunks, scalars, meta_a, meta_d, phi_a, phi_d, state_a, state_d, model,
    crossed_0, crossed_1, crossed_2, basis_0, basis_1, basis_2,
    new_state_a, new_state_d, new_model, weights, basis, send, z_ref, value_ref,
):
    y = solve(scalars)
    for role, meta in enumerate((meta_a, meta_d)):
        values = model[role] + combine(y, [crossed_0[role], crossed_1[role], crossed_2[role]])
        new_model[role] = values
        weigh(values, meta, role, weights, z_ref)
    new_state_a[...] = state_a[...] + combine(y, [basis_0[0], basis_1[0], basis_2[0]])
    new_state_d[...] = state_d[...] + combine(y, [basis_0[1], basis_1[1], basis_2[1]])

    def finish(asc, desc):
        new = (asc - damping * new_state_a[...], desc - damping * new_state_d[...])
        basis[0], basis[1] = new
        return new

    backward_forward(
        chunks, (meta_a.at[0], meta_d.at[0]), z_ref, (phi_a, phi_d),
        Finish(state_a.shape[0], finish), send, value_ref,
    )


def final_kernel(scalars, state_a, basis_0, basis_1, basis_2, desc, out_a, out_d):
    y = solve(scalars)
    out_a[...] = state_a[...] + combine(y, [basis_0[0], basis_1[0], basis_2[0]])
    out_d[...] = desc[0] + combine(y, [desc[1], desc[2], desc[3]])


def body(coef_asc, coef_desc, cross_asc, cross_desc, time_asc, time_desc, height, block_fill):
    owned_asc, terms = coef_asc.shape
    owned_desc = coef_desc.shape[0]
    blocks, width = cross_asc.shape
    na = lax.axis_size("asc")
    nd = lax.axis_size("desc")
    fold = na // nd
    rows = blocks * width // na // LANES
    all_rows = na * rows
    steps = all_rows // STEP_ROWS
    step_width = STEP_ROWS * LANES
    shape = jax.ShapeDtypeStruct

    def call(kernel, outs, scratch, *args):
        return pl.pallas_call(
            kernel,
            out_shape=outs,
            in_specs=whole(len(args)),
            out_specs=jax.tree.map(lambda _: pl.BlockSpec(memory_space=pltpu.VMEM), outs),
            scratch_shapes=scratch,
            compiler_params=params(),
        )(*args)

    to_role = []
    for p in range(na):
        for q in range(nd):
            to_role.append((p * nd + q, (q * fold + p // nd) * nd + p % nd))
    to_native = [(b, a) for a, b in to_role]
    role_desc = lax.ppermute(coef_desc, ("asc", "desc"), to_role)

    packed = call(
        functools.partial(pack_kernel, na, nd, owned_asc, owned_desc),
        shape((nd, fold, FIELDS, rows, LANES), F32),
        [pltpu.VMEM((FIELDS, blocks, width), F32)],
        cross_asc, cross_desc, time_asc, time_desc, height, block_fill.reshape(1, blocks),
    )
    at_asc = lax.all_to_all(packed, "desc", split_axis=0, concat_axis=0, tiled=True)
    at_asc = at_asc.reshape(na, FIELDS, rows, LANES)
    at_desc = lax.all_to_all(at_asc, "asc", split_axis=0, concat_axis=0, tiled=True)

    phi_shape = shape((steps, 2 * terms, step_width), BF16)
    meta_shape = shape((3, all_rows, LANES), F32)
    send_shape = shape((na, 2, rows, LANES), F32)
    pair_shape = shape((2, all_rows, LANES), F32)
    field_shape = shape((2, owned_asc, terms), F32)
    flat_scratch = pltpu.VMEM((all_rows, LANES), F32)
    pass_scratch = [
        pltpu.VMEM((4, all_rows, LANES), F32),
        pltpu.VMEM((2, all_rows, LANES), F32),
    ]
    phi_a, value_asc, meta_a = call(
        functools.partial(setup_asc_kernel, na),
        [phi_shape, shape((all_rows, LANES), F32), meta_shape],
        [flat_scratch],
        at_asc, coef_asc,
    )
    phi_d, meta_d, sent = call(
        functools.partial(setup_desc_kernel, na),
        [phi_shape, meta_shape, send_shape],
        [flat_scratch, flat_scratch],
        at_desc, role_desc, value_asc,
    )

    def exchange(x):
        return lax.all_to_all(x, "asc", split_axis=0, concat_axis=0, tiled=True)

    def share(x):
        return lax.all_to_all(x, ("asc", "desc"), split_axis=0, concat_axis=0, tiled=True)

    fixed = (meta_a, meta_d, phi_a, phi_d)
    state_a, state_d = coef_asc, role_desc
    for outer in range(GN_STEPS):
        if outer == 0:
            got = exchange(sent)
            model, weights, basis_0, sent = call(
                functools.partial(first_kernel, na),
                [pair_shape, pair_shape, field_shape, send_shape],
                pass_scratch,
                got, sent, *fixed, state_a, state_d,
            )
        else:
            state_a, state_d, model, weights, basis_0, sent = call(
                functools.partial(next_kernel, na),
                [
                    shape(state_a.shape, F32), shape(state_d.shape, F32),
                    pair_shape, pair_shape, field_shape, send_shape,
                ],
                pass_scratch,
                scalars, *fixed, state_a, state_d, model,
                *crossed, *bases,
            )
        bases, crossed = [basis_0], []
        for inner in range(2):
            got = exchange(sent)
            crossed_now, basis_now, sent = call(
                functools.partial(image_kernel, na),
                [pair_shape, field_shape, send_shape],
                pass_scratch,
                got, sent, *fixed, weights, bases[-1],
            )
            crossed.append(crossed_now)
            bases.append(basis_now)
        if outer + 1 == GN_STEPS:
            leaving = jnp.stack([state_d, bases[0][1], bases[1][1], bases[2][1]])
            native = lax.ppermute(leaving, ("asc", "desc"), to_native)
        got = exchange(sent)
        crossed_now, scalars = call(
            functools.partial(gram_kernel, na),
            [pair_shape, shape((na * nd, 8, LANES), F32)],
            [],
            got, sent, weights, *crossed, *bases,
        )
        crossed.append(crossed_now)
        scalars = share(scalars)
    return tuple(
        call(
            final_kernel,
            [shape(coef_asc.shape, F32), shape(coef_desc.shape, F32)],
            [],
            scalars, state_a, *bases, native,
        )
    )


def solution(mesh):
    split_rows = P(("asc", "desc"), None)
    return jax.shard_map(
        body,
        mesh=mesh,
        in_specs=(split_rows,) * 7 + (P(("asc", "desc")),),
        out_specs=(split_rows, split_rows),
        check_vma=False,
    )
```

time: 924 us -> 171 us (0.19); the launches traced: 911 us -> 169 us
  blocking collectives: 401 us -> 80.8 us
  starting transfers between devices: 143 us -> 8.32 us
  matrix products: 131 us -> 0 us
  waiting for transfers between devices: 82.2 us -> 7.68 us
  local copies, waits for them, and re-layouts: 74.8 us -> 10 us
  Pallas kernels: 0 us -> 61.3 us
  other arithmetic: 48.4 us -> 0.01 us
  between operations: 30.4 us -> 0.79 us
    psum x10 -> x0, blocking collectives: 401 us -> none  [the longest x6 241 us: norm_total(): return lax.psum(value, ('asc', 'desc'))]
    all_to_all x36 -> x2, starting transfers between devices: 143 us -> 6.29 us  [the longest x1 3.72 us: body(): lax.all_to_all(at_asc, 'asc', split_axis=0, concat_axis=0, tiled=True)]
    dot_general x32 -> x0, matrix products: 131 us -> none  [the longest x16 78.1 us: collect_rows(): lax.dot_general(selector, terms, (((0,), (0,)), ((), ())), precision=lax....]
    all_to_all x0 -> x9, blocking collectives: none -> 80.8 us  [the longest x7 54.7 us: exchange(): return lax.all_to_all(x, 'asc', split_axis=0, concat_axis=0, tiled=True)]
    all_to_all x36 -> x2, waiting for transfers between devices: 82.2 us -> 7.67 us  [the longest x1 7.67 us: share(): lax.all_to_all(x, ('asc', 'desc'), split_axis=0, concat_axis=0, tiled=True)]
    pallas_call x0 -> x12, Pallas kernels: none -> 61.3 us  [call(): pl.pallas_call(kernel, out_shape=outs, in_specs=whole(len(args)), out_spe...]
    all_to_all x36 -> x0, other arithmetic: 26.1 us -> none  [the longest x8 5.84 us: crossing(): lax.all_to_all(weighted.reshape(blocks, cols_asc, count_desc), 'desc', sp...]
    unnamed x111 -> x22, local copies, waits for them, and re-layouts: 34.1 us -> 9.99 us
  transfers between devices with their start and end apart: 36 -> 4, of which waited for: 19 -> 1; matrix products, arithmetic and copies ran while one was open for 15% -> 0% of each run, Pallas kernels for 0% -> 3%
where the time goes in v1:
time: 171 us; the launch traced here: 169 us
  blocking collectives  80.8 us (47%)
  Pallas kernels  61.3 us (36%)
  local copies, waits for them, and re-layouts  10 us (6%)
  starting transfers between devices  8.32 us (5%)
  waiting for transfers between devices  7.68 us (4%)
    pallas_call x12, Pallas kernels, call(): pl.pallas_call(kernel, out_shape=outs, in_specs=whole(len(args)), out_spe...  61.3 us
    all_to_all x7, blocking collectives, exchange(): return lax.all_to_all(x, 'asc', split_axis=0, concat_axis=0, tiled=True)  54.7 us
    all_to_all x1, blocking collectives, body(): lax.all_to_all(packed, 'desc', split_axis=0, concat_axis=0, tiled=True)  13.7 us
    all_to_all x1, blocking collectives, share(): lax.all_to_all(x, ('asc', 'desc'), split_axis=0, concat_axis=0, tiled=True)  12.4 us
    unnamed x22, local copies, waits for them, and re-layouts  9.99 us
    all_to_all x1, waiting for transfers between devices, share(): lax.all_to_all(x, ('asc', 'desc'), split_axis=0, concat_axis=0, tiled=True)  7.67 us
    all_to_all x1, starting transfers between devices, body(): lax.all_to_all(at_asc, 'asc', split_axis=0, concat_axis=0, tiled=True)  3.72 us
  transfers between devices with their start and end apart: 4, of which 1 were waited for; matrix products, arithmetic and copies ran while one was open for 0% of the time, Pallas kernels for 3%

profile of v1, /device:TPU:0, one launch (start us, length us, event | category | flops | bytes accessed | tf_op | source)
XLA Modules:
  0.0 168.9 jit_solution(17443923013393390707)
XLA Ops:
  0.6 0.7 copy-done.5
  1.4 0.8 copy-done.6
  2.2 0.8 copy-done.7
  2.9 0.8 copy-done.8
  3.7 0.8 copy-done.9
  5.7 13.7 %all_to_all.55 = f32[4,2,6,8,128]{4,3,2,1,0:T(8,128)} all-to-all(f32[4,2,6,8,128]{4,3,2,1,0:T(8,128)S(1)} %shard_map.95), channel_id=1, replica_groups=mesh['asc'=8,'desc'=4] {'desc'}, dimensions={0} | all-to-all | bytes 393216 | tf_op jit(solution)/shard_map/all_to_all | solution.py:445
  19.4 3.7 %all-to-all-start.1 = ((f32[8,6,8,128]{3,2,1,0:T(8,128)}), f32[8,6,8,128]{3,2,1,0:T(8,128)S(1)}, u32[]{:S(2)}, u32[]{:S(2)}) async-start(f32[8,6,8,128]{3,2,1,0:T(8,128)} %bitcast.1.packed), calls=%async_computation.1 | async-start | bytes 393216 | tf_op jit(solution)/shard_map/all_to_all | solution.py:447
  23.1 1.4 collective-permute-start
  24.5 0.7 copy-done.3
  25.2 5.3 %shard_map.96 = (bf16[32,256,256]{2,1,0:T(8,128)(2,1)S(1)}, f32[64,128]{1,0:T(8,128)S(1)}, f32[3,64,128]{2,1,0:T(8,128)S(1)}) custom-call(f32[8,6,8,128]{3,2,1,0:T(8,128)} %bitcast.1.packed, f32[32,128]{1,0:T(8,128)S(1)} %copy-done.3), custom_call_target="tpu_custom_call" | custom-call | tf_op jit(solution)/shard_map/pallas_call | solution.py:423
  30.5 1.9 %copy-done = bf16[32,256,256]{2,1,0:T(8,128)(2,1)} copy-done((bf16[32,256,256]{2,1,0:T(8,128)(2,1)}, bf16[32,256,256]{2,1,0:T(8,128)(2,1)S(1)}, u32[]{:S(2)}) %copy-start) | copy-done | bytes 4194328
  32.5 4.4 %shard_map.97 = (bf16[32,256,256]{2,1,0:T(8,128)(2,1)S(1)}, f32[3,64,128]{2,1,0:T(8,128)S(1)}, f32[8,2,8,128]{3,2,1,0:T(8,128)S(1)}) custom-call(f32[8,6,8,128]{3,2,1,0:T(8,128)S(1)} %all-to-all-done.1.packed, f32[32,128]{1,0:T(8,128)S(1)} %collective-permute-done.coef.state_d, f32[64,128]{1,0:T(8,128)S(1)} %get-tuple-element.32.value_asc), custom_call_target="tpu_custom_call" | custom-call | tf_op jit(solution)/shard_map/pallas_call | solution.py:423
  36.8 10.3 %all_to_all.56.got = f32[8,2,8,128]{3,2,1,0:T(8,128)S(1)} all-to-all(f32[8,2,8,128]{3,2,1,0:T(8,128)S(1)} %get-tuple-element.33.sent), channel_id=1, replica_groups=mesh['asc'=8,'desc'=4] {'asc'}, dimensions={0} | all-to-all | bytes 131072 | tf_op jit(solution)/shard_map/all_to_all | solution.py:473
  47.1 2.2 %copy-done.1 = bf16[32,256,256]{2,1,0:T(8,128)(2,1)S(1)} copy-done((bf16[32,256,256]{2,1,0:T(8,128)(2,1)S(1)}, bf16[32,256,256]{2,1,0:T(8,128)(2,1)}, u32[]{:S(2)}) %copy-start.1) | copy-done | bytes 4194328
  49.3 0.7 copy-done.4
  50.0 8.1 %shard_map.98 = (f32[2,64,128]{2,1,0:T(8,128)S(1)}, f32[2,64,128]{2,1,0:T(8,128)S(1)}, f32[2,32,128]{2,1,0:T(8,128)S(1)}, f32[8,2,8,128]{3,2,1,0:T(8,128)S(1)}) custom-call(f32[8,2,8,128]{3,2,1,0:T(8,128)S(1)} %all_to_all.56.got, f32[8,2,8,128]{3,2,1,0:T(8,128)S(1)} %get-tuple-element.33.sent, f32[3,64,128]{2,1,0:T(8,128)S(1)} %get-tuple-element.34.meta_a, ...), custom_call_target="tpu_custom_call" | custom-call | tf_op jit(solution)/shard_map/pallas_call | solution.py:423
  58.1 7.4 %all_to_all.57.got = f32[8,2,8,128]{3,2,1,0:T(8,128)S(1)} all-to-all(f32[8,2,8,128]{3,2,1,0:T(8,128)S(1)} %get-tuple-element.38.sent), channel_id=1, replica_groups=mesh['asc'=8,'desc'=4] {'asc'}, dimensions={0} | all-to-all | bytes 131072 | tf_op jit(solution)/shard_map/all_to_all | solution.py:473
  65.6 8.1 %shard_map.99 = (f32[2,64,128]{2,1,0:T(8,128)S(1)}, f32[2,32,128]{2,1,0:T(8,128)S(1)}, f32[8,2,8,128]{3,2,1,0:T(8,128)S(1)}) custom-call(f32[8,2,8,128]{3,2,1,0:T(8,128)S(1)} %all_to_all.57.got, f32[8,2,8,128]{3,2,1,0:T(8,128)S(1)} %get-tuple-element.38.sent, f32[3,64,128]{2,1,0:T(8,128)S(1)} %get-tuple-element.34.meta_a, ...), custom_call_target="tpu_custom_call" | custom-call | tf_op jit(solution)/shard_map/pallas_call | solution.py:423
  73.7 7.4 %all_to_all.58.got = f32[8,2,8,128]{3,2,1,0:T(8,128)S(1)} all-to-all(f32[8,2,8,128]{3,2,1,0:T(8,128)S(1)} %get-tuple-element.41.sent), channel_id=1, replica_groups=mesh['asc'=8,'desc'=4] {'asc'}, dimensions={0} | all-to-all | bytes 131072 | tf_op jit(solution)/shard_map/all_to_all | solution.py:473
  81.1 8.1 %shard_map.100 = (f32[2,64,128]{2,1,0:T(8,128)S(1)}, f32[2,32,128]{2,1,0:T(8,128)S(1)}, f32[8,2,8,128]{3,2,1,0:T(8,128)S(1)}) custom-call(f32[8,2,8,128]{3,2,1,0:T(8,128)S(1)} %all_to_all.58.got, f32[8,2,8,128]{3,2,1,0:T(8,128)S(1)} %get-tuple-element.41.sent, f32[3,64,128]{2,1,0:T(8,128)S(1)} %get-tuple-element.34.meta_a, ...), custom_call_target="tpu_custom_call" | custom-call | tf_op jit(solution)/shard_map/pallas_call | solution.py:423
  89.2 7.4 %all_to_all.59.got = f32[8,2,8,128]{3,2,1,0:T(8,128)S(1)} all-to-all(f32[8,2,8,128]{3,2,1,0:T(8,128)S(1)} %get-tuple-element.43.sent), channel_id=1, replica_groups=mesh['asc'=8,'desc'=4] {'asc'}, dimensions={0} | all-to-all | bytes 131072 | tf_op jit(solution)/shard_map/all_to_all | solution.py:473
  96.7 12.4 %all_to_all.60.scalars = f32[32,8,128]{2,1,0:T(8,128)S(1)} all-to-all(f32[32,8,128]{2,1,0:T(8,128)S(1)} %get-tuple-element.47), channel_id=1, replica_groups=mesh['asc'=8,'desc'=4] {'asc','desc'}, dimensions={0} | all-to-all | bytes 262144 | tf_op jit(solution)/shard_map/all_to_all | solution.py:476
  109.2 8.8 %shard_map.102 = (f32[32,128]{1,0:T(8,128)S(1)}, f32[32,128]{1,0:T(8,128)S(1)}, f32[2,64,128]{2,1,0:T(8,128)}, f32[2,64,128]{2,1,0:T(8,128)S(1)}, f32[2,32,128]{...) custom-call(f32[32,8,128]{2,1,0:T(8,128)S(1)} %all_to_all.60.scalars, f32[3,64,128]{2,1,0:T(8,128)S(1)} %get-tuple-element.34.meta_a, ...), custom_call_target="tpu_custom_call" | custom-call | tf_op jit(solution)/shard_map/pallas_call | solution.py:423
  118.0 7.4 %all_to_all.61.got = f32[8,2,8,128]{3,2,1,0:T(8,128)S(1)} all-to-all(f32[8,2,8,128]{3,2,1,0:T(8,128)S(1)} %get-tuple-element.50.sent), channel_id=1, replica_groups=mesh['asc'=8,'desc'=4] {'asc'}, dimensions={0} | all-to-all | bytes 131072 | tf_op jit(solution)/shard_map/all_to_all | solution.py:473
  125.3 8.1 %shard_map.103 = (f32[2,64,128]{2,1,0:T(8,128)S(1)}, f32[2,32,128]{2,1,0:T(8,128)S(1)}, f32[8,2,8,128]{3,2,1,0:T(8,128)S(1)}) custom-call(f32[8,2,8,128]{3,2,1,0:T(8,128)S(1)} %all_to_all.61.got, f32[8,2,8,128]{3,2,1,0:T(8,128)S(1)} %get-tuple-element.50.sent, f32[3,64,128]{2,1,0:T(8,128)S(1)} %get-tuple-element.34.meta_a, ...), custom_call_target="tpu_custom_call" | custom-call | tf_op jit(solution)/shard_map/pallas_call | solution.py:423
  133.5 7.4 %all_to_all.62.got = f32[8,2,8,128]{3,2,1,0:T(8,128)S(1)} all-to-all(f32[8,2,8,128]{3,2,1,0:T(8,128)S(1)} %get-tuple-element.53.sent), channel_id=1, replica_groups=mesh['asc'=8,'desc'=4] {'asc'}, dimensions={0} | all-to-all | bytes 131072 | tf_op jit(solution)/shard_map/all_to_all | solution.py:473
  140.9 8.1 %shard_map.104 = (f32[2,64,128]{2,1,0:T(8,128)S(1)}, f32[2,32,128]{2,1,0:T(8,128)S(1)}, f32[8,2,8,128]{3,2,1,0:T(8,128)S(1)}) custom-call(f32[8,2,8,128]{3,2,1,0:T(8,128)S(1)} %all_to_all.62.got, f32[8,2,8,128]{3,2,1,0:T(8,128)S(1)} %get-tuple-element.53.sent, f32[3,64,128]{2,1,0:T(8,128)S(1)} %get-tuple-element.34.meta_a, ...), custom_call_target="tpu_custom_call" | custom-call | tf_op jit(solution)/shard_map/pallas_call | solution.py:423
  149.0 7.4 %all_to_all.63.got = f32[8,2,8,128]{3,2,1,0:T(8,128)S(1)} all-to-all(f32[8,2,8,128]{3,2,1,0:T(8,128)S(1)} %get-tuple-element.55.sent), channel_id=1, replica_groups=mesh['asc'=8,'desc'=4] {'asc'}, dimensions={0} | all-to-all | bytes 131072 | tf_op jit(solution)/shard_map/all_to_all | solution.py:473
  156.4 0.8 shard_map.105
  157.2 2.6 %all-to-all-start.10 = ((f32[32,8,128]{2,1,0:T(8,128)}), f32[32,8,128]{2,1,0:T(8,128)S(1)}, u32[]{:S(2)}, u32[]{:S(2)}) async-start(f32[32,8,128]{2,1,0:T(8,128)} %get-tuple-element.59), calls=%async_computation.10 | async-start | bytes 262144 | tf_op jit(solution)/shard_map/all_to_all | solution.py:476
  160.5 7.7 %all-to-all-done.10.scalars = f32[32,8,128]{2,1,0:T(8,128)S(1)} async-done(((f32[32,8,128]{2,1,0:T(8,128)}), f32[32,8,128]{2,1,0:T(8,128)S(1)}, u32[]{:S(2)}, u32[]{:S(2)}) %all-to-all-start.10) | async-done | bytes 131104 | tf_op jit(solution)/shard_map/all_to_all | solution.py:476
  168.2 0.8 shard_map.106
  (23 shorter events, 2.1 us)
Async XLA Ops:
  0.6 0.8 copy-start.5
  1.4 0.8 copy-start.6
  2.1 0.8 copy-start.7
  2.9 0.8 copy-start.8
  3.7 0.8 copy-start.9
  4.4 0.7 copy-start.10
  19.4 13.0 %all-to-all-start.1 = ((f32[8,6,8,128]{3,2,1,0:T(8,128)}), f32[8,6,8,128]{3,2,1,0:T(8,128)S(1)}, u32[]{:S(2)}, u32[]{:S(2)}) async-start(f32[8,6,8,128]{3,2,1,0:T(8,128)} %bitcast.1.packed), calls=%async_computation.1 | async-start | bytes 393216 | tf_op jit(solution)/shard_map/all_to_all | solution.py:447
  23.1 9.3 %collective-permute-start = (f32[32,128]{1,0:T(8,128)}, f32[32,128]{1,0:T(8,128)S(1)}, u32[]{:S(2)}, u32[]{:S(2)}) collective-permute-start(f32[32,128]{1,0:T(8,128)} %param.9), channel_id=1, source_target_pairs={{0,0},{1,8},{2,16},{3,24},{4,1},{5,9},{6,17},{7,25},{8,2},{9,10},{... | collective-permute-start | bytes 49160 | tf_op jit(solution)/shard_map/ppermute | solution.py:437
  24.5 0.7 copy-start.3
  30.5 1.9 %copy-start = (bf16[32,256,256]{2,1,0:T(8,128)(2,1)}, bf16[32,256,256]{2,1,0:T(8,128)(2,1)S(1)}, u32[]{:S(2)}) copy-start(bf16[32,256,256]{2,1,0:T(8,128)(2,1)S(1)} %get-tuple-element.36.phi_a) | copy-start | bytes 12582916
  47.1 2.2 %copy-start.1 = (bf16[32,256,256]{2,1,0:T(8,128)(2,1)S(1)}, bf16[32,256,256]{2,1,0:T(8,128)(2,1)}, u32[]{:S(2)}) copy-start(bf16[32,256,256]{2,1,0:T(8,128)(2,1)} %copy-done) | copy-start | bytes 12582916
  49.3 0.7 copy-start.4
  50.0 15.5 %copy-start.2 = (bf16[32,256,256]{2,1,0:T(8,128)(2,1)S(1)}, bf16[32,256,256]{2,1,0:T(8,128)(2,1)}, u32[]{:S(2)}) copy-start(bf16[32,256,256]{2,1,0:T(8,128)(2,1)} %copy-done) | copy-start | bytes 12582916
  157.2 11.0 %all-to-all-start.10 = ((f32[32,8,128]{2,1,0:T(8,128)}), f32[32,8,128]{2,1,0:T(8,128)S(1)}, u32[]{:S(2)}, u32[]{:S(2)}) async-start(f32[32,8,128]{2,1,0:T(8,128)} %get-tuple-element.59), calls=%async_computation.10 | async-start | bytes 262144 | tf_op jit(solution)/shard_map/all_to_all | solution.py:476
  159.8 0.7 collective-permute-start.1

commit v2 on v1

--- a/solution.py
+++ b/solution.py
@@ -14,9 +14,11 @@
 
 LANES = 128
 STEP_ROWS = 2
-UNROLL = 2
+UNROLL = 4
+SETUP_UNROLL = 2
+DUMMY_ROWS = 8
 SCALE = 1.0 / 128.0
-FIELDS = 6
+FIELDS = 5
 PIVOT_FLOOR = 1e-6
 F32 = jnp.float32
 BF16 = jnp.bfloat16
@@ -25,12 +27,16 @@
 SIN_TERMS = [(-1.0) ** i * math.pi ** (2 * i + 1) / math.factorial(2 * i + 1) for i in range(7)]
 
 
-def params():
-    return pltpu.CompilerParams(vmem_limit_bytes=32 * 1024 * 1024)
-
-
-def whole(count):
-    return [pl.BlockSpec(memory_space=pltpu.VMEM)] * count
+def in_smem(x):
+    return x.dtype == jnp.int32 and len(x.shape) == 1
+
+
+def params(mebibytes):
+    return pltpu.CompilerParams(vmem_limit_bytes=mebibytes * 1024 * 1024)
+
+
+def place(x):
+    return pl.BlockSpec(memory_space=pltpu.SMEM if in_smem(x) else pltpu.VMEM)
 
 
 def split(x):
@@ -49,7 +55,23 @@
     return lax.rem(ids, owned)
 
 
-def pack_kernel(na, nd, owned_asc, owned_desc, ca, cd, ta, td, height, fill, out, turned):
+def pack_kernel(
+    na, nd, owned_asc, owned_desc, ca_in, cd_in, ta_in, td_in, height_in, fill_in, out,
+    ca, cd, ta, td, height, fill, turned, sems,
+):
+    copies = [
+        pltpu.make_async_copy(source, target, sems.at[i])
+        for i, (source, target) in enumerate(
+            [
+                (fill_in, fill), (ca_in, ca), (ta_in, ta),
+                (cd_in, cd), (td_in, td), (height_in, height),
+            ]
+        )
+    ]
+    for copy in copies:
+        copy.start()
+    for copy in copies:
+        copy.wait()
     blocks, width = ca.shape
     group = width // na
     rows = blocks // na
@@ -60,14 +82,13 @@
         jnp.where(row_id == col_id, fill_row, 0).astype(F32), axis=1, keepdims=True
     )
     lane = lax.broadcasted_iota(jnp.int32, (blocks, width), 1)
-    live = (lane.astype(F32) < fill_col).astype(F32)
+    live = lane.astype(F32) < fill_col
     fields = [
-        local_id(ca[...], owned_asc).astype(F32),
+        jnp.where(live, local_id(ca[...], owned_asc).astype(F32), -1.0),
         ta[...],
-        local_id(cd[...], owned_desc).astype(F32),
+        jnp.where(live, local_id(cd[...], owned_desc).astype(F32), -1.0),
         td[...],
         height[...],
-        live,
     ]
     source = lax.broadcasted_iota(jnp.int32, (width, width), 0)
     target = lax.broadcasted_iota(jnp.int32, (width, width), 1)
@@ -110,8 +131,27 @@
     return c * sign, s * (f * sign)
 
 
-def rows_pair(ref, start):
-    return jnp.concatenate([ref[pl.ds(start + i, 1), :] for i in range(STEP_ROWS)], axis=1)
+def rows_pair(ref, rows):
+    return jnp.concatenate([ref[pl.ds(r, 1), :] for r in rows], axis=1)
+
+
+def used_rows(ids_ref, chunks, rows, table):
+    count = jnp.int32(0)
+    level = lax.broadcasted_iota(jnp.int32, (rows, LANES), 0).astype(F32) + 1.0
+    for j in range(chunks):
+        ids = ids_ref[j * rows : (j + 1) * rows, :]
+        used = jnp.max(jnp.where(ids >= 0.0, level, 0.0)).astype(jnp.int32)
+        for i in range(rows):
+            table[count + i] = j * rows + i
+        count = count + used
+    group = STEP_ROWS * UNROLL
+    for i in range(group):
+        table[count + i] = chunks * rows
+    table[table.shape[0] - 1] = lax.div(count + (group - 1), group)
+
+
+def step_rows(table, n):
+    return [table[n * STEP_ROWS + i] for i in range(STEP_ROWS)]
 
 
 def stacked(field):
@@ -127,15 +167,15 @@
     return jnp.sum(jnp.where(row_iota == ids_row, value, 0.0), axis=0, keepdims=True)
 
 
-def store_rows(ref, start, value):
-    for i in range(STEP_ROWS):
-        ref[pl.ds(start + i, 1), :] = value[:, i * LANES : (i + 1) * LANES]
-
-
-def basis_loop(ids_ref, time_ref, coef, phi_ref, value_ref):
+def store_rows(ref, rows, value):
+    for i, r in enumerate(rows):
+        ref[pl.ds(r, 1), :] = value[:, i * LANES : (i + 1) * LANES]
+
+
+def basis_loop(table, ids_ref, time_ref, coef, phi_ref, value_ref):
     owned, terms = coef.shape
     half = terms // 2
-    steps = phi_ref.shape[0]
+    value_ref[...] = jnp.zeros(value_ref.shape, F32)
     width = phi_ref.shape[2]
     stack = stacked(coef)
     row_iota = lax.broadcasted_iota(jnp.int32, (owned, width), 0).astype(F32)
@@ -143,8 +183,8 @@
     coarse = (lax.broadcasted_iota(jnp.int32, (half // 8, width), 0) * 8).astype(F32)
 
     def step(n):
-        start = n * STEP_ROWS
-        times = rows_pair(time_ref, start)
+        rows = step_rows(table, n)
+        times = rows_pair(time_ref, rows)
         cos_fine, sin_fine = cos_sin_pi(fine * times)
         cos_coarse, sin_coarse = cos_sin_pi(coarse * times)
         cos_parts, sin_parts = [], []
@@ -156,80 +196,93 @@
         high, low = split(jnp.concatenate(cos_parts + sin_parts, axis=0))
         phi = jnp.concatenate([high, low], axis=0)
         phi_ref[n] = phi
-        value = forward_step(stack, phi, rows_pair(ids_ref, start), row_iota, owned)
-        store_rows(value_ref, start, value)
+        value = forward_step(stack, phi, rows_pair(ids_ref, rows), row_iota, owned)
+        store_rows(value_ref, rows, value)
 
     def block(i, carry):
-        for u in range(UNROLL):
-            step(i * UNROLL + u)
+        for u in range(SETUP_UNROLL):
+            step(i * SETUP_UNROLL + u)
         return carry
 
-    lax.fori_loop(0, steps // UNROLL, block, 0)
-
-
-def setup_asc_kernel(chunks, packed, coef, phi, value, meta, times):
-    meta[0] = flat(packed, 0, chunks)
-    times[...] = flat(packed, 1, chunks)
-    meta[1] = flat(packed, 4, chunks)
-    meta[2] = flat(packed, 5, chunks)
-    basis_loop(meta.at[0], times, coef[...], phi, value)
-
-
-def setup_desc_kernel(chunks, packed, coef, value_asc, phi, meta, send, times, value):
+    blocks = table[table.shape[0] - 1] * (UNROLL // SETUP_UNROLL)
+    lax.fori_loop(0, blocks, block, 0)
+
+
+def unpack(packed, chunks, first, meta, times):
+    rows = packed.shape[2]
+    count = chunks * rows
+    meta[0, :count] = flat(packed, first, chunks)
+    meta[0, count:] = jnp.full((DUMMY_ROWS, LANES), -1.0, F32)
+    meta[1, :count] = flat(packed, 4, chunks)
+    meta[1, count:] = jnp.zeros((DUMMY_ROWS, LANES), F32)
+    times[:count] = flat(packed, first + 1, chunks)
+    times[count:] = jnp.zeros((DUMMY_ROWS, LANES), F32)
+
+
+def setup_asc_kernel(chunks, packed, coef, phi, value, meta, table, times):
+    unpack(packed, chunks, 0, meta, times)
+    used_rows(meta.at[0], chunks, packed.shape[2], table)
+    basis_loop(table, meta.at[0], times, coef[...], phi, value)
+
+
+def setup_desc_kernel(chunks, packed, coef, value_asc, phi, meta, send, table, times, value):
     rows = send.shape[2]
-    meta[0] = flat(packed, 2, chunks)
-    times[...] = flat(packed, 3, chunks)
-    meta[1] = flat(packed, 4, chunks)
-    meta[2] = flat(packed, 5, chunks)
-    basis_loop(meta.at[0], times, coef[...], phi, value)
+    unpack(packed, chunks, 2, meta, times)
+    used_rows(meta.at[0], chunks, rows, table)
+    basis_loop(table, meta.at[0], times, coef[...], phi, value)
     for j in range(chunks):
         send[j, 0] = value_asc[j * rows : (j + 1) * rows, :]
         send[j, 1] = value[j * rows : (j + 1) * rows, :]
 
 
-def backward_forward(chunks, ids, z_ref, phis, finish, send, value_ref):
+def backward_forward(chunks, tables, ids, z_ref, phis, finish, send, value_ref):
     owned = finish.owned
     steps, double, width = phis[0].shape
     terms = double // 2
     row_iota = lax.broadcasted_iota(jnp.int32, (owned, width), 0).astype(F32)
 
-    def gather(role, n):
-        start = n * STEP_ROWS
-        hit = row_iota == rows_pair(ids[role], start)
-        high = jnp.where(hit, rows_pair(z_ref.at[2 * role], start), 0.0).astype(BF16)
-        low = jnp.where(hit, rows_pair(z_ref.at[2 * role + 1], start), 0.0).astype(BF16)
-        return lax.dot_general(
-            jnp.concatenate([high, low], axis=0),
-            phis[role][n],
-            (((1,), (1,)), ((), ())),
-            preferred_element_type=F32,
+    def back(role):
+        def gather(n):
+            rows = step_rows(tables[role], n)
+            hit = row_iota == rows_pair(ids[role], rows)
+            high = jnp.where(hit, rows_pair(z_ref.at[2 * role], rows), 0.0).astype(BF16)
+            low = jnp.where(hit, rows_pair(z_ref.at[2 * role + 1], rows), 0.0).astype(BF16)
+            return lax.dot_general(
+                jnp.concatenate([high, low], axis=0),
+                phis[role][n],
+                (((1,), (1,)), ((), ())),
+                preferred_element_type=F32,
+            )
+
+        def block(i, carry):
+            parts = [gather(i * UNROLL + u) for u in range(UNROLL)]
+            while len(parts) > 1:
+                parts = [sum(parts[k : k + 2]) for k in range(0, len(parts), 2)]
+            return carry + parts[0]
+
+        table = tables[role]
+        g = lax.fori_loop(
+            0, table[table.shape[0] - 1], block, jnp.zeros((2 * owned, double), F32)
         )
-
-    def back(i, carry):
-        asc, desc = carry
-        for u in range(UNROLL):
-            asc = asc + gather(0, i * UNROLL + u)
-            desc = desc + gather(1, i * UNROLL + u)
-        return asc, desc
-
-    zero = jnp.zeros((2 * owned, double), F32)
-    sums = lax.fori_loop(0, steps // UNROLL, back, (zero, zero))
-    grads = [g[:owned, :terms] + (g[:owned, terms:] + g[owned:, :terms]) for g in sums]
-    fields = finish(grads[0], -grads[1])
-    stacks = [stacked(f) for f in fields]
-
-    def ahead(i, carry):
-        for u in range(UNROLL):
-            n = i * UNROLL + u
-            start = n * STEP_ROWS
-            for role in range(2):
+        return g[:owned, :terms] + (g[:owned, terms:] + g[owned:, :terms])
+
+    fields = finish(back(0), -back(1))
+    value_ref[...] = jnp.zeros(value_ref.shape, F32)
+    for role in range(2):
+        stack = stacked(fields[role])
+        table = tables[role]
+
+        def block(i, carry):
+            for u in range(UNROLL):
+                n = i * UNROLL + u
+                rows = step_rows(table, n)
                 value = forward_step(
-                    stacks[role], phis[role][n], rows_pair(ids[role], start), row_iota, owned
+                    stack, phis[role][n], rows_pair(ids[role], rows), row_iota, owned
                 )
-                store_rows(value_ref.at[role], start, value)
-        return carry
-
-    lax.fori_loop(0, steps // UNROLL, ahead, 0)
+                store_rows(value_ref.at[role], rows, value)
+            return carry
+
+        lax.fori_loop(0, table[table.shape[0] - 1], block, 0)
     rows = send.shape[2]
     for j in range(chunks):
         for role in range(2):
@@ -246,9 +299,11 @@
 
 
 def store_split(z_ref, role, z):
+    count = z.shape[0]
     high = z.astype(BF16).astype(F32)
-    z_ref[2 * role] = high
-    z_ref[2 * role + 1] = z - high
+    z_ref[2 * role, :count] = high
+    z_ref[2 * role + 1, :count] = z - high
+    z_ref[2 * role : 2 * role + 2, count:] = jnp.zeros((2, DUMMY_ROWS, LANES), F32)
 
 
 def cross_values(chunks, got, sent, role):
@@ -258,15 +313,16 @@
 
 
 def weigh(model, meta, role, weights, z_ref):
-    height, live = meta[1], meta[2]
-    misfit = jnp.where(live > 0.0, height - model, 0.0)
-    weight = live / (1.0 + misfit * misfit / cauchy_square)
+    count = model.shape[0]
+    live = meta[0, :count] >= 0.0
+    misfit = jnp.where(live, meta[1, :count] - model, 0.0)
+    weight = jnp.where(live, 1.0 / (1.0 + misfit * misfit / cauchy_square), 0.0)
     weights[role] = weight
     store_split(z_ref, role, weight * misfit)
 
 
 def first_kernel(
-    chunks, got, sent, meta_a, meta_d, phi_a, phi_d, state_a, state_d,
+    chunks, got, sent, meta_a, meta_d, phi_a, phi_d, table_a, table_d, state_a, state_d,
     model, weights, basis, send, z_ref, value_ref,
 ):
     for role, meta in enumerate((meta_a, meta_d)):
@@ -280,13 +336,13 @@
         return new
 
     backward_forward(
-        chunks, (meta_a.at[0], meta_d.at[0]), z_ref, (phi_a, phi_d),
+        chunks, (table_a, table_d), (meta_a.at[0], meta_d.at[0]), z_ref, (phi_a, phi_d),
         Finish(state_a.shape[0], finish), send, value_ref,
     )
 
 
 def image_kernel(
-    chunks, got, sent, meta_a, meta_d, phi_a, phi_d, weights, before,
+    chunks, got, sent, meta_a, meta_d, phi_a, phi_d, table_a, table_d, weights, before,
     crossed, basis, send, z_ref, value_ref,
 ):
     for role, meta in enumerate((meta_a, meta_d)):
@@ -303,7 +359,7 @@
         return new
 
     backward_forward(
-        chunks, (meta_a.at[0], meta_d.at[0]), z_ref, (phi_a, phi_d),
+        chunks, (table_a, table_d), (meta_a.at[0], meta_d.at[0]), z_ref, (phi_a, phi_d),
         Finish(before.shape[1], finish), send, value_ref,
     )
 
@@ -377,7 +433,7 @@
 
 
 def next_kernel(
-    chunks, scalars, meta_a, meta_d, phi_a, phi_d, state_a, state_d, model,
+    chunks, scalars, meta_a, meta_d, phi_a, phi_d, table_a, table_d, state_a, state_d, model,
     crossed_0, crossed_1, crossed_2, basis_0, basis_1, basis_2,
     new_state_a, new_state_d, new_model, weights, basis, send, z_ref, value_ref,
 ):
@@ -395,7 +451,7 @@
         return new
 
     backward_forward(
-        chunks, (meta_a.at[0], meta_d.at[0]), z_ref, (phi_a, phi_d),
+        chunks, (table_a, table_d), (meta_a.at[0], meta_d.at[0]), z_ref, (phi_a, phi_d),
         Finish(state_a.shape[0], finish), send, value_ref,
     )
 
@@ -415,18 +471,19 @@
     fold = na // nd
     rows = blocks * width // na // LANES
     all_rows = na * rows
-    steps = all_rows // STEP_ROWS
+    group = STEP_ROWS * UNROLL
+    steps = -(-all_rows // group) * UNROLL
     step_width = STEP_ROWS * LANES
     shape = jax.ShapeDtypeStruct
 
-    def call(kernel, outs, scratch, *args):
+    def call(kernel, outs, scratch, *args, in_specs=None, mebibytes=16):
         return pl.pallas_call(
             kernel,
             out_shape=outs,
-            in_specs=whole(len(args)),
-            out_specs=jax.tree.map(lambda _: pl.BlockSpec(memory_space=pltpu.VMEM), outs),
+            in_specs=[place(x) for x in args] if in_specs is None else in_specs,
+            out_specs=jax.tree.map(place, outs),
             scratch_shapes=scratch,
-            compiler_params=params(),
+            compiler_params=params(mebibytes),
         )(*args)
 
     to_role = []
@@ -436,35 +493,44 @@
     to_native = [(b, a) for a, b in to_role]
     role_desc = lax.ppermute(coef_desc, ("asc", "desc"), to_role)
 
+    slots = (cross_asc, cross_desc, time_asc, time_desc, height)
     packed = call(
         functools.partial(pack_kernel, na, nd, owned_asc, owned_desc),
         shape((nd, fold, FIELDS, rows, LANES), F32),
-        [pltpu.VMEM((FIELDS, blocks, width), F32)],
-        cross_asc, cross_desc, time_asc, time_desc, height, block_fill.reshape(1, blocks),
+        [pltpu.VMEM((blocks, width), x.dtype) for x in slots]
+        + [
+            pltpu.VMEM((1, blocks), jnp.int32),
+            pltpu.VMEM((FIELDS, blocks, width), F32),
+            pltpu.SemaphoreType.DMA((len(slots) + 1,)),
+        ],
+        *slots, block_fill.reshape(1, blocks),
+        in_specs=[pl.BlockSpec(memory_space=pltpu.HBM)] * (len(slots) + 1),
+        mebibytes=60,
     )
     at_asc = lax.all_to_all(packed, "desc", split_axis=0, concat_axis=0, tiled=True)
     at_asc = at_asc.reshape(na, FIELDS, rows, LANES)
     at_desc = lax.all_to_all(at_asc, "asc", split_axis=0, concat_axis=0, tiled=True)
 
     phi_shape = shape((steps, 2 * terms, step_width), BF16)
-    meta_shape = shape((3, all_rows, LANES), F32)
+    meta_shape = shape((2, all_rows + DUMMY_ROWS, LANES), F32)
+    table_shape = shape((all_rows + rows + STEP_ROWS * UNROLL + 1,), jnp.int32)
     send_shape = shape((na, 2, rows, LANES), F32)
     pair_shape = shape((2, all_rows, LANES), F32)
     field_shape = shape((2, owned_asc, terms), F32)
-    flat_scratch = pltpu.VMEM((all_rows, LANES), F32)
+    flat_scratch = pltpu.VMEM((all_rows + DUMMY_ROWS, LANES), F32)
     pass_scratch = [
-        pltpu.VMEM((4, all_rows, LANES), F32),
-        pltpu.VMEM((2, all_rows, LANES), F32),
+        pltpu.VMEM((4, all_rows + DUMMY_ROWS, LANES), F32),
+        pltpu.VMEM((2, all_rows + DUMMY_ROWS, LANES), F32),
     ]
-    phi_a, value_asc, meta_a = call(
+    phi_a, value_asc, meta_a, table_a = call(
         functools.partial(setup_asc_kernel, na),
-        [phi_shape, shape((all_rows, LANES), F32), meta_shape],
+        [phi_shape, shape((all_rows + DUMMY_ROWS, LANES), F32), meta_shape, table_shape],
         [flat_scratch],
         at_asc, coef_asc,
     )
-    phi_d, meta_d, sent = call(
+    phi_d, meta_d, sent, table_d = call(
         functools.partial(setup_desc_kernel, na),
-        [phi_shape, meta_shape, send_shape],
+        [phi_shape, meta_shape, send_shape, table_shape],
         [flat_scratch, flat_scratch],
         at_desc, role_desc, value_asc,
     )
@@ -475,7 +541,7 @@
     def share(x):
         return lax.all_to_all(x, ("asc", "desc"), split_axis=0, concat_axis=0, tiled=True)
 
-    fixed = (meta_a, meta_d, phi_a, phi_d)
+    fixed = (meta_a, meta_d, phi_a, phi_d, table_a, table_d)
     state_a, state_d = coef_asc, role_desc
     for outer in range(GN_STEPS):
         if outer == 0:

time: 171 us -> 145 us (0.85)
  the two profiles are of different devices: /device:TPU:0 before, /device:TPU:25 now
where the time goes in v2:
time: 145 us; the launch traced here: 142 us
  blocking collectives  71.1 us (49%)
  Pallas kernels  39.2 us (27%)
  starting transfers between devices  19.7 us (14%)
  waiting for transfers between devices  6.11 us (4%)
  local copies, waits for them, and re-layouts  5.57 us (4%)
    all_to_all x7, blocking collectives, exchange(): return lax.all_to_all(x, 'asc', split_axis=0, concat_axis=0, tiled=True)  52.5 us
    pallas_call x12, Pallas kernels, call(): pl.pallas_call(kernel, out_shape=outs, in_specs=[place(x) for x in args]...  39.2 us
    all_to_all x1, blocking collectives, share(): lax.all_to_all(x, ('asc', 'desc'), split_axis=0, concat_axis=0, tiled=True)  9.52 us
    all_to_all x1, blocking collectives, body(): lax.all_to_all(packed, 'desc', split_axis=0, concat_axis=0, tiled=True)  9.03 us
    ppermute x1, waiting for transfers between devices, body(): native = lax.ppermute(leaving, ('asc', 'desc'), to_native)  6.1 us
    unnamed x10, local copies, waits for them, and re-layouts  5.56 us
    all_to_all x1, starting transfers between devices, share(): lax.all_to_all(x, ('asc', 'desc'), split_axis=0, concat_axis=0, tiled=True)  5.48 us
    ppermute x1, starting transfers between devices, body(): role_desc = lax.ppermute(coef_desc, ('asc', 'desc'), to_role)  5.45 us
  transfers between devices with their start and end apart: 4, of which 1 were waited for; matrix products, arithmetic and copies ran while one was open for 0% of the time, Pallas kernels for 3%

profile of v2, /device:TPU:25, one launch (start us, length us, event | category | flops | bytes accessed | tf_op | source)
XLA Modules:
  0.0 142.4 jit_solution(5404850834519554069)
XLA Ops:
  0.6 2.2 %shard_map.95 = f32[4,2,5,8,128]{4,3,2,1,0:T(8,128)} custom-call(s32[64,128]{1,0:T(8,128)} %ca_in.1, s32[64,128]{1,0:T(8,128)} %cd_in.1, f32[64,128]{1,0:T(8,128)} %ta_in.1, f32[64,128]{1,0:T(8,128)} %td_in.1, f32[64,128]{1,0:T(8,128)} %height_in.1, s32[1,64]{1,0:T(1,128)} %bitcast.4), custom_call_target="tpu_custom_call" | custom-call | tf_op jit(solution)/shard_map/pallas_call | solution.py:480
  2.8 9.0 %all_to_all.55 = f32[4,2,5,8,128]{4,3,2,1,0:T(8,128)} all-to-all(f32[4,2,5,8,128]{4,3,2,1,0:T(8,128)} %shard_map.95), channel_id=1, replica_groups=mesh['asc'=8,'desc'=4] {'desc'}, dimensions={0} | all-to-all | bytes 327680 | tf_op jit(solution)/shard_map/all_to_all | solution.py:510
  11.8 5.0 %all-to-all-start.1 = ((f32[8,5,8,128]{3,2,1,0:T(8,128)}), f32[8,5,8,128]{3,2,1,0:T(8,128)S(1)}, u32[]{:S(2)}, u32[]{:S(2)}) async-start(f32[8,5,8,128]{3,2,1,0:T(8,128)} %bitcast.1.packed), calls=%async_computation.1 | async-start | bytes 327680 | tf_op jit(solution)/shard_map/all_to_all | solution.py:512
  16.8 5.5 %collective-permute-start = (f32[32,128]{1,0:T(8,128)}, f32[32,128]{1,0:T(8,128)S(1)}, u32[]{:S(2)}, u32[]{:S(2)}) collective-permute-start(f32[32,128]{1,0:T(8,128)} %param.9), channel_id=1, source_target_pairs={{0,0},{1,8},{2,16},{3,24},{4,1},{5,9},{6,17},{7,25},{8,2},{9,10},{... | collective-permute-start | bytes 49160 | tf_op jit(solution)/shard_map/ppermute | solution.py:494
  22.3 0.0 copy-start.3
  22.3 0.7 copy-done.3
  23.0 3.8 %shard_map.96 = (bf16[32,256,256]{2,1,0:T(8,128)(2,1)S(1)}, f32[72,128]{1,0:T(8,128)S(1)}, f32[2,72,128]{2,1,0:T(8,128)S(1)}, s32[81]{0:T(128)S(1)}) custom-call(f32[8,5,8,128]{3,2,1,0:T(8,128)} %bitcast.1.packed, f32[32,128]{1,0:T(8,128)S(1)} %copy-done.3), custom_call_target="tpu_custom_call" | custom-call | tf_op jit(solution)/shard_map/pallas_call | solution.py:480
  26.8 1.9 %copy-done = bf16[32,256,256]{2,1,0:T(8,128)(2,1)} copy-done((bf16[32,256,256]{2,1,0:T(8,128)(2,1)}, bf16[32,256,256]{2,1,0:T(8,128)(2,1)S(1)}, u32[]{:S(2)}) %copy-start) | copy-done | bytes 4194328
  28.8 0.0 collective-permute-done.coef.state_d
  28.8 2.9 %shard_map.97 = (bf16[32,256,256]{2,1,0:T(8,128)(2,1)S(1)}, f32[2,72,128]{2,1,0:T(8,128)S(1)}, f32[8,2,8,128]{3,2,1,0:T(8,128)S(1)}, s32[81]{0:T(128)S(1)}) custom-call(f32[8,5,8,128]{3,2,1,0:T(8,128)S(1)} %all-to-all-done.1.packed, f32[32,128]{1,0:T(8,128)S(1)} %collective-permute-done.coef.state_d, f32[72,128]{1,0:T(8,128)S(1)} %get-tuple-element.34.value_asc), custom_call_target="tpu_custom_call" | custom-call | tf_op jit(solution)/shard_map/pallas_call | solution.py:480
  31.7 7.9 %all_to_all.56.got = f32[8,2,8,128]{3,2,1,0:T(8,128)S(1)} all-to-all(f32[8,2,8,128]{3,2,1,0:T(8,128)S(1)} %get-tuple-element.35.sent), channel_id=1, replica_groups=mesh['asc'=8,'desc'=4] {'asc'}, dimensions={0} | all-to-all | bytes 131072 | tf_op jit(solution)/shard_map/all_to_all | solution.py:539
  39.6 2.2 %copy-done.1 = bf16[32,256,256]{2,1,0:T(8,128)(2,1)S(1)} copy-done((bf16[32,256,256]{2,1,0:T(8,128)(2,1)S(1)}, bf16[32,256,256]{2,1,0:T(8,128)(2,1)}, u32[]{:S(2)}) %copy-start.1) | copy-done | bytes 4194328
  41.8 0.7 copy-done.4
  42.5 4.7 %shard_map.98 = (f32[2,64,128]{2,1,0:T(8,128)S(1)}, f32[2,64,128]{2,1,0:T(8,128)S(1)}, f32[2,32,128]{2,1,0:T(8,128)S(1)}, f32[8,2,8,128]{3,2,1,0:T(8,128)S(1)}) custom-call(f32[8,2,8,128]{3,2,1,0:T(8,128)S(1)} %all_to_all.56.got, f32[8,2,8,128]{3,2,1,0:T(8,128)S(1)} %get-tuple-element.35.sent, f32[2,72,128]{2,1,0:T(8,128)S(1)} %get-tuple-element.36.meta_a, ...), custom_call_target="tpu_custom_call" | custom-call | tf_op jit(solution)/shard_map/pallas_call | solution.py:480
  47.1 7.4 %all_to_all.57.got = f32[8,2,8,128]{3,2,1,0:T(8,128)S(1)} all-to-all(f32[8,2,8,128]{3,2,1,0:T(8,128)S(1)} %get-tuple-element.42.sent), channel_id=1, replica_groups=mesh['asc'=8,'desc'=4] {'asc'}, dimensions={0} | all-to-all | bytes 131072 | tf_op jit(solution)/shard_map/all_to_all | solution.py:539
  54.5 4.6 %shard_map.99 = (f32[2,64,128]{2,1,0:T(8,128)S(1)}, f32[2,32,128]{2,1,0:T(8,128)S(1)}, f32[8,2,8,128]{3,2,1,0:T(8,128)S(1)}) custom-call(f32[8,2,8,128]{3,2,1,0:T(8,128)S(1)} %all_to_all.57.got, f32[8,2,8,128]{3,2,1,0:T(8,128)S(1)} %get-tuple-element.42.sent, f32[2,72,128]{2,1,0:T(8,128)S(1)} %get-tuple-element.36.meta_a, ...), custom_call_target="tpu_custom_call" | custom-call | tf_op jit(solution)/shard_map/pallas_call | solution.py:480
  59.2 7.4 %all_to_all.58.got = f32[8,2,8,128]{3,2,1,0:T(8,128)S(1)} all-to-all(f32[8,2,8,128]{3,2,1,0:T(8,128)S(1)} %get-tuple-element.45.sent), channel_id=1, replica_groups=mesh['asc'=8,'desc'=4] {'asc'}, dimensions={0} | all-to-all | bytes 131072 | tf_op jit(solution)/shard_map/all_to_all | solution.py:539
  66.6 4.6 %shard_map.100 = (f32[2,64,128]{2,1,0:T(8,128)S(1)}, f32[2,32,128]{2,1,0:T(8,128)S(1)}, f32[8,2,8,128]{3,2,1,0:T(8,128)S(1)}) custom-call(f32[8,2,8,128]{3,2,1,0:T(8,128)S(1)} %all_to_all.58.got, f32[8,2,8,128]{3,2,1,0:T(8,128)S(1)} %get-tuple-element.45.sent, f32[2,72,128]{2,1,0:T(8,128)S(1)} %get-tuple-element.36.meta_a, ...), custom_call_target="tpu_custom_call" | custom-call | tf_op jit(solution)/shard_map/pallas_call | solution.py:480
  71.2 7.4 %all_to_all.59.got = f32[8,2,8,128]{3,2,1,0:T(8,128)S(1)} all-to-all(f32[8,2,8,128]{3,2,1,0:T(8,128)S(1)} %get-tuple-element.47.sent), channel_id=1, replica_groups=mesh['asc'=8,'desc'=4] {'asc'}, dimensions={0} | all-to-all | bytes 131072 | tf_op jit(solution)/shard_map/all_to_all | solution.py:539
  78.6 0.1 shard_map.101
  78.7 9.5 %all_to_all.60.scalars = f32[32,8,128]{2,1,0:T(8,128)S(1)} all-to-all(f32[32,8,128]{2,1,0:T(8,128)S(1)} %get-tuple-element.51), channel_id=1, replica_groups=mesh['asc'=8,'desc'=4] {'asc','desc'}, dimensions={0} | all-to-all | bytes 262144 | tf_op jit(solution)/shard_map/all_to_all | solution.py:542
  88.3 5.4 %shard_map.102 = (f32[32,128]{1,0:T(8,128)S(1)}, f32[32,128]{1,0:T(8,128)S(1)}, f32[2,64,128]{2,1,0:T(8,128)}, f32[2,64,128]{2,1,0:T(8,128)S(1)}, f32[2,32,128]{...) custom-call(f32[32,8,128]{2,1,0:T(8,128)S(1)} %all_to_all.60.scalars, f32[2,72,128]{2,1,0:T(8,128)S(1)} %get-tuple-element.36.meta_a, ...), custom_call_target="tpu_custom_call" | custom-call | tf_op jit(solution)/shard_map/pallas_call | solution.py:480
  93.7 7.6 %all_to_all.61.got = f32[8,2,8,128]{3,2,1,0:T(8,128)S(1)} all-to-all(f32[8,2,8,128]{3,2,1,0:T(8,128)S(1)} %get-tuple-element.54.sent), channel_id=1, replica_groups=mesh['asc'=8,'desc'=4] {'asc'}, dimensions={0} | all-to-all | bytes 131072 | tf_op jit(solution)/shard_map/all_to_all | solution.py:539
  101.3 4.6 %shard_map.103 = (f32[2,64,128]{2,1,0:T(8,128)S(1)}, f32[2,32,128]{2,1,0:T(8,128)S(1)}, f32[8,2,8,128]{3,2,1,0:T(8,128)S(1)}) custom-call(f32[8,2,8,128]{3,2,1,0:T(8,128)S(1)} %all_to_all.61.got, f32[8,2,8,128]{3,2,1,0:T(8,128)S(1)} %get-tuple-element.54.sent, f32[2,72,128]{2,1,0:T(8,128)S(1)} %get-tuple-element.36.meta_a, ...), custom_call_target="tpu_custom_call" | custom-call | tf_op jit(solution)/shard_map/pallas_call | solution.py:480
  106.0 7.4 %all_to_all.62.got = f32[8,2,8,128]{3,2,1,0:T(8,128)S(1)} all-to-all(f32[8,2,8,128]{3,2,1,0:T(8,128)S(1)} %get-tuple-element.57.sent), channel_id=1, replica_groups=mesh['asc'=8,'desc'=4] {'asc'}, dimensions={0} | all-to-all | bytes 131072 | tf_op jit(solution)/shard_map/all_to_all | solution.py:539
  113.4 4.6 %shard_map.104 = (f32[2,64,128]{2,1,0:T(8,128)S(1)}, f32[2,32,128]{2,1,0:T(8,128)S(1)}, f32[8,2,8,128]{3,2,1,0:T(8,128)S(1)}) custom-call(f32[8,2,8,128]{3,2,1,0:T(8,128)S(1)} %all_to_all.62.got, f32[8,2,8,128]{3,2,1,0:T(8,128)S(1)} %get-tuple-element.57.sent, f32[2,72,128]{2,1,0:T(8,128)S(1)} %get-tuple-element.36.meta_a, ...), custom_call_target="tpu_custom_call" | custom-call | tf_op jit(solution)/shard_map/pallas_call | solution.py:480
  118.0 7.4 %all_to_all.63.got = f32[8,2,8,128]{3,2,1,0:T(8,128)S(1)} all-to-all(f32[8,2,8,128]{3,2,1,0:T(8,128)S(1)} %get-tuple-element.59.sent), channel_id=1, replica_groups=mesh['asc'=8,'desc'=4] {'asc'}, dimensions={0} | all-to-all | bytes 131072 | tf_op jit(solution)/shard_map/all_to_all | solution.py:539
  125.4 0.8 shard_map.105
  126.2 5.5 %all-to-all-start.10 = ((f32[32,8,128]{2,1,0:T(8,128)}), f32[32,8,128]{2,1,0:T(8,128)S(1)}, u32[]{:S(2)}, u32[]{:S(2)}) async-start(f32[32,8,128]{2,1,0:T(8,128)} %get-tuple-element.63), calls=%async_computation.10 | async-start | bytes 262144 | tf_op jit(solution)/shard_map/all_to_all | solution.py:542
  131.7 3.8 %collective-permute-start.1 = (f32[4,32,128]{2,1,0:T(8,128)S(1)}, f32[4,32,128]{2,1,0:T(8,128)S(1)}, u32[]{:S(2)}, u32[]{:S(2)}) collective-permute-start(f32[4,32,128]{2,1,0:T(8,128)S(1)} %pad_maximum_fusion), channel_id=1, source_target_pairs={{0,0},{8,1},{16,2},{24,3},{1,4},{9,5},{17,6},{25,7},{2,8},{10,9},{... | collective-permute-start | bytes 196616 | tf_op jit(solution)/shard_map/ppermute | solution.py:579
  135.6 6.1 %collective-permute-done.1.desc = f32[4,32,128]{2,1,0:T(8,128)S(1)} collective-permute-done((f32[4,32,128]{2,1,0:T(8,128)S(1)}, f32[4,32,128]{2,1,0:T(8,128)S(1)}, u32[]{:S(2)}, u32[]{:S(2)}) %collective-permute-start.1) | collective-permute-done | bytes 65568 | tf_op jit(solution)/shard_map/ppermute | solution.py:579
  141.7 0.8 shard_map.106
  (11 shorter events, 0.0 us)
Async XLA Ops:
  11.8 16.9 %all-to-all-start.1 = ((f32[8,5,8,128]{3,2,1,0:T(8,128)}), f32[8,5,8,128]{3,2,1,0:T(8,128)S(1)}, u32[]{:S(2)}, u32[]{:S(2)}) async-start(f32[8,5,8,128]{3,2,1,0:T(8,128)} %bitcast.1.packed), calls=%async_computation.1 | async-start | bytes 327680 | tf_op jit(solution)/shard_map/all_to_all | solution.py:512
  16.8 11.9 %collective-permute-start = (f32[32,128]{1,0:T(8,128)}, f32[32,128]{1,0:T(8,128)S(1)}, u32[]{:S(2)}, u32[]{:S(2)}) collective-permute-start(f32[32,128]{1,0:T(8,128)} %param.9), channel_id=1, source_target_pairs={{0,0},{1,8},{2,16},{3,24},{4,1},{5,9},{6,17},{7,25},{8,2},{9,10},{... | collective-permute-start | bytes 49160 | tf_op jit(solution)/shard_map/ppermute | solution.py:494
  22.3 0.7 copy-start.3
  26.8 1.9 %copy-start = (bf16[32,256,256]{2,1,0:T(8,128)(2,1)}, bf16[32,256,256]{2,1,0:T(8,128)(2,1)S(1)}, u32[]{:S(2)}) copy-start(bf16[32,256,256]{2,1,0:T(8,128)(2,1)S(1)} %get-tuple-element.38.phi_a) | copy-start | bytes 12582916
  39.6 2.2 %copy-start.1 = (bf16[32,256,256]{2,1,0:T(8,128)(2,1)S(1)}, bf16[32,256,256]{2,1,0:T(8,128)(2,1)}, u32[]{:S(2)}) copy-start(bf16[32,256,256]{2,1,0:T(8,128)(2,1)} %copy-done) | copy-start | bytes 12582916
  41.8 0.7 copy-start.4
  42.5 12.1 %copy-start.2 = (bf16[32,256,256]{2,1,0:T(8,128)(2,1)S(1)}, bf16[32,256,256]{2,1,0:T(8,128)(2,1)}, u32[]{:S(2)}) copy-start(bf16[32,256,256]{2,1,0:T(8,128)(2,1)} %copy-done) | copy-start | bytes 12582916
  126.2 15.5 %all-to-all-start.10 = ((f32[32,8,128]{2,1,0:T(8,128)}), f32[32,8,128]{2,1,0:T(8,128)S(1)}, u32[]{:S(2)}, u32[]{:S(2)}) async-start(f32[32,8,128]{2,1,0:T(8,128)} %get-tuple-element.63), calls=%async_computation.10 | async-start | bytes 262144 | tf_op jit(solution)/shard_map/all_to_all | solution.py:542
  131.7 9.9 %collective-permute-start.1 = (f32[4,32,128]{2,1,0:T(8,128)S(1)}, f32[4,32,128]{2,1,0:T(8,128)S(1)}, u32[]{:S(2)}, u32[]{:S(2)}) collective-permute-start(f32[4,32,128]{2,1,0:T(8,128)S(1)} %pad_maximum_fusion), channel_id=1, source_target_pairs={{0,0},{8,1},{16,2},{24,3},{1,4},{9,5},{17,6},{25,7},{2,8},{10,9},{... | collective-permute-start | bytes 196616 | tf_op jit(solution)/shard_map/ppermute | solution.py:579

commit v3 on v2

--- a/solution.py
+++ b/solution.py
@@ -219,23 +219,46 @@
     times[count:] = jnp.zeros((DUMMY_ROWS, LANES), F32)
 
 
-def setup_asc_kernel(chunks, packed, coef, phi, value, meta, table, times):
-    unpack(packed, chunks, 0, meta, times)
-    used_rows(meta.at[0], chunks, packed.shape[2], table)
-    basis_loop(table, meta.at[0], times, coef[...], phi, value)
-
-
-def setup_desc_kernel(chunks, packed, coef, value_asc, phi, meta, send, table, times, value):
-    rows = send.shape[2]
-    unpack(packed, chunks, 2, meta, times)
-    used_rows(meta.at[0], chunks, rows, table)
-    basis_loop(table, meta.at[0], times, coef[...], phi, value)
-    for j in range(chunks):
-        send[j, 0] = value_asc[j * rows : (j + 1) * rows, :]
-        send[j, 1] = value[j * rows : (j + 1) * rows, :]
-
-
-def backward_forward(chunks, tables, ids, z_ref, phis, finish, send, value_ref):
+def setup_kernel(
+    chunks, at_asc, at_desc, coef_a, coef_d,
+    meta_a, meta_d, phi_a, phi_d, table_a, table_d, value, *rest,
+):
+    sends, (times,) = rest[:chunks], rest[chunks:]
+    rows = at_asc.shape[2]
+    unpack(at_asc, chunks, 0, meta_a, times)
+    used_rows(meta_a.at[0], chunks, rows, table_a)
+    basis_loop(table_a, meta_a.at[0], times, coef_a[...], phi_a, value.at[0])
+    unpack(at_desc, chunks, 2, meta_d, times)
+    used_rows(meta_d.at[0], chunks, rows, table_d)
+    basis_loop(table_d, meta_d.at[0], times, coef_d[...], phi_d, value.at[1])
+    hand_out(value, sends)
+
+
+def partner(index, offset, count, back):
+    if count & (count - 1) == 0:
+        return index ^ offset
+    return (index - offset if back else index + offset) % count
+
+
+def hand_out(value, sends):
+    chunks, rows = len(sends), sends[0].shape[1]
+    me = lax.axis_index("asc")
+    for d, send in enumerate(sends):
+        start = pl.multiple_of(partner(me, d, chunks, False) * rows, rows)
+        for role in range(2):
+            send[role] = value[role, pl.ds(start, rows), :]
+
+
+def take_in(gots, own, flat_got):
+    chunks, rows = len(gots) + 1, own.shape[1]
+    me = lax.axis_index("asc")
+    for d, got in enumerate([own] + list(gots)):
+        start = pl.multiple_of(partner(me, d, chunks, True) * rows, rows)
+        for role in range(2):
+            flat_got[role, pl.ds(start, rows), :] = got[role]
+
+
+def backward_forward(tables, ids, z_ref, phis, finish, value_ref, sends):
     owned = finish.owned
     steps, double, width = phis[0].shape
     terms = double // 2
@@ -283,10 +306,7 @@
             return carry
 
         lax.fori_loop(0, table[table.shape[0] - 1], block, 0)
-    rows = send.shape[2]
-    for j in range(chunks):
-        for role in range(2):
-            send[j, role] = value_ref[role, j * rows : (j + 1) * rows, :]
+    hand_out(value_ref, sends)
 
 
 class Finish:
@@ -306,10 +326,11 @@
     z_ref[2 * role : 2 * role + 2, count:] = jnp.zeros((2, DUMMY_ROWS, LANES), F32)
 
 
-def cross_values(chunks, got, sent, role):
+def cross_values(flat_got, mine, role):
+    count = flat_got.shape[1]
     if role == 0:
-        return flat(sent, 0, chunks) - flat(got, 1, chunks)
-    return flat(got, 0, chunks) - flat(sent, 1, chunks)
+        return mine[0, :count] - flat_got[1]
+    return flat_got[0] - mine[1, :count]
 
 
 def weigh(model, meta, role, weights, z_ref):
@@ -322,11 +343,14 @@
 
 
 def first_kernel(
-    chunks, got, sent, meta_a, meta_d, phi_a, phi_d, table_a, table_d, state_a, state_d,
-    model, weights, basis, send, z_ref, value_ref,
+    chunks, own, mine, meta_a, meta_d, phi_a, phi_d, table_a, table_d, state_a, state_d, *rest,
 ):
+    gots, rest = rest[: chunks - 1], rest[chunks - 1 :]
+    model, weights, basis, value_ref = rest[:4]
+    sends, (z_ref, flat_got) = rest[4 : 4 + chunks], rest[4 + chunks :]
+    take_in(gots, own, flat_got)
     for role, meta in enumerate((meta_a, meta_d)):
-        values = cross_values(chunks, got, sent, role)
+        values = cross_values(flat_got, mine, role)
         model[role] = values
         weigh(values, meta, role, weights, z_ref)
 
@@ -336,17 +360,20 @@
         return new
 
     backward_forward(
-        chunks, (table_a, table_d), (meta_a.at[0], meta_d.at[0]), z_ref, (phi_a, phi_d),
-        Finish(state_a.shape[0], finish), send, value_ref,
+        (table_a, table_d), (meta_a.at[0], meta_d.at[0]), z_ref, (phi_a, phi_d),
+        Finish(state_a.shape[0], finish), value_ref, sends,
     )
 
 
 def image_kernel(
-    chunks, got, sent, meta_a, meta_d, phi_a, phi_d, table_a, table_d, weights, before,
-    crossed, basis, send, z_ref, value_ref,
+    chunks, own, mine, meta_a, meta_d, phi_a, phi_d, table_a, table_d, weights, before, *rest,
 ):
-    for role, meta in enumerate((meta_a, meta_d)):
-        values = cross_values(chunks, got, sent, role)
+    gots, rest = rest[: chunks - 1], rest[chunks - 1 :]
+    crossed, basis, value_ref = rest[:3]
+    sends, (z_ref, flat_got) = rest[3 : 3 + chunks], rest[3 + chunks :]
+    take_in(gots, own, flat_got)
+    for role in range(2):
+        values = cross_values(flat_got, mine, role)
         crossed[role] = values
         store_split(z_ref, role, weights[role] * values)
 
@@ -359,8 +386,8 @@
         return new
 
     backward_forward(
-        chunks, (table_a, table_d), (meta_a.at[0], meta_d.at[0]), z_ref, (phi_a, phi_d),
-        Finish(before.shape[1], finish), send, value_ref,
+        (table_a, table_d), (meta_a.at[0], meta_d.at[0]), z_ref, (phi_a, phi_d),
+        Finish(before.shape[1], finish), value_ref, sends,
     )
 
 
@@ -372,11 +399,12 @@
 
 
 def gram_kernel(
-    chunks, got, sent, weights, crossed_0, crossed_1, basis_0, basis_1, basis_2,
-    crossed_2, scalars,
+    chunks, own, mine, weights, crossed_0, crossed_1, basis_0, basis_1, basis_2, *rest,
 ):
+    gots, (crossed_2, scalars, flat_got) = rest[: chunks - 1], rest[chunks - 1 :]
+    take_in(gots, own, flat_got)
     for role in range(2):
-        crossed_2[role] = cross_values(chunks, got, sent, role)
+        crossed_2[role] = cross_values(flat_got, mine, role)
     weight = weights[0]
     values = [crossed_0[0], crossed_1[0], crossed_2[0]]
     bases = [basis_0, basis_1, basis_2]
@@ -435,8 +463,9 @@
 def next_kernel(
     chunks, scalars, meta_a, meta_d, phi_a, phi_d, table_a, table_d, state_a, state_d, model,
     crossed_0, crossed_1, crossed_2, basis_0, basis_1, basis_2,
-    new_state_a, new_state_d, new_model, weights, basis, send, z_ref, value_ref,
+    new_state_a, new_state_d, new_model, weights, basis, value_ref, *rest,
 ):
+    sends, (z_ref,) = rest[:chunks], rest[chunks:]
     y = solve(scalars)
     for role, meta in enumerate((meta_a, meta_d)):
         values = model[role] + combine(y, [crossed_0[role], crossed_1[role], crossed_2[role]])
@@ -451,8 +480,8 @@
         return new
 
     backward_forward(
-        chunks, (table_a, table_d), (meta_a.at[0], meta_d.at[0]), z_ref, (phi_a, phi_d),
-        Finish(state_a.shape[0], finish), send, value_ref,
+        (table_a, table_d), (meta_a.at[0], meta_d.at[0]), z_ref, (phi_a, phi_d),
+        Finish(state_a.shape[0], finish), value_ref, sends,
     )
 
 
@@ -511,78 +540,81 @@
     at_asc = at_asc.reshape(na, FIELDS, rows, LANES)
     at_desc = lax.all_to_all(at_asc, "asc", split_axis=0, concat_axis=0, tiled=True)
 
+    padded = all_rows + DUMMY_ROWS
     phi_shape = shape((steps, 2 * terms, step_width), BF16)
-    meta_shape = shape((2, all_rows + DUMMY_ROWS, LANES), F32)
-    table_shape = shape((all_rows + rows + STEP_ROWS * UNROLL + 1,), jnp.int32)
-    send_shape = shape((na, 2, rows, LANES), F32)
+    meta_shape = shape((2, padded, LANES), F32)
+    table_shape = shape((all_rows + rows + group + 1,), jnp.int32)
+    value_shape = shape((2, padded, LANES), F32)
+    send_shapes = [shape((2, rows, LANES), F32)] * na
     pair_shape = shape((2, all_rows, LANES), F32)
     field_shape = shape((2, owned_asc, terms), F32)
-    flat_scratch = pltpu.VMEM((all_rows + DUMMY_ROWS, LANES), F32)
-    pass_scratch = [
-        pltpu.VMEM((4, all_rows + DUMMY_ROWS, LANES), F32),
-        pltpu.VMEM((2, all_rows + DUMMY_ROWS, LANES), F32),
-    ]
-    phi_a, value_asc, meta_a, table_a = call(
-        functools.partial(setup_asc_kernel, na),
-        [phi_shape, shape((all_rows + DUMMY_ROWS, LANES), F32), meta_shape, table_shape],
-        [flat_scratch],
-        at_asc, coef_asc,
-    )
-    phi_d, meta_d, sent, table_d = call(
-        functools.partial(setup_desc_kernel, na),
-        [phi_shape, meta_shape, send_shape, table_shape],
-        [flat_scratch, flat_scratch],
-        at_desc, role_desc, value_asc,
-    )
-
-    def exchange(x):
-        return lax.all_to_all(x, "asc", split_axis=0, concat_axis=0, tiled=True)
+    z_scratch = pltpu.VMEM((4, padded, LANES), F32)
+    got_scratch = pltpu.VMEM((2, all_rows, LANES), F32)
+    outs = call(
+        functools.partial(setup_kernel, na),
+        [meta_shape] * 2 + [phi_shape] * 2 + [table_shape] * 2 + [value_shape] + send_shapes,
+        [pltpu.VMEM((padded, LANES), F32)],
+        at_asc, at_desc, coef_asc, role_desc,
+    )
+    fixed, mine, sends = outs[:6], outs[6], outs[7:]
+
+    def exchange(chunks):
+        return [
+            lax.ppermute(
+                chunks[d], "asc", [(i, partner(i, d, na, False)) for i in range(na)]
+            )
+            for d in range(1, na)
+        ]
 
     def share(x):
         return lax.all_to_all(x, ("asc", "desc"), split_axis=0, concat_axis=0, tiled=True)
 
-    fixed = (meta_a, meta_d, phi_a, phi_d, table_a, table_d)
     state_a, state_d = coef_asc, role_desc
     for outer in range(GN_STEPS):
         if outer == 0:
-            got = exchange(sent)
-            model, weights, basis_0, sent = call(
+            gots = exchange(sends)
+            outs = call(
                 functools.partial(first_kernel, na),
-                [pair_shape, pair_shape, field_shape, send_shape],
-                pass_scratch,
-                got, sent, *fixed, state_a, state_d,
+                [pair_shape, pair_shape, field_shape, value_shape] + send_shapes,
+                [z_scratch, got_scratch],
+                sends[0], mine, *fixed, state_a, state_d, *gots,
             )
+            model, weights, basis_0, mine = outs[:4]
+            sends = outs[4:]
         else:
-            state_a, state_d, model, weights, basis_0, sent = call(
+            outs = call(
                 functools.partial(next_kernel, na),
                 [
                     shape(state_a.shape, F32), shape(state_d.shape, F32),
-                    pair_shape, pair_shape, field_shape, send_shape,
-                ],
-                pass_scratch,
+                    pair_shape, pair_shape, field_shape, value_shape,
+                ] + send_shapes,
+                [z_scratch],
                 scalars, *fixed, state_a, state_d, model,
                 *crossed, *bases,
             )
+            state_a, state_d, model, weights, basis_0, mine = outs[:6]
+            sends = outs[6:]
         bases, crossed = [basis_0], []
         for inner in range(2):
-            got = exchange(sent)
-            crossed_now, basis_now, sent = call(
+            gots = exchange(sends)
+            outs = call(
                 functools.partial(image_kernel, na),
-                [pair_shape, field_shape, send_shape],
-                pass_scratch,
-                got, sent, *fixed, weights, bases[-1],
+                [pair_shape, field_shape, value_shape] + send_shapes,
+                [z_scratch, got_scratch],
+                sends[0], mine, *fixed, weights, bases[-1], *gots,
             )
-            crossed.append(crossed_now)
-            bases.append(basis_now)
+            crossed.append(outs[0])
+            bases.append(outs[1])
+            mine, sends = outs[2], outs[3:]
         if outer + 1 == GN_STEPS:
             leaving = jnp.stack([state_d, bases[0][1], bases[1][1], bases[2][1]])
             native = lax.ppermute(leaving, ("asc", "desc"), to_native)
-        got = exchange(sent)
+        gots = exchange(sends)
         crossed_now, scalars = call(
             functools.partial(gram_kernel, na),
             [pair_shape, shape((na * nd, 8, LANES), F32)],
-            [],
-            got, sent, weights, *crossed, *bases,
+            [got_scratch],
+            sends[0], mine, weights, *crossed, *bases, *gots,
         )
         crossed.append(crossed_now)
         scalars = share(scalars)

time: 145 us -> 154 us (1.062)
  the two profiles are of different devices: /device:TPU:25 before, /device:TPU:0 now
where the time goes in v3:
time: 154 us; the launch traced here: 152 us
  starting transfers between devices  56.6 us (37%)
  Pallas kernels  38.7 us (25%)
  waiting for transfers between devices  31.2 us (20%)
  blocking collectives  24.2 us (16%)
    ppermute x49, starting transfers between devices, exchange(): lax.ppermute(chunks[d], 'asc', [(i, partner(i, d, na, False)) for i in ra...  47.6 us
    pallas_call x11, Pallas kernels, call(): pl.pallas_call(kernel, out_shape=outs, in_specs=[place(x) for x in args]...  38.7 us
    ppermute x49, waiting for transfers between devices, exchange(): lax.ppermute(chunks[d], 'asc', [(i, partner(i, d, na, False)) for i in ra...  19 us
    all_to_all x1, blocking collectives, body(): lax.all_to_all(packed, 'desc', split_axis=0, concat_axis=0, tiled=True)  13.4 us
    all_to_all x1, blocking collectives, share(): lax.all_to_all(x, ('asc', 'desc'), split_axis=0, concat_axis=0, tiled=True)  10.8 us
    all_to_all x1, waiting for transfers between devices, share(): lax.all_to_all(x, ('asc', 'desc'), split_axis=0, concat_axis=0, tiled=True)  7.67 us
    all_to_all x1, waiting for transfers between devices, body(): lax.all_to_all(at_asc, 'asc', split_axis=0, concat_axis=0, tiled=True)  4.52 us
    all_to_all x1, starting transfers between devices, body(): lax.all_to_all(at_asc, 'asc', split_axis=0, concat_axis=0, tiled=True)  3.72 us
  transfers between devices with their start and end apart: 53, of which 16 were waited for; matrix products, arithmetic and copies ran while one was open for 0% of the time, Pallas kernels for 0%

profile of v3, /device:TPU:0, one launch (start us, length us, event | category | flops | bytes accessed | tf_op | source)
XLA Modules:
  0.0 152.3 jit_solution(11089322919340840080)
XLA Ops:
  0.6 2.2 %shard_map.95 = f32[4,2,5,8,128]{4,3,2,1,0:T(8,128)} custom-call(s32[64,128]{1,0:T(8,128)} %ca_in.1, s32[64,128]{1,0:T(8,128)} %cd_in.1, f32[64,128]{1,0:T(8,128)} %ta_in.1, f32[64,128]{1,0:T(8,128)} %td_in.1, f32[64,128]{1,0:T(8,128)} %height_in.1, s32[1,64]{1,0:T(1,128)} %bitcast.4), custom_call_target="tpu_custom_call" | custom-call | tf_op jit(solution)/shard_map/pallas_call | solution.py:509
  2.8 13.4 %all_to_all.20 = f32[4,2,5,8,128]{4,3,2,1,0:T(8,128)} all-to-all(f32[4,2,5,8,128]{4,3,2,1,0:T(8,128)} %shard_map.95), channel_id=1, replica_groups=mesh['asc'=8,'desc'=4] {'desc'}, dimensions={0} | all-to-all | bytes 327680 | tf_op jit(solution)/shard_map/all_to_all | solution.py:539
  16.2 3.7 %all-to-all-start.1 = ((f32[8,5,8,128]{3,2,1,0:T(8,128)}), f32[8,5,8,128]{3,2,1,0:T(8,128)S(1)}, u32[]{:S(2)}, u32[]{:S(2)}) async-start(f32[8,5,8,128]{3,2,1,0:T(8,128)} %bitcast.1.at_asc), calls=%async_computation.1 | async-start | bytes 327680 | tf_op jit(solution)/shard_map/all_to_all | solution.py:541
  21.3 4.5 %all-to-all-done.1.at_desc = f32[8,5,8,128]{3,2,1,0:T(8,128)S(1)} async-done(((f32[8,5,8,128]{3,2,1,0:T(8,128)}), f32[8,5,8,128]{3,2,1,0:T(8,128)S(1)}, u32[]{:S(2)}, u32[]{:S(2)}) %all-to-all-start.1) | async-done | bytes 163872 | tf_op jit(solution)/shard_map/all_to_all | solution.py:541
  26.5 6.1 %shard_map.96 = (f32[2,72,128]{2,1,0:T(8,128)S(1)}, f32[2,72,128]{2,1,0:T(8,128)S(1)}, bf16[32,256,256]{2,1,0:T(8,128)(2,1)S(1)}, bf16[32,256,256]{2,1,0:T(8,128...) custom-call(f32[8,5,8,128]{3,2,1,0:T(8,128)} %bitcast.1.at_asc, ...), custom_call_target="tpu_custom_call" | custom-call | tf_op jit(solution)/shard_map/pallas_call | solution.py:509
  32.7 3.0 %collective-permute-start.2 = (f32[2,8,128]{2,1,0:T(8,128)S(1)}, f32[2,8,128]{2,1,0:T(8,128)S(1)}, u32[]{:S(2)}, u32[]{:S(2)}) collective-permute-start(f32[2,8,128]{2,1,0:T(8,128)S(1)} %get-tuple-element.98), channel_id=1, source_target_pairs={{0,8},{4,12},{8,0},{12,4},{16,24},{20,28},{24,16},{28,20},{1,9},{5... | collective-permute-start | bytes 24584 | tf_op jit(solution)/shard_map/ppermute | solution.py:563
  35.7 3.7 %collective-permute-start.4 = (f32[2,8,128]{2,1,0:T(8,128)S(1)}, f32[2,8,128]{2,1,0:T(8,128)S(1)}, u32[]{:S(2)}, u32[]{:S(2)}) collective-permute-start(f32[2,8,128]{2,1,0:T(8,128)S(1)} %get-tuple-element.100), channel_id=1, source_target_pairs={{0,16},{4,20},{8,24},{12,28},{16,0},{20,4},{24,8},{28,12},{1,17},{... | collective-permute-start | bytes 24584 | tf_op jit(solution)/shard_map/ppermute | solution.py:563
  39.4 2.9 %collective-permute-start.6 = (f32[2,8,128]{2,1,0:T(8,128)S(1)}, f32[2,8,128]{2,1,0:T(8,128)S(1)}, u32[]{:S(2)}, u32[]{:S(2)}) collective-permute-start(f32[2,8,128]{2,1,0:T(8,128)S(1)} %get-tuple-element.102), channel_id=1, source_target_pairs={{0,24},{4,28},{8,16},{12,20},{16,8},{20,12},{24,0},{28,4},{1,25},{... | collective-permute-start | bytes 24584 | tf_op jit(solution)/shard_map/ppermute | solution.py:563
  43.9 2.3 %collective-permute-done.7.rest_6_ = f32[2,8,128]{2,1,0:T(8,128)S(1)} collective-permute-done((f32[2,8,128]{2,1,0:T(8,128)S(1)}, f32[2,8,128]{2,1,0:T(8,128)S(1)}, u32[]{:S(2)}, u32[]{:S(2)}) %collective-permute-start.7) | collective-permute-done | bytes 8224 | tf_op jit(solution)/shard_map/ppermute | solution.py:563
  46.2 4.7 %shard_map.97 = (f32[2,64,128]{2,1,0:T(8,128)S(1)}, f32[2,64,128]{2,1,0:T(8,128)S(1)}, f32[2,32,128]{2,1,0:T(8,128)S(1)}, f32[2,72,128]{2,1,0:T(8,128)S(1)}, f32...) custom-call(f32[2,8,128]{2,1,0:T(8,128)S(1)} %get-tuple-element.89.o, ...), custom_call_target="tpu_custom_call" | custom-call | tf_op jit(solution)/shard_map/pallas_call | solution.py:509
  51.1 1.8 %collective-permute-start.10 = (f32[2,8,128]{2,1,0:T(8,128)S(1)}, f32[2,8,128]{2,1,0:T(8,128)S(1)}, u32[]{:S(2)}, u32[]{:S(2)}) collective-permute-start(f32[2,8,128]{2,1,0:T(8,128)S(1)} %get-tuple-element.110), channel_id=1, source_target_pairs={{0,12},{4,8},{8,4},{12,0},{16,28},{20,24},{24,20},{28,16},{1,13},{... | collective-permute-start | bytes 24584 | tf_op jit(solution)/shard_map/ppermute | solution.py:563
  55.1 2.1 %collective-permute-start.14 = (f32[2,8,128]{2,1,0:T(8,128)S(1)}, f32[2,8,128]{2,1,0:T(8,128)S(1)}, u32[]{:S(2)}, u32[]{:S(2)}) collective-permute-start(f32[2,8,128]{2,1,0:T(8,128)S(1)} %get-tuple-element.114), channel_id=1, source_target_pairs={{0,28},{4,24},{8,20},{12,16},{16,12},{20,8},{24,4},{28,0},{1,29},{... | collective-permute-start | bytes 24584 | tf_op jit(solution)/shard_map/ppermute | solution.py:563
  57.3 1.9 %collective-permute-done.13.rest_5_ = f32[2,8,128]{2,1,0:T(8,128)S(1)} collective-permute-done((f32[2,8,128]{2,1,0:T(8,128)S(1)}, f32[2,8,128]{2,1,0:T(8,128)S(1)}, u32[]{:S(2)}, u32[]{:S(2)}) %collective-permute-start.13) | collective-permute-done | bytes 8224 | tf_op jit(solution)/shard_map/ppermute | solution.py:563
  59.2 4.7 %shard_map.98 = (f32[2,64,128]{2,1,0:T(8,128)S(1)}, f32[2,32,128]{2,1,0:T(8,128)S(1)}, f32[2,72,128]{2,1,0:T(8,128)S(1)}, f32[2,8,128]{2,1,0:T(8,128)S(1)}, f32[...) custom-call(f32[2,8,128]{2,1,0:T(8,128)S(1)} %get-tuple-element.104., ...), custom_call_target="tpu_custom_call" | custom-call | tf_op jit(solution)/shard_map/pallas_call | solution.py:509
  67.5 2.4 %collective-permute-start.20 = (f32[2,8,128]{2,1,0:T(8,128)S(1)}, f32[2,8,128]{2,1,0:T(8,128)S(1)}, u32[]{:S(2)}, u32[]{:S(2)}) collective-permute-start(f32[2,8,128]{2,1,0:T(8,128)S(1)} %get-tuple-element.123), channel_id=1, source_target_pairs={{0,24},{4,28},{8,16},{12,20},{16,8},{20,12},{24,0},{28,4},{1,25},{... | collective-permute-start | bytes 24584 | tf_op jit(solution)/shard_map/ppermute | solution.py:563
  70.2 1.8 %collective-permute-done.20.rest_5_ = f32[2,8,128]{2,1,0:T(8,128)S(1)} collective-permute-done((f32[2,8,128]{2,1,0:T(8,128)S(1)}, f32[2,8,128]{2,1,0:T(8,128)S(1)}, u32[]{:S(2)}, u32[]{:S(2)}) %collective-permute-start.20) | collective-permute-done | bytes 8224 | tf_op jit(solution)/shard_map/ppermute | solution.py:563
  72.0 1.8 %collective-permute-done.21.rest_6_ = f32[2,8,128]{2,1,0:T(8,128)S(1)} collective-permute-done((f32[2,8,128]{2,1,0:T(8,128)S(1)}, f32[2,8,128]{2,1,0:T(8,128)S(1)}, u32[]{:S(2)}, u32[]{:S(2)}) %collective-permute-start.21) | collective-permute-done | bytes 8224 | tf_op jit(solution)/shard_map/ppermute | solution.py:563
  73.9 4.7 %shard_map.99 = (f32[2,64,128]{2,1,0:T(8,128)S(1)}, f32[2,32,128]{2,1,0:T(8,128)S(1)}, f32[2,72,128]{2,1,0:T(8,128)S(1)}, f32[2,8,128]{2,1,0:T(8,128)S(1)}, f32[...) custom-call(f32[2,8,128]{2,1,0:T(8,128)S(1)} %get-tuple-element.115., ...), custom_call_target="tpu_custom_call" | custom-call | tf_op jit(solution)/shard_map/pallas_call | solution.py:509
  82.8 2.1 %collective-permute-start.28 = (f32[2,8,128]{2,1,0:T(8,128)S(1)}, f32[2,8,128]{2,1,0:T(8,128)S(1)}, u32[]{:S(2)}, u32[]{:S(2)}) collective-permute-start(f32[2,8,128]{2,1,0:T(8,128)S(1)} %get-tuple-element.136), channel_id=1, source_target_pairs={{0,28},{4,24},{8,20},{12,16},{16,12},{20,8},{24,4},{28,0},{1,29},{... | collective-permute-start | bytes 24584 | tf_op jit(solution)/shard_map/ppermute | solution.py:563
  84.9 1.9 %collective-permute-done.27.rest_5_ = f32[2,8,128]{2,1,0:T(8,128)S(1)} collective-permute-done((f32[2,8,128]{2,1,0:T(8,128)S(1)}, f32[2,8,128]{2,1,0:T(8,128)S(1)}, u32[]{:S(2)}, u32[]{:S(2)}) %collective-permute-start.27) | collective-permute-done | bytes 8224 | tf_op jit(solution)/shard_map/ppermute | solution.py:563
  87.0 10.8 %all_to_all.21.scalars = f32[32,8,128]{2,1,0:T(8,128)S(1)} all-to-all(f32[32,8,128]{2,1,0:T(8,128)S(1)} %get-tuple-element.137), channel_id=1, replica_groups=mesh['asc'=8,'desc'=4] {'asc','desc'}, dimensions={0} | all-to-all | bytes 262144 | tf_op jit(solution)/shard_map/all_to_all | solution.py:570
  97.8 5.4 %shard_map.101 = (f32[32,128]{1,0:T(8,128)S(1)}, f32[32,128]{1,0:T(8,128)S(1)}, f32[2,64,128]{2,1,0:T(8,128)}, f32[2,64,128]{2,1,0:T(8,128)S(1)}, f32[2,32,128]{...) custom-call(f32[32,8,128]{2,1,0:T(8,128)S(1)} %all_to_all.21.scalars, ...), custom_call_target="tpu_custom_call" | custom-call | tf_op jit(solution)/shard_map/pallas_call | solution.py:509
  107.1 2.4 %collective-permute-start.35 = (f32[2,8,128]{2,1,0:T(8,128)S(1)}, f32[2,8,128]{2,1,0:T(8,128)S(1)}, u32[]{:S(2)}, u32[]{:S(2)}) collective-permute-start(f32[2,8,128]{2,1,0:T(8,128)S(1)} %get-tuple-element.150), channel_id=1, source_target_pairs={{0,28},{4,24},{8,20},{12,16},{16,12},{20,8},{24,4},{28,0},{1,29},{... | collective-permute-start | bytes 24584 | tf_op jit(solution)/shard_map/ppermute | solution.py:563
  111.3 4.7 %shard_map.102 = (f32[2,64,128]{2,1,0:T(8,128)S(1)}, f32[2,32,128]{2,1,0:T(8,128)S(1)}, f32[2,72,128]{2,1,0:T(8,128)S(1)}, f32[2,8,128]{2,1,0:T(8,128)S(1)}, f32...) custom-call(f32[2,8,128]{2,1,0:T(8,128)S(1)} %get-tuple-element.140., ...), custom_call_target="tpu_custom_call" | custom-call | tf_op jit(solution)/shard_map/pallas_call | solution.py:509
  119.8 2.4 %collective-permute-start.41 = (f32[2,8,128]{2,1,0:T(8,128)S(1)}, f32[2,8,128]{2,1,0:T(8,128)S(1)}, u32[]{:S(2)}, u32[]{:S(2)}) collective-permute-start(f32[2,8,128]{2,1,0:T(8,128)S(1)} %get-tuple-element.159), channel_id=1, source_target_pairs={{0,24},{4,28},{8,16},{12,20},{16,8},{20,12},{24,0},{28,4},{1,25},{... | collective-permute-start | bytes 24584 | tf_op jit(solution)/shard_map/ppermute | solution.py:563
  122.5 1.8 %collective-permute-done.41.rest_5_ = f32[2,8,128]{2,1,0:T(8,128)S(1)} collective-permute-done((f32[2,8,128]{2,1,0:T(8,128)S(1)}, f32[2,8,128]{2,1,0:T(8,128)S(1)}, u32[]{:S(2)}, u32[]{:S(2)}) %collective-permute-start.41) | collective-permute-done | bytes 8224 | tf_op jit(solution)/shard_map/ppermute | solution.py:563
  124.3 1.9 %collective-permute-done.42.rest_6_ = f32[2,8,128]{2,1,0:T(8,128)S(1)} collective-permute-done((f32[2,8,128]{2,1,0:T(8,128)S(1)}, f32[2,8,128]{2,1,0:T(8,128)S(1)}, u32[]{:S(2)}, u32[]{:S(2)}) %collective-permute-start.42) | collective-permute-done | bytes 8224 | tf_op jit(solution)/shard_map/ppermute | solution.py:563
  126.2 4.7 %shard_map.103 = (f32[2,64,128]{2,1,0:T(8,128)S(1)}, f32[2,32,128]{2,1,0:T(8,128)S(1)}, f32[2,72,128]{2,1,0:T(8,128)S(1)}, f32[2,8,128]{2,1,0:T(8,128)S(1)}, f32...) custom-call(f32[2,8,128]{2,1,0:T(8,128)S(1)} %get-tuple-element.151., ...), custom_call_target="tpu_custom_call" | custom-call | tf_op jit(solution)/shard_map/pallas_call | solution.py:509
  135.1 2.1 %collective-permute-start.49 = (f32[2,8,128]{2,1,0:T(8,128)S(1)}, f32[2,8,128]{2,1,0:T(8,128)S(1)}, u32[]{:S(2)}, u32[]{:S(2)}) collective-permute-start(f32[2,8,128]{2,1,0:T(8,128)S(1)} %get-tuple-element.172), channel_id=1, source_target_pairs={{0,28},{4,24},{8,20},{12,16},{16,12},{20,8},{24,4},{28,0},{1,29},{... | collective-permute-start | bytes 24584 | tf_op jit(solution)/shard_map/ppermute | solution.py:563
  137.2 1.9 %collective-permute-done.48.rest_5_ = f32[2,8,128]{2,1,0:T(8,128)S(1)} collective-permute-done((f32[2,8,128]{2,1,0:T(8,128)S(1)}, f32[2,8,128]{2,1,0:T(8,128)S(1)}, u32[]{:S(2)}, u32[]{:S(2)}) %collective-permute-start.48) | collective-permute-done | bytes 8224 | tf_op jit(solution)/shard_map/ppermute | solution.py:563
  139.9 3.3 %all-to-all-start.3 = ((f32[32,8,128]{2,1,0:T(8,128)}), f32[32,8,128]{2,1,0:T(8,128)S(1)}, u32[]{:S(2)}, u32[]{:S(2)}) async-start(f32[32,8,128]{2,1,0:T(8,128)} %get-tuple-element.173), calls=%async_computation.3 | async-start | bytes 262144 | tf_op jit(solution)/shard_map/all_to_all | solution.py:570
  143.9 7.7 %all-to-all-done.3.scalars = f32[32,8,128]{2,1,0:T(8,128)S(1)} async-done(((f32[32,8,128]{2,1,0:T(8,128)}), f32[32,8,128]{2,1,0:T(8,128)S(1)}, u32[]{:S(2)}, u32[]{:S(2)}) %all-to-all-start.3) | async-done | bytes 131104 | tf_op jit(solution)/shard_map/all_to_all | solution.py:570
  (95 shorter events, 31.1 us)
Async XLA Ops:
  16.2 9.6 %all-to-all-start.1 = ((f32[8,5,8,128]{3,2,1,0:T(8,128)}), f32[8,5,8,128]{3,2,1,0:T(8,128)S(1)}, u32[]{:S(2)}, u32[]{:S(2)}) async-start(f32[8,5,8,128]{3,2,1,0:T(8,128)} %bitcast.1.at_asc), calls=%async_computation.1 | async-start | bytes 327680 | tf_op jit(solution)/shard_map/all_to_all | solution.py:541
  32.6 6.7 %collective-permute-start.1 = (f32[2,8,128]{2,1,0:T(8,128)S(1)}, f32[2,8,128]{2,1,0:T(8,128)S(1)}, u32[]{:S(2)}, u32[]{:S(2)}) collective-permute-start(f32[2,8,128]{2,1,0:T(8,128)S(1)} %get-tuple-element.97), channel_id=1, source_target_pairs={{0,4},{4,0},{8,12},{12,8},{16,20},{20,16},{24,28},{28,24},{1,5},{5... | collective-permute-start | bytes 24584 | tf_op jit(solution)/shard_map/ppermute | solution.py:563
  32.7 9.5 %collective-permute-start.2 = (f32[2,8,128]{2,1,0:T(8,128)S(1)}, f32[2,8,128]{2,1,0:T(8,128)S(1)}, u32[]{:S(2)}, u32[]{:S(2)}) collective-permute-start(f32[2,8,128]{2,1,0:T(8,128)S(1)} %get-tuple-element.98), channel_id=1, source_target_pairs={{0,8},{4,12},{8,0},{12,4},{16,24},{20,28},{24,16},{28,20},{1,9},{5... | collective-permute-start | bytes 24584 | tf_op jit(solution)/shard_map/ppermute | solution.py:563
  35.7 6.7 %collective-permute-start.3 = (f32[2,8,128]{2,1,0:T(8,128)S(1)}, f32[2,8,128]{2,1,0:T(8,128)S(1)}, u32[]{:S(2)}, u32[]{:S(2)}) collective-permute-start(f32[2,8,128]{2,1,0:T(8,128)S(1)} %get-tuple-element.99), channel_id=1, source_target_pairs={{0,12},{4,8},{8,4},{12,0},{16,28},{20,24},{24,20},{28,16},{1,13},{... | collective-permute-start | bytes 24584 | tf_op jit(solution)/shard_map/ppermute | solution.py:563
  35.7 6.7 %collective-permute-start.4 = (f32[2,8,128]{2,1,0:T(8,128)S(1)}, f32[2,8,128]{2,1,0:T(8,128)S(1)}, u32[]{:S(2)}, u32[]{:S(2)}) collective-permute-start(f32[2,8,128]{2,1,0:T(8,128)S(1)} %get-tuple-element.100), channel_id=1, source_target_pairs={{0,16},{4,20},{8,24},{12,28},{16,0},{20,4},{24,8},{28,12},{1,17},{... | collective-permute-start | bytes 24584 | tf_op jit(solution)/shard_map/ppermute | solution.py:563
  39.4 4.6 %collective-permute-start.6 = (f32[2,8,128]{2,1,0:T(8,128)S(1)}, f32[2,8,128]{2,1,0:T(8,128)S(1)}, u32[]{:S(2)}, u32[]{:S(2)}) collective-permute-start(f32[2,8,128]{2,1,0:T(8,128)S(1)} %get-tuple-element.102), channel_id=1, source_target_pairs={{0,24},{4,28},{8,16},{12,20},{16,8},{20,12},{24,0},{28,4},{1,25},{... | collective-permute-start | bytes 24584 | tf_op jit(solution)/shard_map/ppermute | solution.py:563
  51.0 4.2 %collective-permute-start.9 = (f32[2,8,128]{2,1,0:T(8,128)S(1)}, f32[2,8,128]{2,1,0:T(8,128)S(1)}, u32[]{:S(2)}, u32[]{:S(2)}) collective-permute-start(f32[2,8,128]{2,1,0:T(8,128)S(1)} %get-tuple-element.109), channel_id=1, source_target_pairs={{0,8},{4,12},{8,0},{12,4},{16,24},{20,28},{24,16},{28,20},{1,9},{5... | collective-permute-start | bytes 24584 | tf_op jit(solution)/shard_map/ppermute | solution.py:563
  51.1 6.2 %collective-permute-start.10 = (f32[2,8,128]{2,1,0:T(8,128)S(1)}, f32[2,8,128]{2,1,0:T(8,128)S(1)}, u32[]{:S(2)}, u32[]{:S(2)}) collective-permute-start(f32[2,8,128]{2,1,0:T(8,128)S(1)} %get-tuple-element.110), channel_id=1, source_target_pairs={{0,12},{4,8},{8,4},{12,0},{16,28},{20,24},{24,20},{28,16},{1,13},{... | collective-permute-start | bytes 24584 | tf_op jit(solution)/shard_map/ppermute | solution.py:563
  52.8 4.4 %collective-permute-start.11 = (f32[2,8,128]{2,1,0:T(8,128)S(1)}, f32[2,8,128]{2,1,0:T(8,128)S(1)}, u32[]{:S(2)}, u32[]{:S(2)}) collective-permute-start(f32[2,8,128]{2,1,0:T(8,128)S(1)} %get-tuple-element.111), channel_id=1, source_target_pairs={{0,16},{4,20},{8,24},{12,28},{16,0},{20,4},{24,8},{28,12},{1,17},{... | collective-permute-start | bytes 24584 | tf_op jit(solution)/shard_map/ppermute | solution.py:563
  54.5 4.6 %collective-permute-start.13 = (f32[2,8,128]{2,1,0:T(8,128)S(1)}, f32[2,8,128]{2,1,0:T(8,128)S(1)}, u32[]{:S(2)}, u32[]{:S(2)}) collective-permute-start(f32[2,8,128]{2,1,0:T(8,128)S(1)} %get-tuple-element.113), channel_id=1, source_target_pairs={{0,24},{4,28},{8,16},{12,20},{16,8},{20,12},{24,0},{28,4},{1,25},{... | collective-permute-start | bytes 24584 | tf_op jit(solution)/shard_map/ppermute | solution.py:563
  55.1 4.0 %collective-permute-start.14 = (f32[2,8,128]{2,1,0:T(8,128)S(1)}, f32[2,8,128]{2,1,0:T(8,128)S(1)}, u32[]{:S(2)}, u32[]{:S(2)}) collective-permute-start(f32[2,8,128]{2,1,0:T(8,128)S(1)} %get-tuple-element.114), channel_id=1, source_target_pairs={{0,28},{4,24},{8,20},{12,16},{16,12},{20,8},{24,4},{28,0},{1,29},{... | collective-permute-start | bytes 24584 | tf_op jit(solution)/shard_map/ppermute | solution.py:563
  63.9 5.9 %collective-permute-start.16 = (f32[2,8,128]{2,1,0:T(8,128)S(1)}, f32[2,8,128]{2,1,0:T(8,128)S(1)}, u32[]{:S(2)}, u32[]{:S(2)}) collective-permute-start(f32[2,8,128]{2,1,0:T(8,128)S(1)} %get-tuple-element.119), channel_id=1, source_target_pairs={{0,8},{4,12},{8,0},{12,4},{16,24},{20,28},{24,16},{28,20},{1,9},{5... | collective-permute-start | bytes 24584 | tf_op jit(solution)/shard_map/ppermute | solution.py:563
  65.3 4.9 %collective-permute-start.17 = (f32[2,8,128]{2,1,0:T(8,128)S(1)}, f32[2,8,128]{2,1,0:T(8,128)S(1)}, u32[]{:S(2)}, u32[]{:S(2)}) collective-permute-start(f32[2,8,128]{2,1,0:T(8,128)S(1)} %get-tuple-element.120), channel_id=1, source_target_pairs={{0,12},{4,8},{8,4},{12,0},{16,28},{20,24},{24,20},{28,16},{1,13},{... | collective-permute-start | bytes 24584 | tf_op jit(solution)/shard_map/ppermute | solution.py:563
  65.8 4.4 %collective-permute-start.18 = (f32[2,8,128]{2,1,0:T(8,128)S(1)}, f32[2,8,128]{2,1,0:T(8,128)S(1)}, u32[]{:S(2)}, u32[]{:S(2)}) collective-permute-start(f32[2,8,128]{2,1,0:T(8,128)S(1)} %get-tuple-element.121), channel_id=1, source_target_pairs={{0,16},{4,20},{8,24},{12,28},{16,0},{20,4},{24,8},{28,12},{1,17},{... | collective-permute-start | bytes 24584 | tf_op jit(solution)/shard_map/ppermute | solution.py:563
  67.5 4.6 %collective-permute-start.20 = (f32[2,8,128]{2,1,0:T(8,128)S(1)}, f32[2,8,128]{2,1,0:T(8,128)S(1)}, u32[]{:S(2)}, u32[]{:S(2)}) collective-permute-start(f32[2,8,128]{2,1,0:T(8,128)S(1)} %get-tuple-element.123), channel_id=1, source_target_pairs={{0,24},{4,28},{8,16},{12,20},{16,8},{20,12},{24,0},{28,4},{1,25},{... | collective-permute-start | bytes 24584 | tf_op jit(solution)/shard_map/ppermute | solution.py:563
  78.6 4.2 %collective-permute-start.23 = (f32[2,8,128]{2,1,0:T(8,128)S(1)}, f32[2,8,128]{2,1,0:T(8,128)S(1)}, u32[]{:S(2)}, u32[]{:S(2)}) collective-permute-start(f32[2,8,128]{2,1,0:T(8,128)S(1)} %get-tuple-element.131), channel_id=1, source_target_pairs={{0,8},{4,12},{8,0},{12,4},{16,24},{20,28},{24,16},{28,20},{1,9},{5... | collective-permute-start | bytes 24584 | tf_op jit(solution)/shard_map/ppermute | solution.py:563
  79.0 5.9 %collective-permute-start.24 = (f32[2,8,128]{2,1,0:T(8,128)S(1)}, f32[2,8,128]{2,1,0:T(8,128)S(1)}, u32[]{:S(2)}, u32[]{:S(2)}) collective-permute-start(f32[2,8,128]{2,1,0:T(8,128)S(1)} %get-tuple-element.132), channel_id=1, source_target_pairs={{0,12},{4,8},{8,4},{12,0},{16,28},{20,24},{24,20},{28,16},{1,13},{... | collective-permute-start | bytes 24584 | tf_op jit(solution)/shard_map/ppermute | solution.py:563
  80.5 4.4 %collective-permute-start.25 = (f32[2,8,128]{2,1,0:T(8,128)S(1)}, f32[2,8,128]{2,1,0:T(8,128)S(1)}, u32[]{:S(2)}, u32[]{:S(2)}) collective-permute-start(f32[2,8,128]{2,1,0:T(8,128)S(1)} %get-tuple-element.133), channel_id=1, source_target_pairs={{0,16},{4,20},{8,24},{12,28},{16,0},{20,4},{24,8},{28,12},{1,17},{... | collective-permute-start | bytes 24584 | tf_op jit(solution)/shard_map/ppermute | solution.py:563
  82.2 4.6 %collective-permute-start.27 = (f32[2,8,128]{2,1,0:T(8,128)S(1)}, f32[2,8,128]{2,1,0:T(8,128)S(1)}, u32[]{:S(2)}, u32[]{:S(2)}) collective-permute-start(f32[2,8,128]{2,1,0:T(8,128)S(1)} %get-tuple-element.135), channel_id=1, source_target_pairs={{0,24},{4,28},{8,16},{12,20},{16,8},{20,12},{24,0},{28,4},{1,25},{... | collective-permute-start | bytes 24584 | tf_op jit(solution)/shard_map/ppermute | solution.py:563
  103.5 6.0 %collective-permute-start.31 = (f32[2,8,128]{2,1,0:T(8,128)S(1)}, f32[2,8,128]{2,1,0:T(8,128)S(1)}, u32[]{:S(2)}, u32[]{:S(2)}) collective-permute-start(f32[2,8,128]{2,1,0:T(8,128)S(1)} %get-tuple-element.146), channel_id=1, source_target_pairs={{0,12},{4,8},{8,4},{12,0},{16,28},{20,24},{24,20},{28,16},{1,13},{... | collective-permute-start | bytes 24584 | tf_op jit(solution)/shard_map/ppermute | solution.py:563
  105.1 4.4 %collective-permute-start.32 = (f32[2,8,128]{2,1,0:T(8,128)S(1)}, f32[2,8,128]{2,1,0:T(8,128)S(1)}, u32[]{:S(2)}, u32[]{:S(2)}) collective-permute-start(f32[2,8,128]{2,1,0:T(8,128)S(1)} %get-tuple-element.147), channel_id=1, source_target_pairs={{0,16},{4,20},{8,24},{12,28},{16,0},{20,4},{24,8},{28,12},{1,17},{... | collective-permute-start | bytes 24584 | tf_op jit(solution)/shard_map/ppermute | solution.py:563
  106.8 4.6 %collective-permute-start.34 = (f32[2,8,128]{2,1,0:T(8,128)S(1)}, f32[2,8,128]{2,1,0:T(8,128)S(1)}, u32[]{:S(2)}, u32[]{:S(2)}) collective-permute-start(f32[2,8,128]{2,1,0:T(8,128)S(1)} %get-tuple-element.149), channel_id=1, source_target_pairs={{0,24},{4,28},{8,16},{12,20},{16,8},{20,12},{24,0},{28,4},{1,25},{... | collective-permute-start | bytes 24584 | tf_op jit(solution)/shard_map/ppermute | solution.py:563
  107.1 4.2 %collective-permute-start.35 = (f32[2,8,128]{2,1,0:T(8,128)S(1)}, f32[2,8,128]{2,1,0:T(8,128)S(1)}, u32[]{:S(2)}, u32[]{:S(2)}) collective-permute-start(f32[2,8,128]{2,1,0:T(8,128)S(1)} %get-tuple-element.150), channel_id=1, source_target_pairs={{0,28},{4,24},{8,20},{12,16},{16,12},{20,8},{24,4},{28,0},{1,29},{... | collective-permute-start | bytes 24584 | tf_op jit(solution)/shard_map/ppermute | solution.py:563
  116.0 6.1 %collective-permute-start.37 = (f32[2,8,128]{2,1,0:T(8,128)S(1)}, f32[2,8,128]{2,1,0:T(8,128)S(1)}, u32[]{:S(2)}, u32[]{:S(2)}) collective-permute-start(f32[2,8,128]{2,1,0:T(8,128)S(1)} %get-tuple-element.155), channel_id=1, source_target_pairs={{0,8},{4,12},{8,0},{12,4},{16,24},{20,28},{24,16},{28,20},{1,9},{5... | collective-permute-start | bytes 24584 | tf_op jit(solution)/shard_map/ppermute | solution.py:563
  117.4 4.9 %collective-permute-start.38 = (f32[2,8,128]{2,1,0:T(8,128)S(1)}, f32[2,8,128]{2,1,0:T(8,128)S(1)}, u32[]{:S(2)}, u32[]{:S(2)}) collective-permute-start(f32[2,8,128]{2,1,0:T(8,128)S(1)} %get-tuple-element.156), channel_id=1, source_target_pairs={{0,12},{4,8},{8,4},{12,0},{16,28},{20,24},{24,20},{28,16},{1,13},{... | collective-permute-start | bytes 24584 | tf_op jit(solution)/shard_map/ppermute | solution.py:563
  117.9 4.4 %collective-permute-start.39 = (f32[2,8,128]{2,1,0:T(8,128)S(1)}, f32[2,8,128]{2,1,0:T(8,128)S(1)}, u32[]{:S(2)}, u32[]{:S(2)}) collective-permute-start(f32[2,8,128]{2,1,0:T(8,128)S(1)} %get-tuple-element.157), channel_id=1, source_target_pairs={{0,16},{4,20},{8,24},{12,28},{16,0},{20,4},{24,8},{28,12},{1,17},{... | collective-permute-start | bytes 24584 | tf_op jit(solution)/shard_map/ppermute | solution.py:563
  119.8 4.6 %collective-permute-start.41 = (f32[2,8,128]{2,1,0:T(8,128)S(1)}, f32[2,8,128]{2,1,0:T(8,128)S(1)}, u32[]{:S(2)}, u32[]{:S(2)}) collective-permute-start(f32[2,8,128]{2,1,0:T(8,128)S(1)} %get-tuple-element.159), channel_id=1, source_target_pairs={{0,24},{4,28},{8,16},{12,20},{16,8},{20,12},{24,0},{28,4},{1,25},{... | collective-permute-start | bytes 24584 | tf_op jit(solution)/shard_map/ppermute | solution.py:563
  130.9 4.2 %collective-permute-start.44 = (f32[2,8,128]{2,1,0:T(8,128)S(1)}, f32[2,8,128]{2,1,0:T(8,128)S(1)}, u32[]{:S(2)}, u32[]{:S(2)}) collective-permute-start(f32[2,8,128]{2,1,0:T(8,128)S(1)} %get-tuple-element.167), channel_id=1, source_target_pairs={{0,8},{4,12},{8,0},{12,4},{16,24},{20,28},{24,16},{28,20},{1,9},{5... | collective-permute-start | bytes 24584 | tf_op jit(solution)/shard_map/ppermute | solution.py:563
  131.3 5.9 %collective-permute-start.45 = (f32[2,8,128]{2,1,0:T(8,128)S(1)}, f32[2,8,128]{2,1,0:T(8,128)S(1)}, u32[]{:S(2)}, u32[]{:S(2)}) collective-permute-start(f32[2,8,128]{2,1,0:T(8,128)S(1)} %get-tuple-element.168), channel_id=1, source_target_pairs={{0,12},{4,8},{8,4},{12,0},{16,28},{20,24},{24,20},{28,16},{1,13},{... | collective-permute-start | bytes 24584 | tf_op jit(solution)/shard_map/ppermute | solution.py:563
  132.8 4.4 %collective-permute-start.46 = (f32[2,8,128]{2,1,0:T(8,128)S(1)}, f32[2,8,128]{2,1,0:T(8,128)S(1)}, u32[]{:S(2)}, u32[]{:S(2)}) collective-permute-start(f32[2,8,128]{2,1,0:T(8,128)S(1)} %get-tuple-element.169), channel_id=1, source_target_pairs={{0,16},{4,20},{8,24},{12,28},{16,0},{20,4},{24,8},{28,12},{1,17},{... | collective-permute-start | bytes 24584 | tf_op jit(solution)/shard_map/ppermute | solution.py:563
  134.5 4.6 %collective-permute-start.48 = (f32[2,8,128]{2,1,0:T(8,128)S(1)}, f32[2,8,128]{2,1,0:T(8,128)S(1)}, u32[]{:S(2)}, u32[]{:S(2)}) collective-permute-start(f32[2,8,128]{2,1,0:T(8,128)S(1)} %get-tuple-element.171), channel_id=1, source_target_pairs={{0,24},{4,28},{8,16},{12,20},{16,8},{20,12},{24,0},{28,4},{1,25},{... | collective-permute-start | bytes 24584 | tf_op jit(solution)/shard_map/ppermute | solution.py:563
  139.9 11.7 %all-to-all-start.3 = ((f32[32,8,128]{2,1,0:T(8,128)}), f32[32,8,128]{2,1,0:T(8,128)S(1)}, u32[]{:S(2)}, u32[]{:S(2)}) async-start(f32[32,8,128]{2,1,0:T(8,128)} %get-tuple-element.173), calls=%async_computation.3 | async-start | bytes 262144 | tf_op jit(solution)/shard_map/all_to_all | solution.py:570
  (23 other events, 97.4 us)

commit v4 on v2

v4 whole, which is shorter than its diff:
```python
import functools
import math

import jax
import jax.numpy as jnp
from jax import lax
from jax.experimental import pallas as pl
from jax.experimental.pallas import tpu as pltpu
from jax.sharding import PartitionSpec as P

GN_STEPS = 2
damping = 2.0
cauchy_square = 2.25

LANES = 128
STEP_ROWS = 2
UNROLL = 4
SETUP_UNROLL = 2
DUMMY_ROWS = 8
SCALE = 1.0 / 128.0
FIELDS = 5
PIVOT_FLOOR = 1e-6
F32 = jnp.float32
BF16 = jnp.bfloat16

COS_TERMS = [(-1.0) ** i * math.pi ** (2 * i) / math.factorial(2 * i) for i in range(8)]
SIN_TERMS = [(-1.0) ** i * math.pi ** (2 * i + 1) / math.factorial(2 * i + 1) for i in range(7)]


def in_smem(x):
    return x.dtype == jnp.int32 and len(x.shape) == 1


def params(mebibytes):
    return pltpu.CompilerParams(vmem_limit_bytes=mebibytes * 1024 * 1024)


def place(x):
    return pl.BlockSpec(memory_space=pltpu.SMEM if in_smem(x) else pltpu.VMEM)


def split(x):
    high = x.astype(BF16)
    low = (x - high.astype(F32)).astype(BF16)
    return high, low


def flat(ref, field, chunks):
    return jnp.concatenate([ref[j, field] for j in range(chunks)], axis=0)


def local_id(ids, owned):
    if owned & (owned - 1) == 0:
        return ids & (owned - 1)
    return lax.rem(ids, owned)


def pack_kernel(
    na, nd, owned_asc, owned_desc, ca_in, cd_in, ta_in, td_in, height_in, fill_in, out,
    ca, cd, ta, td, height, fill, turned, sems,
):
    copies = [
        pltpu.make_async_copy(source, target, sems.at[i])
        for i, (source, target) in enumerate(
            [
                (fill_in, fill), (ca_in, ca), (ta_in, ta),
                (cd_in, cd), (td_in, td), (height_in, height),
            ]
        )
    ]
    for copy in copies:
        copy.start()
    for copy in copies:
        copy.wait()
    blocks, width = ca.shape
    group = width // na
    rows = blocks // na
    fill_row = fill[...]
    row_id = lax.broadcasted_iota(jnp.int32, (blocks, blocks), 0)
    col_id = lax.broadcasted_iota(jnp.int32, (blocks, blocks), 1)
    fill_col = jnp.sum(
        jnp.where(row_id == col_id, fill_row, 0).astype(F32), axis=1, keepdims=True
    )
    lane = lax.broadcasted_iota(jnp.int32, (blocks, width), 1)
    live = lane.astype(F32) < fill_col
    fields = [
        jnp.where(live, local_id(ca[...], owned_asc).astype(F32), -1.0),
        ta[...],
        jnp.where(live, local_id(cd[...], owned_desc).astype(F32), -1.0),
        td[...],
        height[...],
    ]
    source = lax.broadcasted_iota(jnp.int32, (width, width), 0)
    target = lax.broadcasted_iota(jnp.int32, (width, width), 1)
    owner = target // group
    place = target - owner * group
    order = (source == place * na + owner).astype(F32).astype(BF16)
    for f, x in enumerate(fields):
        high = x.astype(BF16)
        rest = x - high.astype(F32)
        middle = rest.astype(BF16)
        low = (rest - middle.astype(F32)).astype(BF16)
        turned[f] = (
            jnp.dot(high, order, preferred_element_type=F32)
            + jnp.dot(middle, order, preferred_element_type=F32)
        ) + jnp.dot(low, order, preferred_element_type=F32)
    lane_group = lax.broadcasted_iota(jnp.int32, (rows, width), 1) // group
    for f in range(FIELDS):
        parts = [None] * na
        for k in range(na):
            piece = turned[f, pl.ds(k, rows, stride=na), :]
            for r in range(na):
                amount = ((k - r) * group) % width
                moved = pltpu.roll(piece, amount, 1) if amount else piece
                parts[r] = moved if k == 0 else jnp.where(lane_group == k, moved, parts[r])
        for r in range(na):
            out[r % nd, r // nd, f] = parts[r]


def cos_sin_pi(x):
    turns = jnp.floor(x + 0.5)
    f = x - turns
    sign = 1.0 - 2.0 * (turns - 2.0 * jnp.floor(turns * 0.5))
    u = f * f
    c = COS_TERMS[-1]
    for term in COS_TERMS[-2::-1]:
        c = c * u + term
    s = SIN_TERMS[-1]
    for term in SIN_TERMS[-2::-1]:
        s = s * u + term
    return c * sign, s * (f * sign)


def rows_pair(ref, rows):
    return jnp.concatenate([ref[pl.ds(r, 1), :] for r in rows], axis=1)


def used_rows(ids_ref, chunks, rows, table):
    count = jnp.int32(0)
    level = lax.broadcasted_iota(jnp.int32, (rows, LANES), 0).astype(F32) + 1.0
    for j in range(chunks):
        ids = ids_ref[j * rows : (j + 1) * rows, :]
        used = jnp.max(jnp.where(ids >= 0.0, level, 0.0)).astype(jnp.int32)
        for i in range(rows):
            table[count + i] = j * rows + i
        count = count + used
    group = STEP_ROWS * UNROLL
    for i in range(group):
        table[count + i] = chunks * rows
    table[table.shape[0] - 1] = lax.div(count + (group - 1), group)


def step_rows(table, n):
    return [table[n * STEP_ROWS + i] for i in range(STEP_ROWS)]


def stacked(field):
    high, low = split(field)
    top = jnp.concatenate([high, high], axis=1)
    bottom = jnp.concatenate([low, jnp.zeros_like(low)], axis=1)
    return jnp.concatenate([top, bottom], axis=0)


def forward_step(stack, phi, ids_row, row_iota, owned):
    both = jnp.dot(stack, phi, preferred_element_type=F32)
    value = both[:owned] + both[owned:]
    return jnp.sum(jnp.where(row_iota == ids_row, value, 0.0), axis=0, keepdims=True)


def store_rows(ref, rows, value):
    for i, r in enumerate(rows):
        ref[pl.ds(r, 1), :] = value[:, i * LANES : (i + 1) * LANES]


def basis_loop(table, ids_ref, time_ref, coef, phi_ref, value_ref):
    owned, terms = coef.shape
    half = terms // 2
    value_ref[...] = jnp.zeros(value_ref.shape, F32)
    width = phi_ref.shape[2]
    stack = stacked(coef)
    row_iota = lax.broadcasted_iota(jnp.int32, (owned, width), 0).astype(F32)
    fine = (lax.broadcasted_iota(jnp.int32, (8, width), 0) + 1).astype(F32)
    coarse = (lax.broadcasted_iota(jnp.int32, (half // 8, width), 0) * 8).astype(F32)

    def step(n):
        rows = step_rows(table, n)
        times = rows_pair(time_ref, rows)
        cos_fine, sin_fine = cos_sin_pi(fine * times)
        cos_coarse, sin_coarse = cos_sin_pi(coarse * times)
        cos_parts, sin_parts = [], []
        for j in range(half // 8):
            cj = cos_coarse[j : j + 1]
            sj = sin_coarse[j : j + 1]
            cos_parts.append(cj * cos_fine - sj * sin_fine)
            sin_parts.append(sj * cos_fine + cj * sin_fine)
        high, low = split(jnp.concatenate(cos_parts + sin_parts, axis=0))
        phi = jnp.concatenate([high, low], axis=0)
        phi_ref[n] = phi
        value = forward_step(stack, phi, rows_pair(ids_ref, rows), row_iota, owned)
        store_rows(value_ref, rows, value)

    def block(i, carry):
        for u in range(SETUP_UNROLL):
            step(i * SETUP_UNROLL + u)
        return carry

    blocks = table[table.shape[0] - 1] * (UNROLL // SETUP_UNROLL)
    lax.fori_loop(0, blocks, block, 0)


class Role:
    def __init__(self, sign, table, meta, phi, z_ref, value_ref):
        self.sign = sign
        self.table = table
        self.ids = meta.at[0]
        self.meta = meta
        self.phi = phi
        self.z_ref = z_ref
        self.value_ref = value_ref
        self.count = meta.shape[1] - DUMMY_ROWS

    def cross(self, mine, other):
        return mine - other if self.sign > 0 else other - mine

    def backward(self, z, owned):
        high = z.astype(BF16).astype(F32)
        self.z_ref[0, : self.count] = high
        self.z_ref[1, : self.count] = z - high
        self.z_ref[:, self.count :] = jnp.zeros((2, DUMMY_ROWS, LANES), F32)
        steps, double, width = self.phi.shape
        terms = double // 2
        row_iota = lax.broadcasted_iota(jnp.int32, (owned, width), 0).astype(F32)

        def gather(n):
            rows = step_rows(self.table, n)
            hit = row_iota == rows_pair(self.ids, rows)
            parts = [
                jnp.where(hit, rows_pair(self.z_ref.at[k], rows), 0.0).astype(BF16)
                for k in range(2)
            ]
            return lax.dot_general(
                jnp.concatenate(parts, axis=0),
                self.phi[n],
                (((1,), (1,)), ((), ())),
                preferred_element_type=F32,
            )

        def block(i, carry):
            parts = [gather(i * UNROLL + u) for u in range(UNROLL)]
            while len(parts) > 1:
                parts = [sum(parts[k : k + 2]) for k in range(0, len(parts), 2)]
            return carry + parts[0]

        blocks = self.table[self.table.shape[0] - 1]
        g = lax.fori_loop(0, blocks, block, jnp.zeros((2 * owned, double), F32))
        return self.sign * (g[:owned, :terms] + (g[:owned, terms:] + g[owned:, :terms]))

    def forward(self, field):
        owned = field.shape[0]
        stack = stacked(field)
        width = self.phi.shape[2]
        row_iota = lax.broadcasted_iota(jnp.int32, (owned, width), 0).astype(F32)
        self.value_ref[...] = jnp.zeros(self.value_ref.shape, F32)

        def block(i, carry):
            for u in range(UNROLL):
                n = i * UNROLL + u
                rows = step_rows(self.table, n)
                value = forward_step(
                    stack, self.phi[n], rows_pair(self.ids, rows), row_iota, owned
                )
                store_rows(self.value_ref, rows, value)
            return carry

        lax.fori_loop(0, self.table[self.table.shape[0] - 1], block, 0)
        return self.value_ref[: self.count]

    def weigh(self, model):
        live = self.meta[0, : self.count] >= 0.0
        misfit = jnp.where(live, self.meta[1, : self.count] - model, 0.0)
        weight = jnp.where(live, 1.0 / (1.0 + misfit * misfit / cauchy_square), 0.0)
        return weight, weight * misfit

    def gradient(self, z, state):
        return self.backward(z, state.shape[0]) - damping * state

    def image(self, z, before):
        return SCALE * (self.backward(z, before.shape[0]) + damping * before)


def write_chunks(send, first, values):
    chunks, rows = send.shape[0], send.shape[2]
    for j in range(chunks):
        send[j, first] = values[j * rows : (j + 1) * rows, :]


def fill_padded(ref, values):
    count = values.shape[0]
    ref[:count] = values
    ref[count:] = jnp.zeros((ref.shape[0] - count,) + values.shape[1:], F32)


def setup_asc_kernel(
    chunks, packed, coef, role_desc, meta, phi, table, value, onward, times, value_ref
):
    rows = packed.shape[2]
    count = chunks * rows
    meta[0, :count] = flat(packed, 0, chunks)
    meta[0, count:] = jnp.full((DUMMY_ROWS, LANES), -1.0, F32)
    fill_padded(meta.at[1], flat(packed, 4, chunks))
    fill_padded(times, flat(packed, 1, chunks))
    used_rows(meta.at[0], chunks, rows, table)
    basis_loop(table, meta.at[0], times, coef[...], phi, value_ref)
    value[...] = value_ref[:count]
    for j in range(chunks):
        onward[j, 0] = packed[j, 2]
        onward[j, 1] = packed[j, 3]
        onward[j, 2] = packed[j, 4]
    write_chunks(onward, 3, value_ref[:count])


def setup_desc_kernel(
    chunks, packed, state, meta, phi, table, model, weights, basis_0, value_0, send,
    times, z_ref, value_ref,
):
    rows = packed.shape[2]
    count = chunks * rows
    meta[0, :count] = flat(packed, 0, chunks)
    meta[0, count:] = jnp.full((DUMMY_ROWS, LANES), -1.0, F32)
    fill_padded(meta.at[1], flat(packed, 2, chunks))
    fill_padded(times, flat(packed, 1, chunks))
    used_rows(meta.at[0], chunks, rows, table)
    basis_loop(table, meta.at[0], times, state[...], phi, value_ref)
    role = Role(-1.0, table, meta, phi, z_ref, value_ref)
    own = value_ref[:count]
    write_chunks(send, 0, own)
    modelled = role.cross(own, flat(packed, 3, chunks))
    model[...] = modelled
    weights[...], z = role.weigh(modelled)
    basis_0[...] = role.gradient(z, state[...])
    own = role.forward(basis_0[...])
    value_0[...] = own
    write_chunks(send, 1, own)


def first_asc_kernel(
    chunks, got, value, meta, phi, table, state,
    model, weights, crossed_0, basis_0, basis_1, value_1, send, z_ref, value_ref,
):
    role = Role(1.0, table, meta, phi, z_ref, value_ref)
    modelled = role.cross(value[...], flat(got, 0, chunks))
    model[...] = modelled
    weights[...], z = role.weigh(modelled)
    basis_0[...] = role.gradient(z, state[...])
    own = role.forward(basis_0[...])
    write_chunks(send, 0, own)
    crossed = role.cross(own, flat(got, 1, chunks))
    crossed_0[...] = crossed
    basis_1[...] = role.image(weights[...] * crossed, basis_0[...])
    own = role.forward(basis_1[...])
    value_1[...] = own
    write_chunks(send, 1, own)


def images_kernel(
    sign, chunks, got, value_0, meta, phi, table, weights, basis_0,
    crossed_0, crossed_1, basis_1, basis_2, value_2, send, z_ref, value_ref,
):
    role = Role(sign, table, meta, phi, z_ref, value_ref)
    crossed = role.cross(value_0[...], flat(got, 0, chunks))
    crossed_0[...] = crossed
    basis_1[...] = role.image(weights[...] * crossed, basis_0[...])
    own = role.forward(basis_1[...])
    write_chunks(send, 0, own)
    crossed = role.cross(own, flat(got, 1, chunks))
    crossed_1[...] = crossed
    basis_2[...] = role.image(weights[...] * crossed, basis_1[...])
    own = role.forward(basis_2[...])
    value_2[...] = own
    write_chunks(send, 1, own)


def total(x):
    return jnp.sum(jnp.sum(x, axis=0, keepdims=True), axis=1, keepdims=True)


PAIRS = [(0, 0), (0, 1), (0, 2), (1, 1), (1, 2), (2, 2)]


def gram_kernel(
    sign, chunks, got, value_1, meta, phi, table, weights, crossed_0, basis_0, basis_1,
    other_0, other_1, other_2,
    crossed_1, crossed_2, basis_2, value_2, scalars, z_ref, value_ref,
):
    role = Role(sign, table, meta, phi, z_ref, value_ref)
    weight = weights[...]
    crossed = role.cross(value_1[...], flat(got, 0, chunks))
    crossed_1[...] = crossed
    basis_2[...] = role.image(weight * crossed, basis_1[...])
    own = role.forward(basis_2[...])
    value_2[...] = own
    last = role.cross(own, flat(got, 1, chunks))
    crossed_2[...] = last
    values = [crossed_0[...], crossed, last]
    mine = [basis_0[...], basis_1[...], basis_2[...]]
    others = [other_0[...], other_1[...], other_2[...]]
    lane = lax.broadcasted_iota(jnp.int32, (1, LANES), 1)
    line = jnp.zeros((1, LANES), F32)
    for place_in_line, (i, j) in enumerate(PAIRS):
        dots = total(mine[i] * mine[j] + others[i] * others[j])
        curve = total(weight * values[i] * values[j]) + damping * dots
        line = jnp.where(lane == place_in_line, curve, line)
        if i == 0:
            line = jnp.where(lane == len(PAIRS) + j, dots, line)
    for d in range(scalars.shape[0]):
        scalars[d] = line


def solve(scalars):
    summed = scalars[0]
    for d in range(1, scalars.shape[0]):
        summed = summed + scalars[d]
    line = summed
    lane = lax.broadcasted_iota(jnp.int32, (1, LANES), 1)

    def pick(place):
        return jnp.sum(jnp.where(lane == place, line, 0.0), axis=1, keepdims=True)

    g = {pair: pick(place) for place, pair in enumerate(PAIRS)}
    right = [pick(len(PAIRS) + i) for i in range(3)]
    s = [
        jnp.where(g[i, i] > 0.0, lax.rsqrt(jnp.maximum(g[i, i], 1e-37)), 0.0) for i in range(3)
    ]
    l10 = g[0, 1] * s[0] * s[1]
    l20 = g[0, 2] * s[0] * s[2]
    g21 = g[1, 2] * s[1] * s[2]
    c = [right[i] * s[i] for i in range(3)]

    def inverse(pivot):
        good = pivot > PIVOT_FLOOR
        return jnp.where(good, 1.0 / jnp.where(good, pivot, 1.0), 0.0)

    inv1 = inverse(1.0 - l10 * l10)
    t21 = g21 - l20 * l10
    l21 = t21 * inv1
    inv2 = inverse(1.0 - l20 * l20 - l21 * t21)
    u1 = c[1] - l10 * c[0]
    u2 = c[2] - l20 * c[0] - l21 * u1
    x2 = u2 * inv2
    x1 = u1 * inv1 - l21 * x2
    x0 = c[0] - l10 * x1 - l20 * x2
    return [x0 * s[0], x1 * s[1], x2 * s[2]]


def combine(y, parts):
    return y[0] * parts[0] + (y[1] * parts[1] + y[2] * parts[2])


def next_asc_kernel(
    chunks, scalars, meta, phi, table, model, crossed_0, crossed_1, crossed_2,
    basis_a0, basis_a1, basis_a2, basis_d0, basis_d1, basis_d2, state_a, state_d, value_2,
    new_a, new_d, shares, weights, basis_0, value_0, send, z_ref, value_ref,
):
    role = Role(1.0, table, meta, phi, z_ref, value_ref)
    write_chunks(send, 0, value_2[...])
    y = solve(scalars)
    for i in range(3):
        shares[i : i + 1] = jnp.broadcast_to(y[i], (1, LANES))
    modelled = model[...] + combine(y, [crossed_0[...], crossed_1[...], crossed_2[...]])
    new_a[...] = state_a[...] + combine(y, [basis_a0[...], basis_a1[...], basis_a2[...]])
    new_d[...] = state_d[...] + combine(y, [basis_d0[...], basis_d1[...], basis_d2[...]])
    weights[...], z = role.weigh(modelled)
    basis_0[...] = role.gradient(z, new_a[...])
    own = role.forward(basis_0[...])
    value_0[...] = own
    write_chunks(send, 1, own)


def next_desc_kernel(
    chunks, got, shares, meta, phi, table, model, crossed_0, crossed_1, value_2, state,
    weights, new_crossed_0, basis_0, basis_1, value_1, send, z_ref, value_ref,
):
    role = Role(-1.0, table, meta, phi, z_ref, value_ref)
    y = [shares[i : i + 1] for i in range(3)]
    crossed_2 = role.cross(value_2[...], flat(got, 0, chunks))
    modelled = model[...] + combine(y, [crossed_0[...], crossed_1[...], crossed_2])
    weights[...], z = role.weigh(modelled)
    basis_0[...] = role.gradient(z, state[...])
    own = role.forward(basis_0[...])
    write_chunks(send, 0, own)
    crossed = role.cross(own, flat(got, 1, chunks))
    new_crossed_0[...] = crossed
    basis_1[...] = role.image(weights[...] * crossed, basis_0[...])
    own = role.forward(basis_1[...])
    value_1[...] = own
    write_chunks(send, 1, own)


def final_kernel(scalars, state_a, basis_0, basis_1, basis_2, desc, out_a, out_d):
    y = solve(scalars)
    out_a[...] = state_a[...] + combine(y, [basis_0[...], basis_1[...], basis_2[...]])
    out_d[...] = desc[0] + combine(y, [desc[1], desc[2], desc[3]])


def body(coef_asc, coef_desc, cross_asc, cross_desc, time_asc, time_desc, height, block_fill):
    owned_asc, terms = coef_asc.shape
    owned_desc = coef_desc.shape[0]
    blocks, width = cross_asc.shape
    na = lax.axis_size("asc")
    nd = lax.axis_size("desc")
    fold = na // nd
    rows = blocks * width // na // LANES
    all_rows = na * rows
    group = STEP_ROWS * UNROLL
    steps = -(-all_rows // group) * UNROLL
    step_width = STEP_ROWS * LANES
    shape = jax.ShapeDtypeStruct

    def call(kernel, outs, scratch, *args, in_specs=None, mebibytes=16):
        return pl.pallas_call(
            kernel,
            out_shape=outs,
            in_specs=[place(x) for x in args] if in_specs is None else in_specs,
            out_specs=jax.tree.map(place, outs),
            scratch_shapes=scratch,
            compiler_params=params(mebibytes),
        )(*args)

    to_role = []
    for p in range(na):
        for q in range(nd):
            to_role.append((p * nd + q, (q * fold + p // nd) * nd + p % nd))
    to_native = [(b, a) for a, b in to_role]
    role_desc = lax.ppermute(coef_desc, ("asc", "desc"), to_role)

    slots = (cross_asc, cross_desc, time_asc, time_desc, height)
    packed = call(
        functools.partial(pack_kernel, na, nd, owned_asc, owned_desc),
        shape((nd, fold, FIELDS, rows, LANES), F32),
        [pltpu.VMEM((blocks, width), x.dtype) for x in slots]
        + [
            pltpu.VMEM((1, blocks), jnp.int32),
            pltpu.VMEM((FIELDS, blocks, width), F32),
            pltpu.SemaphoreType.DMA((len(slots) + 1,)),
        ],
        *slots, block_fill.reshape(1, blocks),
        in_specs=[pl.BlockSpec(memory_space=pltpu.HBM)] * (len(slots) + 1),
        mebibytes=60,
    )
    at_asc = lax.all_to_all(packed, "desc", split_axis=0, concat_axis=0, tiled=True)
    at_asc = at_asc.reshape(na, FIELDS, rows, LANES)

    padded = all_rows + DUMMY_ROWS
    meta_shape = shape((2, padded, LANES), F32)
    phi_shape = shape((steps, 2 * terms, step_width), BF16)
    table_shape = shape((all_rows + rows + group + 1,), jnp.int32)
    role_shapes = [meta_shape, phi_shape, table_shape]
    slot_shape = shape((all_rows, LANES), F32)
    send_shape = shape((na, 2, rows, LANES), F32)
    field_a = shape(coef_asc.shape, F32)
    field_d = shape(coef_desc.shape, F32)
    line_shape = shape((na * nd, 1, LANES), F32)
    times_scratch = pltpu.VMEM((padded, LANES), F32)
    scratch = [pltpu.VMEM((2, padded, LANES), F32), pltpu.VMEM((padded, LANES), F32)]

    def exchange(x):
        return lax.all_to_all(x, "asc", split_axis=0, concat_axis=0, tiled=True)

    def share(x):
        return lax.all_to_all(x, ("asc", "desc"), split_axis=0, concat_axis=0, tiled=True)

    *asc, value, onward = call(
        functools.partial(setup_asc_kernel, na),
        role_shapes + [slot_shape, shape((na, 4, rows, LANES), F32)],
        [times_scratch, scratch[1]],
        at_asc, coef_asc, role_desc,
    )
    *desc, model_d, weights_d, d0, own_d, send = call(
        functools.partial(setup_desc_kernel, na),
        role_shapes + [slot_shape, slot_shape, field_d, slot_shape, send_shape],
        [times_scratch] + scratch,
        exchange(onward), role_desc,
    )
    model_a, weights_a, crossed_a0, a0, a1, own_a, send = call(
        functools.partial(first_asc_kernel, na),
        [slot_shape, slot_shape, slot_shape, field_a, field_a, slot_shape, send_shape],
        scratch,
        exchange(send), value, *asc, coef_asc,
    )
    crossed_d0, crossed_d1, d1, d2, own_d, send = call(
        functools.partial(images_kernel, -1.0, na),
        [slot_shape, slot_shape, field_d, field_d, slot_shape, send_shape],
        scratch,
        exchange(send), own_d, *desc, weights_d, d0,
    )
    crossed_a1, crossed_a2, a2, own_a, scalars = call(
        functools.partial(gram_kernel, 1.0, na),
        [slot_shape, slot_shape, field_a, slot_shape, line_shape],
        scratch,
        exchange(send), own_a, *asc, weights_a, crossed_a0, a0, a1, d0, d1, d2,
    )
    state_a, state_d, shares, weights_a, a0, own_a, send = call(
        functools.partial(next_asc_kernel, na),
        [
            field_a, field_d, shape((8, LANES), F32),
            slot_shape, field_a, slot_shape, send_shape,
        ],
        scratch,
        share(scalars), *asc, model_a, crossed_a0, crossed_a1, crossed_a2,
        a0, a1, a2, d0, d1, d2, coef_asc, role_desc, own_a,
    )
    weights_d, crossed_d0, d0, d1, own_d, send = call(
        functools.partial(next_desc_kernel, na),
        [slot_shape, slot_shape, field_d, field_d, slot_shape, send_shape],
        scratch,
        exchange(send), shares, *desc, model_d, crossed_d0, crossed_d1, own_d, state_d,
    )
    _, _, a1, a2, _, send = call(
        functools.partial(images_kernel, 1.0, na),
        [slot_shape, slot_shape, field_a, field_a, slot_shape, send_shape],
        scratch,
        exchange(send), own_a, *asc, weights_a, a0,
    )
    _, _, d2, _, scalars = call(
        functools.partial(gram_kernel, -1.0, na),
        [slot_shape, slot_shape, field_d, slot_shape, line_shape],
        scratch,
        exchange(send), own_d, *desc, weights_d, crossed_d0, d0, d1, a0, a1, a2,
    )
    leaving = jnp.stack([state_d, d0, d1, d2])
    native = lax.ppermute(leaving, ("asc", "desc"), to_native)
    return tuple(
        call(
            final_kernel,
            [field_a, field_d],
            [],
            share(scalars), state_a, a0, a1, a2, native,
        )
    )


def solution(mesh):
    split_rows = P(("asc", "desc"), None)
    return jax.shard_map(
        body,
        mesh=mesh,
        in_specs=(split_rows,) * 7 + (P(("asc", "desc")),),
        out_specs=(split_rows, split_rows),
        check_vma=False,
    )
```

time: 145 us -> 135 us (0.931)
  the two profiles are of different devices: /device:TPU:25 before, /device:TPU:0 now
where the time goes in v4:
time: 135 us; the launch traced here: 133 us
  blocking collectives  78.5 us (58%)
  Pallas kernels  38.7 us (29%)
  starting transfers between devices  8.35 us (6%)
  waiting for transfers between devices  5.06 us (4%)
  local copies, waits for them, and re-layouts  1.43 us (1%)
    all_to_all x7, blocking collectives, exchange(): return lax.all_to_all(x, 'asc', split_axis=0, concat_axis=0, tiled=True)  57.7 us
    pallas_call x11, Pallas kernels, call(): pl.pallas_call(kernel, out_shape=outs, in_specs=[place(x) for x in args]...  38.7 us
    all_to_all x2, blocking collectives, share(): lax.all_to_all(x, ('asc', 'desc'), split_axis=0, concat_axis=0, tiled=True)  20.8 us
    all_to_all x1, starting transfers between devices, body(): lax.all_to_all(packed, 'desc', split_axis=0, concat_axis=0, tiled=True)  6.33 us
    all_to_all x1, waiting for transfers between devices, body(): lax.all_to_all(packed, 'desc', split_axis=0, concat_axis=0, tiled=True)  5.06 us
  transfers between devices with their start and end apart: 3, of which 1 were waited for; matrix products, arithmetic and copies ran while one was open for 0% of the time, Pallas kernels for 0%

profile of v4, /device:TPU:0, one launch (start us, length us, event | category | flops | bytes accessed | tf_op | source)
XLA Modules:
  0.0 132.7 jit_solution(8615096968703236144)
XLA Ops:
  0.6 2.2 %shard_map.95 = f32[4,2,5,8,128]{4,3,2,1,0:T(8,128)} custom-call(s32[64,128]{1,0:T(8,128)} %ca_in.1, s32[64,128]{1,0:T(8,128)} %cd_in.1, f32[64,128]{1,0:T(8,128)} %ta_in.1, f32[64,128]{1,0:T(8,128)} %td_in.1, f32[64,128]{1,0:T(8,128)} %height_in.1, s32[1,64]{1,0:T(1,128)} %bitcast.11), custom_call_target="tpu_custom_call" | custom-call | tf_op jit(solution)/shard_map/pallas_call | solution.py:520
  2.8 6.3 %all-to-all-start = ((f32[4,2,5,8,128]{4,3,2,1,0:T(8,128)}), f32[4,2,5,8,128]{4,3,2,1,0:T(8,128)S(1)}, u32[]{:S(2)}, u32[]{:S(2)}) async-start(f32[4,2,5,8,128]{4,3,2,1,0:T(8,128)} %shard_map.95), calls=%async_computation | async-start | bytes 327680 | tf_op jit(solution)/shard_map/all_to_all | solution.py:550
  9.1 1.4 %collective-permute-start = (f32[32,128]{1,0:T(8,128)}, f32[32,128]{1,0:T(8,128)S(1)}, u32[]{:S(2)}, u32[]{:S(2)}) collective-permute-start(f32[32,128]{1,0:T(8,128)} %param.9), channel_id=1, source_target_pairs={{0,0},{1,8},{2,16},{3,24},{4,1},{5,9},{6,17},{7,25},{8,2},{9,10},{... | collective-permute-start | bytes 49160 | tf_op jit(solution)/shard_map/ppermute | solution.py:534
  10.5 0.0 collective-permute-done.role_desc.state.state_d
  10.5 5.1 %all-to-all-done = f32[4,2,5,8,128]{4,3,2,1,0:T(8,128)S(1)} async-done(((f32[4,2,5,8,128]{4,3,2,1,0:T(8,128)}), f32[4,2,5,8,128]{4,3,2,1,0:T(8,128)S(1)}, u32[]{:S(2)}, u32[]{:S(2)}) %all-to-all-start) | async-done | bytes 163872 | tf_op jit(solution)/shard_map/all_to_all | solution.py:550
  15.6 0.0 copy-start
  15.6 0.7 copy-done
  16.3 2.9 %shard_map.96 = (f32[2,72,128]{2,1,0:T(8,128)S(1)}, bf16[32,256,256]{2,1,0:T(8,128)(2,1)S(1)}, s32[81]{0:T(128)S(1)}, f32[64,128]{1,0:T(8,128)S(1)}, f32[8,4,8,128]{3,2,1,0:T(8,128)S(1)}) custom-call(f32[8,5,8,128]{3,2,1,0:T(8,128)S(1)} %bitcast.6, f32[32,128]{1,0:T(8,128)S(1)} %copy-done, f32[32,128]{1,0:T(8,128)S(1)} %collective-permute-done.role_desc.state.state_d), custom_call_target="tpu_custom_call" | custom-call | tf_op jit(solution)/shard_map/pallas_call | solution.py:520
  19.2 12.8 %all_to_all.50.packed = f32[8,4,8,128]{3,2,1,0:T(8,128)S(1)} all-to-all(f32[8,4,8,128]{3,2,1,0:T(8,128)S(1)} %get-tuple-element.51), channel_id=1, replica_groups=mesh['asc'=8,'desc'=4] {'asc'}, dimensions={0} | all-to-all | bytes 262144 | tf_op jit(solution)/shard_map/all_to_all | solution.py:567
  31.9 5.0 %shard_map.97 = (f32[2,72,128]{2,1,0:T(8,128)S(1)}, bf16[32,256,256]{2,1,0:T(8,128)(2,1)S(1)}, s32[81]{0:T(128)S(1)}, f32[64,128]{1,0:T(8,128)S(1)}, f32[64,128]...) custom-call(f32[8,4,8,128]{3,2,1,0:T(8,128)S(1)} %all_to_all.50.packed, ...), custom_call_target="tpu_custom_call" | custom-call | tf_op jit(solution)/shard_map/pallas_call | solution.py:520
  36.9 7.4 %all_to_all.51.got = f32[8,2,8,128]{3,2,1,0:T(8,128)S(1)} all-to-all(f32[8,2,8,128]{3,2,1,0:T(8,128)S(1)} %get-tuple-element.52), channel_id=1, replica_groups=mesh['asc'=8,'desc'=4] {'asc'}, dimensions={0} | all-to-all | bytes 131072 | tf_op jit(solution)/shard_map/all_to_all | solution.py:567
  44.3 0.0 copy-start.1
  44.3 0.7 copy-done.1
  45.0 4.6 %shard_map.98 = (f32[64,128]{1,0:T(8,128)S(1)}, f32[64,128]{1,0:T(8,128)S(1)}, f32[64,128]{1,0:T(8,128)S(1)}, f32[32,128]{1,0:T(8,128)S(1)}, f32[32,128]{1,0:T(8...) custom-call(f32[8,2,8,128]{3,2,1,0:T(8,128)S(1)} %all_to_all.51.got, ...), custom_call_target="tpu_custom_call" | custom-call | tf_op jit(solution)/shard_map/pallas_call | solution.py:520
  49.7 7.7 %all_to_all.52.got = f32[8,2,8,128]{3,2,1,0:T(8,128)S(1)} all-to-all(f32[8,2,8,128]{3,2,1,0:T(8,128)S(1)} %get-tuple-element.57), channel_id=1, replica_groups=mesh['asc'=8,'desc'=4] {'asc'}, dimensions={0} | all-to-all | bytes 131072 | tf_op jit(solution)/shard_map/all_to_all | solution.py:567
  57.3 4.6 %shard_map.99 = (f32[64,128]{1,0:T(8,128)S(1)}, f32[64,128]{1,0:T(8,128)S(1)}, f32[32,128]{1,0:T(8,128)S(1)}, f32[32,128]{1,0:T(8,128)S(1)}, f32[64,128]{1,0:T(8,128)S(1)}, /*index=5*/f32[8,2,8,128]{3,2,1,0:T(8,128)S(1)}) custom-call(f32[8,2,8,128]{3,2,1,0:T(8,128)S(1)} %all_to_all.52.got, f32[64,128]{1,0:T(8,128)S(1)} %get-tuple-element.58.value_0, ...), custom_call_target="tpu_custom_call" | custom-call | tf_op jit(solution)/shard_map/pallas_call | solution.py:520
  62.0 7.4 %all_to_all.53.got = f32[8,2,8,128]{3,2,1,0:T(8,128)S(1)} all-to-all(f32[8,2,8,128]{3,2,1,0:T(8,128)S(1)} %get-tuple-element.64), channel_id=1, replica_groups=mesh['asc'=8,'desc'=4] {'asc'}, dimensions={0} | all-to-all | bytes 131072 | tf_op jit(solution)/shard_map/all_to_all | solution.py:567
  69.4 2.7 %shard_map.100 = (f32[64,128]{1,0:T(8,128)S(1)}, f32[64,128]{1,0:T(8,128)S(1)}, f32[32,128]{1,0:T(8,128)S(1)}, f32[64,128]{1,0:T(8,128)S(1)}, f32[32,1,128]{2,1,0:T(1,128)S(1)}) custom-call(f32[8,2,8,128]{3,2,1,0:T(8,128)S(1)} %all_to_all.53.got, f32[64,128]{1,0:T(8,128)S(1)} %get-tuple-element.65.value_1, f32[2,72,128]{2,1,0:T(8,128)S(1)} %get-tuple-element.54.meta, ...), custom_call_target="tpu_custom_call" | custom-call | tf_op jit(solution)/shard_map/pallas_call | solution.py:520
  72.1 8.9 %all_to_all.54.scalars = f32[32,1,128]{2,1,0:T(1,128)S(1)} all-to-all(f32[32,1,128]{2,1,0:T(1,128)S(1)} %get-tuple-element.72), channel_id=1, replica_groups=mesh['asc'=8,'desc'=4] {'asc','desc'}, dimensions={0} | all-to-all | bytes 32768 | tf_op jit(solution)/shard_map/all_to_all | solution.py:570
  81.0 2.8 %shard_map.101 = (f32[32,128]{1,0:T(8,128)S(1)}, f32[32,128]{1,0:T(8,128)S(1)}, f32[8,128]{1,0:T(8,128)S(1)}, f32[64,128]{1,0:T(8,128)S(1)}, f32[32,128]{1,0:T(8...) custom-call(f32[32,1,128]{2,1,0:T(1,128)S(1)} %all_to_all.54.scalars, ...), custom_call_target="tpu_custom_call" | custom-call | tf_op jit(solution)/shard_map/pallas_call | solution.py:520
  83.7 7.4 %all_to_all.55.got = f32[8,2,8,128]{3,2,1,0:T(8,128)S(1)} all-to-all(f32[8,2,8,128]{3,2,1,0:T(8,128)S(1)} %get-tuple-element.78), channel_id=1, replica_groups=mesh['asc'=8,'desc'=4] {'asc'}, dimensions={0} | all-to-all | bytes 131072 | tf_op jit(solution)/shard_map/all_to_all | solution.py:567
  91.1 4.7 %shard_map.102 = (f32[64,128]{1,0:T(8,128)S(1)}, f32[64,128]{1,0:T(8,128)S(1)}, f32[32,128]{1,0:T(8,128)S(1)}, f32[32,128]{1,0:T(8,128)S(1)}, f32[64,128]{1,0:T(8,128)S(1)}, /*index=5*/f32[8,2,8,128]{3,2,1,0:T(8,128)S(1)}) custom-call(f32[8,2,8,128]{3,2,1,0:T(8,128)S(1)} %all_to_all.55.got, f32[8,128]{1,0:T(8,128)S(1)} %get-tuple-element.79.shares, ...), custom_call_target="tpu_custom_call" | custom-call | tf_op jit(solution)/shard_map/pallas_call | solution.py:520
  95.8 7.4 %all_to_all.56.got = f32[8,2,8,128]{3,2,1,0:T(8,128)S(1)} all-to-all(f32[8,2,8,128]{3,2,1,0:T(8,128)S(1)} %get-tuple-element.85), channel_id=1, replica_groups=mesh['asc'=8,'desc'=4] {'asc'}, dimensions={0} | all-to-all | bytes 131072 | tf_op jit(solution)/shard_map/all_to_all | solution.py:567
  103.2 5.3 %shard_map.103 = (f32[64,128]{1,0:T(8,128)}, f32[64,128]{1,0:T(8,128)}, f32[32,128]{1,0:T(8,128)S(1)}, f32[32,128]{1,0:T(8,128)S(1)}, f32[64,128]{1,0:T(8,128)}, /*index=5*/f32[8,2,8,128]{3,2,1,0:T(8,128)S(1)}) custom-call(f32[8,2,8,128]{3,2,1,0:T(8,128)S(1)} %all_to_all.56.got, f32[64,128]{1,0:T(8,128)S(1)} %get-tuple-element.86.value_0, ...), custom_call_target="tpu_custom_call" | custom-call | tf_op jit(solution)/shard_map/pallas_call | solution.py:520
  108.5 7.6 %all_to_all.57.got = f32[8,2,8,128]{3,2,1,0:T(8,128)S(1)} all-to-all(f32[8,2,8,128]{3,2,1,0:T(8,128)S(1)} %get-tuple-element.89), channel_id=1, replica_groups=mesh['asc'=8,'desc'=4] {'asc'}, dimensions={0} | all-to-all | bytes 131072 | tf_op jit(solution)/shard_map/all_to_all | solution.py:567
  116.1 3.2 %shard_map.104 = (f32[64,128]{1,0:T(8,128)}, f32[64,128]{1,0:T(8,128)}, f32[32,128]{1,0:T(8,128)S(1)}, f32[64,128]{1,0:T(8,128)}, f32[32,1,128]{2,1,0:T(1,128)S(1)}) custom-call(f32[8,2,8,128]{3,2,1,0:T(8,128)S(1)} %all_to_all.57.got, f32[64,128]{1,0:T(8,128)S(1)} %get-tuple-element.90.value_1, f32[2,72,128]{2,1,0:T(8,128)S(1)} %get-tuple-element.59.meta, ...), custom_call_target="tpu_custom_call" | custom-call | tf_op jit(solution)/shard_map/pallas_call | solution.py:520
  119.4 0.7 collective-permute-start.1
  120.0 12.0 %all_to_all.58.scalars = f32[32,1,128]{2,1,0:T(1,128)S(1)} all-to-all(f32[32,1,128]{2,1,0:T(1,128)S(1)} %get-tuple-element.97), channel_id=1, replica_groups=mesh['asc'=8,'desc'=4] {'asc','desc'}, dimensions={0} | all-to-all | bytes 32768 | tf_op jit(solution)/shard_map/all_to_all | solution.py:570
  132.0 0.0 collective-permute-done.1.desc
  132.0 0.8 shard_map.105
  (1 shorter events, 0.0 us)
Async XLA Ops:
  2.8 12.8 %all-to-all-start = ((f32[4,2,5,8,128]{4,3,2,1,0:T(8,128)}), f32[4,2,5,8,128]{4,3,2,1,0:T(8,128)S(1)}, u32[]{:S(2)}, u32[]{:S(2)}) async-start(f32[4,2,5,8,128]{4,3,2,1,0:T(8,128)} %shard_map.95), calls=%async_computation | async-start | bytes 327680 | tf_op jit(solution)/shard_map/all_to_all | solution.py:550
  9.1 1.4 %collective-permute-start = (f32[32,128]{1,0:T(8,128)}, f32[32,128]{1,0:T(8,128)S(1)}, u32[]{:S(2)}, u32[]{:S(2)}) collective-permute-start(f32[32,128]{1,0:T(8,128)} %param.9), channel_id=1, source_target_pairs={{0,0},{1,8},{2,16},{3,24},{4,1},{5,9},{6,17},{7,25},{8,2},{9,10},{... | collective-permute-start | bytes 49160 | tf_op jit(solution)/shard_map/ppermute | solution.py:534
  15.6 0.7 copy-start
  44.3 0.7 copy-start.1
  119.4 12.6 %collective-permute-start.1 = (f32[4,32,128]{2,1,0:T(8,128)S(1)}, f32[4,32,128]{2,1,0:T(8,128)S(1)}, u32[]{:S(2)}, u32[]{:S(2)}) collective-permute-start(f32[4,32,128]{2,1,0:T(8,128)S(1)} %pad_maximum_fusion), channel_id=1, source_target_pairs={{0,0},{8,1},{16,2},{24,3},{1,4},{9,5},{17,6},{25,7},{2,8},{10,9},{... | collective-permute-start | bytes 196616 | tf_op jit(solution)/shard_map/ppermute | solution.py:631

commit v5 on v4

--- a/solution.py
+++ b/solution.py
@@ -15,8 +15,10 @@
 LANES = 128
 STEP_ROWS = 2
 UNROLL = 4
-SETUP_UNROLL = 2
+BLOCK_ROWS = STEP_ROWS * UNROLL
+STEP_LANES = STEP_ROWS * LANES
 DUMMY_ROWS = 8
+TURN = 2
 SCALE = 1.0 / 128.0
 FIELDS = 5
 PIVOT_FLOOR = 1e-6
@@ -144,14 +146,26 @@
         for i in range(rows):
             table[count + i] = j * rows + i
         count = count + used
-    group = STEP_ROWS * UNROLL
-    for i in range(group):
+    for i in range(BLOCK_ROWS):
         table[count + i] = chunks * rows
-    table[table.shape[0] - 1] = lax.div(count + (group - 1), group)
-
-
-def step_rows(table, n):
-    return [table[n * STEP_ROWS + i] for i in range(STEP_ROWS)]
+    table[table.shape[0] - 1] = lax.div(count + (BLOCK_ROWS - 1), BLOCK_ROWS)
+
+
+def listed_rows(table, first, count):
+    return [table[first + i] for i in range(count)]
+
+
+def over_blocks(table, step, carry):
+    blocks = table[table.shape[0] - 1]
+    turns = lax.div(blocks, TURN)
+
+    def turn(i, carry):
+        for u in range(TURN):
+            carry = step(i * TURN + u, carry)
+        return carry
+
+    carry = lax.fori_loop(0, turns, turn, carry)
+    return lax.fori_loop(turns * TURN, blocks, step, carry)
 
 
 def stacked(field):
@@ -176,14 +190,14 @@
     owned, terms = coef.shape
     half = terms // 2
     value_ref[...] = jnp.zeros(value_ref.shape, F32)
-    width = phi_ref.shape[2]
+    width = STEP_LANES
     stack = stacked(coef)
     row_iota = lax.broadcasted_iota(jnp.int32, (owned, width), 0).astype(F32)
     fine = (lax.broadcasted_iota(jnp.int32, (8, width), 0) + 1).astype(F32)
     coarse = (lax.broadcasted_iota(jnp.int32, (half // 8, width), 0) * 8).astype(F32)
 
-    def step(n):
-        rows = step_rows(table, n)
+    def step(block, u):
+        rows = listed_rows(table, block * BLOCK_ROWS + u * STEP_ROWS, STEP_ROWS)
         times = rows_pair(time_ref, rows)
         cos_fine, sin_fine = cos_sin_pi(fine * times)
         cos_coarse, sin_coarse = cos_sin_pi(coarse * times)
@@ -195,17 +209,16 @@
             sin_parts.append(sj * cos_fine + cj * sin_fine)
         high, low = split(jnp.concatenate(cos_parts + sin_parts, axis=0))
         phi = jnp.concatenate([high, low], axis=0)
-        phi_ref[n] = phi
+        phi_ref[block, :, u * width : (u + 1) * width] = phi
         value = forward_step(stack, phi, rows_pair(ids_ref, rows), row_iota, owned)
         store_rows(value_ref, rows, value)
 
-    def block(i, carry):
-        for u in range(SETUP_UNROLL):
-            step(i * SETUP_UNROLL + u)
+    def whole_block(block, carry):
+        for u in range(UNROLL):
+            step(block, u)
         return carry
 
-    blocks = table[table.shape[0] - 1] * (UNROLL // SETUP_UNROLL)
-    lax.fori_loop(0, blocks, block, 0)
+    lax.fori_loop(0, table[table.shape[0] - 1], whole_block, 0)
 
 
 class Role:
@@ -227,52 +240,42 @@
         self.z_ref[0, : self.count] = high
         self.z_ref[1, : self.count] = z - high
         self.z_ref[:, self.count :] = jnp.zeros((2, DUMMY_ROWS, LANES), F32)
-        steps, double, width = self.phi.shape
+        blocks, double, width = self.phi.shape
         terms = double // 2
         row_iota = lax.broadcasted_iota(jnp.int32, (owned, width), 0).astype(F32)
 
-        def gather(n):
-            rows = step_rows(self.table, n)
+        def gather(block, carry):
+            rows = listed_rows(self.table, block * BLOCK_ROWS, BLOCK_ROWS)
             hit = row_iota == rows_pair(self.ids, rows)
             parts = [
                 jnp.where(hit, rows_pair(self.z_ref.at[k], rows), 0.0).astype(BF16)
                 for k in range(2)
             ]
-            return lax.dot_general(
+            return carry + lax.dot_general(
                 jnp.concatenate(parts, axis=0),
-                self.phi[n],
+                self.phi[block],
                 (((1,), (1,)), ((), ())),
                 preferred_element_type=F32,
             )
 
-        def block(i, carry):
-            parts = [gather(i * UNROLL + u) for u in range(UNROLL)]
-            while len(parts) > 1:
-                parts = [sum(parts[k : k + 2]) for k in range(0, len(parts), 2)]
-            return carry + parts[0]
-
-        blocks = self.table[self.table.shape[0] - 1]
-        g = lax.fori_loop(0, blocks, block, jnp.zeros((2 * owned, double), F32))
+        g = over_blocks(self.table, gather, jnp.zeros((2 * owned, double), F32))
         return self.sign * (g[:owned, :terms] + (g[:owned, terms:] + g[owned:, :terms]))
 
     def forward(self, field):
         owned = field.shape[0]
         stack = stacked(field)
-        width = self.phi.shape[2]
-        row_iota = lax.broadcasted_iota(jnp.int32, (owned, width), 0).astype(F32)
+        row_iota = lax.broadcasted_iota(jnp.int32, (owned, STEP_LANES), 0).astype(F32)
         self.value_ref[...] = jnp.zeros(self.value_ref.shape, F32)
 
-        def block(i, carry):
+        def ahead(block, carry):
             for u in range(UNROLL):
-                n = i * UNROLL + u
-                rows = step_rows(self.table, n)
-                value = forward_step(
-                    stack, self.phi[n], rows_pair(self.ids, rows), row_iota, owned
-                )
+                rows = listed_rows(self.table, block * BLOCK_ROWS + u * STEP_ROWS, STEP_ROWS)
+                phi = self.phi[block, :, u * STEP_LANES : (u + 1) * STEP_LANES]
+                value = forward_step(stack, phi, rows_pair(self.ids, rows), row_iota, owned)
                 store_rows(self.value_ref, rows, value)
             return carry
 
-        lax.fori_loop(0, self.table[self.table.shape[0] - 1], block, 0)
+        over_blocks(self.table, ahead, 0)
         return self.value_ref[: self.count]
 
     def weigh(self, model):
@@ -301,8 +304,9 @@
 
 
 def setup_asc_kernel(
-    chunks, packed, coef, role_desc, meta, phi, table, value, onward, times, value_ref
-):
+    chunks, packed, coef, role_desc, meta, phi, table, state, value, onward, times, value_ref
+):
+    state[...] = coef[...]
     rows = packed.shape[2]
     count = chunks * rows
     meta[0, :count] = flat(packed, 0, chunks)
@@ -511,9 +515,7 @@
     fold = na // nd
     rows = blocks * width // na // LANES
     all_rows = na * rows
-    group = STEP_ROWS * UNROLL
-    steps = -(-all_rows // group) * UNROLL
-    step_width = STEP_ROWS * LANES
+    all_blocks = -(-all_rows // BLOCK_ROWS)
     shape = jax.ShapeDtypeStruct
 
     def call(kernel, outs, scratch, *args, in_specs=None, mebibytes=16):
@@ -552,8 +554,8 @@
 
     padded = all_rows + DUMMY_ROWS
     meta_shape = shape((2, padded, LANES), F32)
-    phi_shape = shape((steps, 2 * terms, step_width), BF16)
-    table_shape = shape((all_rows + rows + group + 1,), jnp.int32)
+    phi_shape = shape((all_blocks, 2 * terms, BLOCK_ROWS * LANES), BF16)
+    table_shape = shape((all_rows + rows + BLOCK_ROWS + 1,), jnp.int32)
     role_shapes = [meta_shape, phi_shape, table_shape]
     slot_shape = shape((all_rows, LANES), F32)
     send_shape = shape((na, 2, rows, LANES), F32)
@@ -569,9 +571,9 @@
     def share(x):
         return lax.all_to_all(x, ("asc", "desc"), split_axis=0, concat_axis=0, tiled=True)
 
-    *asc, value, onward = call(
+    *asc, state_a, value, onward = call(
         functools.partial(setup_asc_kernel, na),
-        role_shapes + [slot_shape, shape((na, 4, rows, LANES), F32)],
+        role_shapes + [field_a, slot_shape, shape((na, 4, rows, LANES), F32)],
         [times_scratch, scratch[1]],
         at_asc, coef_asc, role_desc,
     )
@@ -585,7 +587,7 @@
         functools.partial(first_asc_kernel, na),
         [slot_shape, slot_shape, slot_shape, field_a, field_a, slot_shape, send_shape],
         scratch,
-        exchange(send), value, *asc, coef_asc,
+        exchange(send), value, *asc, state_a,
     )
     crossed_d0, crossed_d1, d1, d2, own_d, send = call(
         functools.partial(images_kernel, -1.0, na),
@@ -607,7 +609,7 @@
         ],
         scratch,
         share(scalars), *asc, model_a, crossed_a0, crossed_a1, crossed_a2,
-        a0, a1, a2, d0, d1, d2, coef_asc, role_desc, own_a,
+        a0, a1, a2, d0, d1, d2, state_a, role_desc, own_a,
     )
     weights_d, crossed_d0, d0, d1, own_d, send = call(
         functools.partial(next_desc_kernel, na),

time: 135 us -> 127 us (0.941); the launches traced: 133 us -> 127 us
  Pallas kernels: 38.7 us -> 35.2 us
  blocking collectives: 78.5 us -> 77 us
    pallas_call x11, Pallas kernels: 38.7 us -> 35.2 us  [call(): pl.pallas_call(kernel, out_shape=outs, in_specs=[place(x) for x in args]...]
    all_to_all x7, blocking collectives: 57.7 us -> 56.2 us  [exchange(): return lax.all_to_all(x, 'asc', split_axis=0, concat_axis=0, tiled=True)]
where the time goes in v5:
time: 127 us
  blocking collectives  77 us (61%)
  Pallas kernels  35.2 us (28%)
  starting transfers between devices  8.35 us (7%)
  waiting for transfers between devices  5.06 us (4%)
    all_to_all x7, blocking collectives, exchange(): return lax.all_to_all(x, 'asc', split_axis=0, concat_axis=0, tiled=True)  56.2 us
    pallas_call x11, Pallas kernels, call(): pl.pallas_call(kernel, out_shape=outs, in_specs=[place(x) for x in args]...  35.2 us
    all_to_all x2, blocking collectives, share(): lax.all_to_all(x, ('asc', 'desc'), split_axis=0, concat_axis=0, tiled=True)  20.8 us
    all_to_all x1, starting transfers between devices, body(): lax.all_to_all(packed, 'desc', split_axis=0, concat_axis=0, tiled=True)  6.33 us
    all_to_all x1, waiting for transfers between devices, body(): lax.all_to_all(packed, 'desc', split_axis=0, concat_axis=0, tiled=True)  5.06 us
  transfers between devices with their start and end apart: 3, of which 1 were waited for; matrix products, arithmetic and copies ran while one was open for 0% of the time, Pallas kernels for 0%

profile of v5, /device:TPU:0, one launch (start us, length us, event | category | flops | bytes accessed | tf_op | source)
XLA Modules:
  0.0 127.0 jit_solution(3607222203881591994)
XLA Ops:
  0.6 2.2 %shard_map.95 = f32[4,2,5,8,128]{4,3,2,1,0:T(8,128)} custom-call(s32[64,128]{1,0:T(8,128)} %ca_in.1, s32[64,128]{1,0:T(8,128)} %cd_in.1, f32[64,128]{1,0:T(8,128)} %ta_in.1, f32[64,128]{1,0:T(8,128)} %td_in.1, f32[64,128]{1,0:T(8,128)} %height_in.1, s32[1,64]{1,0:T(1,128)} %bitcast.11), custom_call_target="tpu_custom_call" | custom-call | tf_op jit(solution)/shard_map/pallas_call | solution.py:522
  2.8 6.3 %all-to-all-start = ((f32[4,2,5,8,128]{4,3,2,1,0:T(8,128)}), f32[4,2,5,8,128]{4,3,2,1,0:T(8,128)S(1)}, u32[]{:S(2)}, u32[]{:S(2)}) async-start(f32[4,2,5,8,128]{4,3,2,1,0:T(8,128)} %shard_map.95), calls=%async_computation | async-start | bytes 327680 | tf_op jit(solution)/shard_map/all_to_all | solution.py:552
  9.1 1.4 %collective-permute-start = (f32[32,128]{1,0:T(8,128)}, f32[32,128]{1,0:T(8,128)S(1)}, u32[]{:S(2)}, u32[]{:S(2)}) collective-permute-start(f32[32,128]{1,0:T(8,128)} %param.9), channel_id=1, source_target_pairs={{0,0},{1,8},{2,16},{3,24},{4,1},{5,9},{6,17},{7,25},{8,2},{9,10},{... | collective-permute-start | bytes 49160 | tf_op jit(solution)/shard_map/ppermute | solution.py:536
  10.5 0.0 collective-permute-done.role_desc.state.state_d
  10.5 5.1 %all-to-all-done = f32[4,2,5,8,128]{4,3,2,1,0:T(8,128)S(1)} async-done(((f32[4,2,5,8,128]{4,3,2,1,0:T(8,128)}), f32[4,2,5,8,128]{4,3,2,1,0:T(8,128)S(1)}, u32[]{:S(2)}, u32[]{:S(2)}) %all-to-all-start) | async-done | bytes 163872 | tf_op jit(solution)/shard_map/all_to_all | solution.py:552
  15.6 0.0 copy-start
  15.6 0.7 copy-done
  16.3 2.9 %shard_map.96 = (f32[2,72,128]{2,1,0:T(8,128)S(1)}, bf16[8,256,1024]{2,1,0:T(8,128)(2,1)S(1)}, s32[81]{0:T(128)S(1)}, f32[32,128]{1,0:T(8,128)S(1)}, f32[64,128]...) custom-call(f32[8,5,8,128]{3,2,1,0:T(8,128)S(1)} %bitcast.6, f32[32,128]{1,0:T(8,128)S(1)} %copy-done, ...), custom_call_target="tpu_custom_call" | custom-call | tf_op jit(solution)/shard_map/pallas_call | solution.py:522
  19.2 11.8 %all_to_all.50.packed = f32[8,4,8,128]{3,2,1,0:T(8,128)S(1)} all-to-all(f32[8,4,8,128]{3,2,1,0:T(8,128)S(1)} %get-tuple-element.52), channel_id=1, replica_groups=mesh['asc'=8,'desc'=4] {'asc'}, dimensions={0} | all-to-all | bytes 262144 | tf_op jit(solution)/shard_map/all_to_all | solution.py:569
  30.9 4.0 %shard_map.97 = (f32[2,72,128]{2,1,0:T(8,128)S(1)}, bf16[8,256,1024]{2,1,0:T(8,128)(2,1)S(1)}, s32[81]{0:T(128)S(1)}, f32[64,128]{1,0:T(8,128)S(1)}, f32[64,128]...) custom-call(f32[8,4,8,128]{3,2,1,0:T(8,128)S(1)} %all_to_all.50.packed, ...), custom_call_target="tpu_custom_call" | custom-call | tf_op jit(solution)/shard_map/pallas_call | solution.py:522
  35.0 7.4 %all_to_all.51.got = f32[8,2,8,128]{3,2,1,0:T(8,128)S(1)} all-to-all(f32[8,2,8,128]{3,2,1,0:T(8,128)S(1)} %get-tuple-element.53), channel_id=1, replica_groups=mesh['asc'=8,'desc'=4] {'asc'}, dimensions={0} | all-to-all | bytes 131072 | tf_op jit(solution)/shard_map/all_to_all | solution.py:569
  42.4 4.6 %shard_map.98 = (f32[64,128]{1,0:T(8,128)S(1)}, f32[64,128]{1,0:T(8,128)S(1)}, f32[64,128]{1,0:T(8,128)S(1)}, f32[32,128]{1,0:T(8,128)S(1)}, f32[32,128]{1,0:T(8...) custom-call(f32[8,2,8,128]{3,2,1,0:T(8,128)S(1)} %all_to_all.51.got, ...), custom_call_target="tpu_custom_call" | custom-call | tf_op jit(solution)/shard_map/pallas_call | solution.py:522
  47.0 7.4 %all_to_all.52.got = f32[8,2,8,128]{3,2,1,0:T(8,128)S(1)} all-to-all(f32[8,2,8,128]{3,2,1,0:T(8,128)S(1)} %get-tuple-element.59), channel_id=1, replica_groups=mesh['asc'=8,'desc'=4] {'asc'}, dimensions={0} | all-to-all | bytes 131072 | tf_op jit(solution)/shard_map/all_to_all | solution.py:569
  54.4 3.6 %shard_map.99 = (f32[64,128]{1,0:T(8,128)S(1)}, f32[64,128]{1,0:T(8,128)S(1)}, f32[32,128]{1,0:T(8,128)S(1)}, f32[32,128]{1,0:T(8,128)S(1)}, f32[64,128]{1,0:T(8,128)S(1)}, /*index=5*/f32[8,2,8,128]{3,2,1,0:T(8,128)S(1)}) custom-call(f32[8,2,8,128]{3,2,1,0:T(8,128)S(1)} %all_to_all.52.got, f32[64,128]{1,0:T(8,128)S(1)} %get-tuple-element.60.value_0, ...), custom_call_target="tpu_custom_call" | custom-call | tf_op jit(solution)/shard_map/pallas_call | solution.py:522
  58.0 7.4 %all_to_all.53.got = f32[8,2,8,128]{3,2,1,0:T(8,128)S(1)} all-to-all(f32[8,2,8,128]{3,2,1,0:T(8,128)S(1)} %get-tuple-element.66), channel_id=1, replica_groups=mesh['asc'=8,'desc'=4] {'asc'}, dimensions={0} | all-to-all | bytes 131072 | tf_op jit(solution)/shard_map/all_to_all | solution.py:569
  65.4 2.7 %shard_map.100 = (f32[64,128]{1,0:T(8,128)S(1)}, f32[64,128]{1,0:T(8,128)S(1)}, f32[32,128]{1,0:T(8,128)S(1)}, f32[64,128]{1,0:T(8,128)S(1)}, f32[32,1,128]{2,1,0:T(1,128)S(1)}) custom-call(f32[8,2,8,128]{3,2,1,0:T(8,128)S(1)} %all_to_all.53.got, f32[64,128]{1,0:T(8,128)S(1)} %get-tuple-element.67.value_1, f32[2,72,128]{2,1,0:T(8,128)S(1)} %get-tuple-element.55.meta, ...), custom_call_target="tpu_custom_call" | custom-call | tf_op jit(solution)/shard_map/pallas_call | solution.py:522
  68.2 8.9 %all_to_all.54.scalars = f32[32,1,128]{2,1,0:T(1,128)S(1)} all-to-all(f32[32,1,128]{2,1,0:T(1,128)S(1)} %get-tuple-element.74), channel_id=1, replica_groups=mesh['asc'=8,'desc'=4] {'asc','desc'}, dimensions={0} | all-to-all | bytes 32768 | tf_op jit(solution)/shard_map/all_to_all | solution.py:572
  77.0 2.8 %shard_map.101 = (f32[32,128]{1,0:T(8,128)S(1)}, f32[32,128]{1,0:T(8,128)S(1)}, f32[8,128]{1,0:T(8,128)S(1)}, f32[64,128]{1,0:T(8,128)S(1)}, f32[32,128]{1,0:T(8...) custom-call(f32[32,1,128]{2,1,0:T(1,128)S(1)} %all_to_all.54.scalars, ...), custom_call_target="tpu_custom_call" | custom-call | tf_op jit(solution)/shard_map/pallas_call | solution.py:522
  79.8 7.4 %all_to_all.55.got = f32[8,2,8,128]{3,2,1,0:T(8,128)S(1)} all-to-all(f32[8,2,8,128]{3,2,1,0:T(8,128)S(1)} %get-tuple-element.80), channel_id=1, replica_groups=mesh['asc'=8,'desc'=4] {'asc'}, dimensions={0} | all-to-all | bytes 131072 | tf_op jit(solution)/shard_map/all_to_all | solution.py:569
  87.2 3.6 %shard_map.102 = (f32[64,128]{1,0:T(8,128)S(1)}, f32[64,128]{1,0:T(8,128)S(1)}, f32[32,128]{1,0:T(8,128)S(1)}, f32[32,128]{1,0:T(8,128)S(1)}, f32[64,128]{1,0:T(8,128)S(1)}, /*index=5*/f32[8,2,8,128]{3,2,1,0:T(8,128)S(1)}) custom-call(f32[8,2,8,128]{3,2,1,0:T(8,128)S(1)} %all_to_all.55.got, f32[8,128]{1,0:T(8,128)S(1)} %get-tuple-element.81.shares, ...), custom_call_target="tpu_custom_call" | custom-call | tf_op jit(solution)/shard_map/pallas_call | solution.py:522
  90.8 7.4 %all_to_all.56.got = f32[8,2,8,128]{3,2,1,0:T(8,128)S(1)} all-to-all(f32[8,2,8,128]{3,2,1,0:T(8,128)S(1)} %get-tuple-element.87), channel_id=1, replica_groups=mesh['asc'=8,'desc'=4] {'asc'}, dimensions={0} | all-to-all | bytes 131072 | tf_op jit(solution)/shard_map/all_to_all | solution.py:569
  98.2 5.3 %shard_map.103 = (f32[64,128]{1,0:T(8,128)}, f32[64,128]{1,0:T(8,128)}, f32[32,128]{1,0:T(8,128)S(1)}, f32[32,128]{1,0:T(8,128)S(1)}, f32[64,128]{1,0:T(8,128)}, /*index=5*/f32[8,2,8,128]{3,2,1,0:T(8,128)S(1)}) custom-call(f32[8,2,8,128]{3,2,1,0:T(8,128)S(1)} %all_to_all.56.got, f32[64,128]{1,0:T(8,128)S(1)} %get-tuple-element.88.value_0, ...), custom_call_target="tpu_custom_call" | custom-call | tf_op jit(solution)/shard_map/pallas_call | solution.py:522
  103.5 7.4 %all_to_all.57.got = f32[8,2,8,128]{3,2,1,0:T(8,128)S(1)} all-to-all(f32[8,2,8,128]{3,2,1,0:T(8,128)S(1)} %get-tuple-element.91), channel_id=1, replica_groups=mesh['asc'=8,'desc'=4] {'asc'}, dimensions={0} | all-to-all | bytes 131072 | tf_op jit(solution)/shard_map/all_to_all | solution.py:569
  110.9 2.7 %shard_map.104 = (f32[64,128]{1,0:T(8,128)}, f32[64,128]{1,0:T(8,128)}, f32[32,128]{1,0:T(8,128)S(1)}, f32[64,128]{1,0:T(8,128)}, f32[32,1,128]{2,1,0:T(1,128)S(1)}) custom-call(f32[8,2,8,128]{3,2,1,0:T(8,128)S(1)} %all_to_all.57.got, f32[64,128]{1,0:T(8,128)S(1)} %get-tuple-element.92.value_1, f32[2,72,128]{2,1,0:T(8,128)S(1)} %get-tuple-element.61.meta, ...), custom_call_target="tpu_custom_call" | custom-call | tf_op jit(solution)/shard_map/pallas_call | solution.py:522
  113.6 0.7 collective-permute-start.1
  114.3 11.9 %all_to_all.58.scalars = f32[32,1,128]{2,1,0:T(1,128)S(1)} all-to-all(f32[32,1,128]{2,1,0:T(1,128)S(1)} %get-tuple-element.99), channel_id=1, replica_groups=mesh['asc'=8,'desc'=4] {'asc','desc'}, dimensions={0} | all-to-all | bytes 32768 | tf_op jit(solution)/shard_map/all_to_all | solution.py:572
  126.2 0.0 collective-permute-done.1.desc
  126.2 0.8 shard_map.105
  (1 shorter events, 0.0 us)
Async XLA Ops:
  2.8 12.8 %all-to-all-start = ((f32[4,2,5,8,128]{4,3,2,1,0:T(8,128)}), f32[4,2,5,8,128]{4,3,2,1,0:T(8,128)S(1)}, u32[]{:S(2)}, u32[]{:S(2)}) async-start(f32[4,2,5,8,128]{4,3,2,1,0:T(8,128)} %shard_map.95), calls=%async_computation | async-start | bytes 327680 | tf_op jit(solution)/shard_map/all_to_all | solution.py:552
  9.1 1.4 %collective-permute-start = (f32[32,128]{1,0:T(8,128)}, f32[32,128]{1,0:T(8,128)S(1)}, u32[]{:S(2)}, u32[]{:S(2)}) collective-permute-start(f32[32,128]{1,0:T(8,128)} %param.9), channel_id=1, source_target_pairs={{0,0},{1,8},{2,16},{3,24},{4,1},{5,9},{6,17},{7,25},{8,2},{9,10},{... | collective-permute-start | bytes 49160 | tf_op jit(solution)/shard_map/ppermute | solution.py:536
  15.6 0.7 copy-start
  113.6 12.6 %collective-permute-start.1 = (f32[4,32,128]{2,1,0:T(8,128)S(1)}, f32[4,32,128]{2,1,0:T(8,128)S(1)}, u32[]{:S(2)}, u32[]{:S(2)}) collective-permute-start(f32[4,32,128]{2,1,0:T(8,128)S(1)} %pad_maximum_fusion), channel_id=1, source_target_pairs={{0,0},{8,1},{16,2},{24,3},{1,4},{9,5},{17,6},{25,7},{2,8},{10,9},{... | collective-permute-start | bytes 196616 | tf_op jit(solution)/shard_map/ppermute | solution.py:633

commit v6 on v5

--- a/solution.py
+++ b/solution.py
@@ -18,7 +18,7 @@
 BLOCK_ROWS = STEP_ROWS * UNROLL
 STEP_LANES = STEP_ROWS * LANES
 DUMMY_ROWS = 8
-TURN = 2
+TURNS = (4, 2, 1)
 SCALE = 1.0 / 128.0
 FIELDS = 5
 PIVOT_FLOOR = 1e-6
@@ -47,6 +47,19 @@
     return high, low
 
 
+def flat_first(ref, field, fold, rows):
+    parts = []
+    for j in range(ref.shape[0] * fold):
+        start = (j % fold * FIELDS + field) * rows
+        parts.append(ref[j // fold, start : start + rows])
+    return jnp.concatenate(parts, axis=0)
+
+
+def flat_second(ref, field, rows):
+    start = field * rows
+    return jnp.concatenate([ref[j, start : start + rows] for j in range(ref.shape[0])], axis=0)
+
+
 def flat(ref, field, chunks):
     return jnp.concatenate([ref[j, field] for j in range(chunks)], axis=0)
 
@@ -58,15 +71,15 @@
 
 
 def pack_kernel(
-    na, nd, owned_asc, owned_desc, ca_in, cd_in, ta_in, td_in, height_in, fill_in, out,
-    ca, cd, ta, td, height, fill, turned, sems,
+    na, nd, owned_asc, coef_in, ca_in, cd_in, ta_in, td_in, height_in, fill_in, out,
+    coef, ca, cd, ta, td, height, fill, turned, sems,
 ):
     copies = [
         pltpu.make_async_copy(source, target, sems.at[i])
         for i, (source, target) in enumerate(
             [
                 (fill_in, fill), (ca_in, ca), (ta_in, ta),
-                (cd_in, cd), (td_in, td), (height_in, height),
+                (cd_in, cd), (td_in, td), (height_in, height), (coef_in, coef),
             ]
         )
     ]
@@ -74,6 +87,7 @@
         copy.start()
     for copy in copies:
         copy.wait()
+    owned_desc = coef.shape[0]
     blocks, width = ca.shape
     group = width // na
     rows = blocks // na
@@ -116,7 +130,10 @@
                 moved = pltpu.roll(piece, amount, 1) if amount else piece
                 parts[r] = moved if k == 0 else jnp.where(lane_group == k, moved, parts[r])
         for r in range(na):
-            out[r % nd, r // nd, f] = parts[r]
+            start = (r // nd * FIELDS + f) * rows
+            out[r % nd, start : start + rows] = parts[r]
+    for q in range(nd):
+        out[q, out.shape[1] - owned_desc :] = coef[...]
 
 
 def cos_sin_pi(x):
@@ -157,15 +174,18 @@
 
 def over_blocks(table, step, carry):
     blocks = table[table.shape[0] - 1]
-    turns = lax.div(blocks, TURN)
-
-    def turn(i, carry):
-        for u in range(TURN):
-            carry = step(i * TURN + u, carry)
-        return carry
-
-    carry = lax.fori_loop(0, turns, turn, carry)
-    return lax.fori_loop(turns * TURN, blocks, step, carry)
+    done = jnp.int32(0)
+    for size in TURNS:
+        turns = lax.div(blocks - done, size)
+
+        def turn(i, carry, done=done, size=size):
+            for u in range(size):
+                carry = step(done + i * size + u, carry)
+            return carry
+
+        carry = lax.fori_loop(0, turns, turn, carry)
+        done = done + turns * size
+    return carry
 
 
 def stacked(field):
@@ -304,41 +324,45 @@
 
 
 def setup_asc_kernel(
-    chunks, packed, coef, role_desc, meta, phi, table, state, value, onward, times, value_ref
+    fold, rows, packed, coef, meta, phi, table, state, value, onward, times, value_ref
 ):
     state[...] = coef[...]
-    rows = packed.shape[2]
+    chunks = packed.shape[0] * fold
     count = chunks * rows
-    meta[0, :count] = flat(packed, 0, chunks)
+    meta[0, :count] = flat_first(packed, 0, fold, rows)
     meta[0, count:] = jnp.full((DUMMY_ROWS, LANES), -1.0, F32)
-    fill_padded(meta.at[1], flat(packed, 4, chunks))
-    fill_padded(times, flat(packed, 1, chunks))
+    fill_padded(meta.at[1], flat_first(packed, 4, fold, rows))
+    fill_padded(times, flat_first(packed, 1, fold, rows))
     used_rows(meta.at[0], chunks, rows, table)
     basis_loop(table, meta.at[0], times, coef[...], phi, value_ref)
     value[...] = value_ref[:count]
     for j in range(chunks):
-        onward[j, 0] = packed[j, 2]
-        onward[j, 1] = packed[j, 3]
-        onward[j, 2] = packed[j, 4]
-    write_chunks(onward, 3, value_ref[:count])
+        base = j % fold * FIELDS
+        for f in range(3):
+            start = (base + f + 2) * rows
+            onward[j, f * rows : (f + 1) * rows] = packed[j // fold, start : start + rows]
+        onward[j, 3 * rows : 4 * rows] = value_ref[j * rows : (j + 1) * rows]
+        onward[j, 4 * rows :] = packed[j // fold, fold * FIELDS * rows :]
 
 
 def setup_desc_kernel(
-    chunks, packed, state, meta, phi, table, model, weights, basis_0, value_0, send,
+    fold, rows, packed, meta, phi, table, state, model, weights, basis_0, value_0, send,
     times, z_ref, value_ref,
 ):
-    rows = packed.shape[2]
+    chunks = packed.shape[0]
     count = chunks * rows
-    meta[0, :count] = flat(packed, 0, chunks)
+    home = lax.rem(lax.axis_index("asc"), fold) * (chunks // fold) + lax.axis_index("desc")
+    state[...] = packed[home, 4 * rows :]
+    meta[0, :count] = flat_second(packed, 0, rows)
     meta[0, count:] = jnp.full((DUMMY_ROWS, LANES), -1.0, F32)
-    fill_padded(meta.at[1], flat(packed, 2, chunks))
-    fill_padded(times, flat(packed, 1, chunks))
+    fill_padded(meta.at[1], flat_second(packed, 2, rows))
+    fill_padded(times, flat_second(packed, 1, rows))
     used_rows(meta.at[0], chunks, rows, table)
     basis_loop(table, meta.at[0], times, state[...], phi, value_ref)
     role = Role(-1.0, table, meta, phi, z_ref, value_ref)
     own = value_ref[:count]
     write_chunks(send, 0, own)
-    modelled = role.cross(own, flat(packed, 3, chunks))
+    modelled = role.cross(own, flat_second(packed, 3, rows))
     model[...] = modelled
     weights[...], z = role.weigh(modelled)
     basis_0[...] = role.gradient(z, state[...])
@@ -533,24 +557,22 @@
         for q in range(nd):
             to_role.append((p * nd + q, (q * fold + p // nd) * nd + p % nd))
     to_native = [(b, a) for a, b in to_role]
-    role_desc = lax.ppermute(coef_desc, ("asc", "desc"), to_role)
-
     slots = (cross_asc, cross_desc, time_asc, time_desc, height)
     packed = call(
-        functools.partial(pack_kernel, na, nd, owned_asc, owned_desc),
-        shape((nd, fold, FIELDS, rows, LANES), F32),
-        [pltpu.VMEM((blocks, width), x.dtype) for x in slots]
+        functools.partial(pack_kernel, na, nd, owned_asc),
+        shape((nd, fold * FIELDS * rows + owned_desc, LANES), F32),
+        [pltpu.VMEM(coef_desc.shape, F32)]
+        + [pltpu.VMEM((blocks, width), x.dtype) for x in slots]
         + [
             pltpu.VMEM((1, blocks), jnp.int32),
             pltpu.VMEM((FIELDS, blocks, width), F32),
-            pltpu.SemaphoreType.DMA((len(slots) + 1,)),
+            pltpu.SemaphoreType.DMA((len(slots) + 2,)),
         ],
-        *slots, block_fill.reshape(1, blocks),
-        in_specs=[pl.BlockSpec(memory_space=pltpu.HBM)] * (len(slots) + 1),
+        coef_desc, *slots, block_fill.reshape(1, blocks),
+        in_specs=[pl.BlockSpec(memory_space=pltpu.HBM)] * (len(slots) + 2),
         mebibytes=60,
     )
     at_asc = lax.all_to_all(packed, "desc", split_axis=0, concat_axis=0, tiled=True)
-    at_asc = at_asc.reshape(na, FIELDS, rows, LANES)
 
     padded = all_rows + DUMMY_ROWS
     meta_shape = shape((2, padded, LANES), F32)
@@ -572,16 +594,16 @@
         return lax.all_to_all(x, ("asc", "desc"), split_axis=0, concat_axis=0, tiled=True)
 
     *asc, state_a, value, onward = call(
-        functools.partial(setup_asc_kernel, na),
-        role_shapes + [field_a, slot_shape, shape((na, 4, rows, LANES), F32)],
+        functools.partial(setup_asc_kernel, fold, rows),
+        role_shapes + [field_a, slot_shape, shape((na, 4 * rows + owned_desc, LANES), F32)],
         [times_scratch, scratch[1]],
-        at_asc, coef_asc, role_desc,
-    )
-    *desc, model_d, weights_d, d0, own_d, send = call(
-        functools.partial(setup_desc_kernel, na),
-        role_shapes + [slot_shape, slot_shape, field_d, slot_shape, send_shape],
+        at_asc, coef_asc,
+    )
+    *desc, state_d, model_d, weights_d, d0, own_d, send = call(
+        functools.partial(setup_desc_kernel, fold, rows),
+        role_shapes + [field_d, slot_shape, slot_shape, field_d, slot_shape, send_shape],
         [times_scratch] + scratch,
-        exchange(onward), role_desc,
+        exchange(onward),
     )
     model_a, weights_a, crossed_a0, a0, a1, own_a, send = call(
         functools.partial(first_asc_kernel, na),
@@ -609,7 +631,7 @@
         ],
         scratch,
         share(scalars), *asc, model_a, crossed_a0, crossed_a1, crossed_a2,
-        a0, a1, a2, d0, d1, d2, state_a, role_desc, own_a,
+        a0, a1, a2, d0, d1, d2, state_a, state_d, own_a,
     )
     weights_d, crossed_d0, d0, d1, own_d, send = call(
         functools.partial(next_desc_kernel, na),

time: 127 us -> 124 us (0.976)
  blocking collectives: 77 us -> 90.6 us
  starting transfers between devices: 8.35 us -> 0.65 us
  waiting for transfers between devices: 5.06 us -> 0.01 us
  Pallas kernels: 35.2 us -> 32.4 us
    all_to_all x0 -> x1, blocking collectives: none -> 14.5 us  [body(): lax.all_to_all(packed, 'desc', split_axis=0, concat_axis=0, tiled=True)]
    all_to_all x1 -> x0, starting transfers between devices: 6.33 us -> none  [body(): lax.all_to_all(packed, 'desc', split_axis=0, concat_axis=0, tiled=True)]
    all_to_all x1 -> x0, waiting for transfers between devices: 5.06 us -> none  [body(): lax.all_to_all(packed, 'desc', split_axis=0, concat_axis=0, tiled=True)]
    pallas_call x11, Pallas kernels: 35.2 us -> 32.4 us  [call(): pl.pallas_call(kernel, out_shape=outs, in_specs=[place(x) for x in args]...]
    ppermute x1 -> x0, starting transfers between devices: 1.37 us -> none  [body(): role_desc = lax.ppermute(coef_desc, ('asc', 'desc'), to_role)]
  transfers between devices with their start and end apart: 3 -> 1, of which waited for: 1 -> 0; matrix products, arithmetic and copies ran while one was open for 0% -> 0% of each run, Pallas kernels for 0% -> 0%
where the time goes in v6:
time: 124 us; the launch traced here: 125 us
  blocking collectives  90.6 us (73%)
  Pallas kernels  32.4 us (26%)
    all_to_all x7, blocking collectives, exchange(): return lax.all_to_all(x, 'asc', split_axis=0, concat_axis=0, tiled=True)  55.3 us
    pallas_call x11, Pallas kernels, call(): pl.pallas_call(kernel, out_shape=outs, in_specs=[place(x) for x in args]...  32.4 us
    all_to_all x2, blocking collectives, share(): lax.all_to_all(x, ('asc', 'desc'), split_axis=0, concat_axis=0, tiled=True)  20.8 us
    all_to_all x1, blocking collectives, body(): lax.all_to_all(packed, 'desc', split_axis=0, concat_axis=0, tiled=True)  14.5 us
  transfers between devices with their start and end apart: 1, of which 0 were waited for; matrix products, arithmetic and copies ran while one was open for 0% of the time, Pallas kernels for 0%

profile of v6, /device:TPU:0, one launch (start us, length us, event | category | flops | bytes accessed | tf_op | source)
XLA Modules:
  0.0 125.1 jit_solution(1420365921548483966)
XLA Ops:
  0.6 2.2 %shard_map.95 = f32[4,112,128]{2,1,0:T(8,128)} custom-call(f32[32,128]{1,0:T(8,128)} %coef_in.1, s32[64,128]{1,0:T(8,128)} %ca_in.1, s32[64,128]{1,0:T(8,128)} %cd_in.1, f32[64,128]{1,0:T(8,128)} %ta_in.1, f32[64,128]{1,0:T(8,128)} %td_in.1, f32[64,128]{1,0:T(8,128)} %height_in.1, s32[1,64]{1,0:T(1,128)} %bitcast.9), custom_call_target="tpu_custom_call" | custom-call | tf_op jit(solution)/shard_map/pallas_call | solution.py:546
  2.8 14.5 %all_to_all.50.packed = f32[4,112,128]{2,1,0:T(8,128)S(1)} all-to-all(f32[4,112,128]{2,1,0:T(8,128)} %shard_map.95), channel_id=1, replica_groups=mesh['asc'=8,'desc'=4] {'desc'}, dimensions={0} | all-to-all | bytes 458752 | tf_op jit(solution)/shard_map/all_to_all | solution.py:575
  17.3 0.0 copy-start
  17.3 0.7 copy-done
  18.1 2.4 %shard_map.96 = (f32[2,72,128]{2,1,0:T(8,128)S(1)}, bf16[8,256,1024]{2,1,0:T(8,128)(2,1)S(1)}, s32[81]{0:T(128)S(1)}, f32[32,128]{1,0:T(8,128)S(1)}, f32[64,128]{1,0:T(8,128)S(1)}, /*index=5*/f32[8,64,128]{2,1,0:T(8,128)S(1)}) custom-call(f32[4,112,128]{2,1,0:T(8,128)S(1)} %all_to_all.50.packed, f32[32,128]{1,0:T(8,128)S(1)} %copy-done), custom_call_target="tpu_custom_call" | custom-call | tf_op jit(solution)/shard_map/pallas_call | solution.py:546
  20.5 10.4 %all_to_all.51.packed = f32[8,64,128]{2,1,0:T(8,128)S(1)} all-to-all(f32[8,64,128]{2,1,0:T(8,128)S(1)} %get-tuple-element.53), channel_id=1, replica_groups=mesh['asc'=8,'desc'=4] {'asc'}, dimensions={0} | all-to-all | bytes 524288 | tf_op jit(solution)/shard_map/all_to_all | solution.py:591
  30.9 4.7 %shard_map.97 = (f32[2,72,128]{2,1,0:T(8,128)S(1)}, bf16[8,256,1024]{2,1,0:T(8,128)(2,1)S(1)}, s32[81]{0:T(128)S(1)}, f32[32,128]{1,0:T(8,128)S(1)}, f32[64,128]...) custom-call(f32[8,64,128]{2,1,0:T(8,128)S(1)} %all_to_all.51.packed), custom_call_target="tpu_custom_call" | custom-call | tf_op jit(solution)/shard_map/pallas_call | solution.py:546
  35.6 7.4 %all_to_all.52.got = f32[8,2,8,128]{3,2,1,0:T(8,128)S(1)} all-to-all(f32[8,2,8,128]{3,2,1,0:T(8,128)S(1)} %get-tuple-element.54), channel_id=1, replica_groups=mesh['asc'=8,'desc'=4] {'asc'}, dimensions={0} | all-to-all | bytes 131072 | tf_op jit(solution)/shard_map/all_to_all | solution.py:591
  43.0 3.1 %shard_map.98 = (f32[64,128]{1,0:T(8,128)S(1)}, f32[64,128]{1,0:T(8,128)S(1)}, f32[64,128]{1,0:T(8,128)S(1)}, f32[32,128]{1,0:T(8,128)S(1)}, f32[32,128]{1,0:T(8...) custom-call(f32[8,2,8,128]{3,2,1,0:T(8,128)S(1)} %all_to_all.52.got, ...), custom_call_target="tpu_custom_call" | custom-call | tf_op jit(solution)/shard_map/pallas_call | solution.py:546
  46.2 7.6 %all_to_all.53.got = f32[8,2,8,128]{3,2,1,0:T(8,128)S(1)} all-to-all(f32[8,2,8,128]{3,2,1,0:T(8,128)S(1)} %get-tuple-element.60), channel_id=1, replica_groups=mesh['asc'=8,'desc'=4] {'asc'}, dimensions={0} | all-to-all | bytes 131072 | tf_op jit(solution)/shard_map/all_to_all | solution.py:591
  53.8 4.1 %shard_map.99 = (f32[64,128]{1,0:T(8,128)S(1)}, f32[64,128]{1,0:T(8,128)S(1)}, f32[32,128]{1,0:T(8,128)S(1)}, f32[32,128]{1,0:T(8,128)S(1)}, f32[64,128]{1,0:T(8,128)S(1)}, /*index=5*/f32[8,2,8,128]{3,2,1,0:T(8,128)S(1)}) custom-call(f32[8,2,8,128]{3,2,1,0:T(8,128)S(1)} %all_to_all.53.got, f32[64,128]{1,0:T(8,128)S(1)} %get-tuple-element.61.value_0, ...), custom_call_target="tpu_custom_call" | custom-call | tf_op jit(solution)/shard_map/pallas_call | solution.py:546
  58.0 7.4 %all_to_all.54.got = f32[8,2,8,128]{3,2,1,0:T(8,128)S(1)} all-to-all(f32[8,2,8,128]{3,2,1,0:T(8,128)S(1)} %get-tuple-element.67), channel_id=1, replica_groups=mesh['asc'=8,'desc'=4] {'asc'}, dimensions={0} | all-to-all | bytes 131072 | tf_op jit(solution)/shard_map/all_to_all | solution.py:591
  65.4 2.0 %shard_map.100 = (f32[64,128]{1,0:T(8,128)S(1)}, f32[64,128]{1,0:T(8,128)S(1)}, f32[32,128]{1,0:T(8,128)S(1)}, f32[64,128]{1,0:T(8,128)S(1)}, f32[32,1,128]{2,1,0:T(1,128)S(1)}) custom-call(f32[8,2,8,128]{3,2,1,0:T(8,128)S(1)} %all_to_all.54.got, f32[64,128]{1,0:T(8,128)S(1)} %get-tuple-element.68.value_1, f32[2,72,128]{2,1,0:T(8,128)S(1)} %get-tuple-element.56.meta, ...), custom_call_target="tpu_custom_call" | custom-call | tf_op jit(solution)/shard_map/pallas_call | solution.py:546
  67.3 9.3 %all_to_all.55.scalars = f32[32,1,128]{2,1,0:T(1,128)S(1)} all-to-all(f32[32,1,128]{2,1,0:T(1,128)S(1)} %get-tuple-element.75), channel_id=1, replica_groups=mesh['asc'=8,'desc'=4] {'asc','desc'}, dimensions={0} | all-to-all | bytes 32768 | tf_op jit(solution)/shard_map/all_to_all | solution.py:594
  76.6 2.2 %shard_map.101 = (f32[32,128]{1,0:T(8,128)S(1)}, f32[32,128]{1,0:T(8,128)S(1)}, f32[8,128]{1,0:T(8,128)S(1)}, f32[64,128]{1,0:T(8,128)S(1)}, f32[32,128]{1,0:T(8...) custom-call(f32[32,1,128]{2,1,0:T(1,128)S(1)} %all_to_all.55.scalars, ...), custom_call_target="tpu_custom_call" | custom-call | tf_op jit(solution)/shard_map/pallas_call | solution.py:546
  78.8 7.4 %all_to_all.56.got = f32[8,2,8,128]{3,2,1,0:T(8,128)S(1)} all-to-all(f32[8,2,8,128]{3,2,1,0:T(8,128)S(1)} %get-tuple-element.82), channel_id=1, replica_groups=mesh['asc'=8,'desc'=4] {'asc'}, dimensions={0} | all-to-all | bytes 131072 | tf_op jit(solution)/shard_map/all_to_all | solution.py:591
  86.2 4.1 %shard_map.102 = (f32[64,128]{1,0:T(8,128)S(1)}, f32[64,128]{1,0:T(8,128)S(1)}, f32[32,128]{1,0:T(8,128)S(1)}, f32[32,128]{1,0:T(8,128)S(1)}, f32[64,128]{1,0:T(8,128)S(1)}, /*index=5*/f32[8,2,8,128]{3,2,1,0:T(8,128)S(1)}) custom-call(f32[8,2,8,128]{3,2,1,0:T(8,128)S(1)} %all_to_all.56.got, f32[8,128]{1,0:T(8,128)S(1)} %get-tuple-element.83.shares, ...), custom_call_target="tpu_custom_call" | custom-call | tf_op jit(solution)/shard_map/pallas_call | solution.py:546
  90.4 7.4 %all_to_all.57.got = f32[8,2,8,128]{3,2,1,0:T(8,128)S(1)} all-to-all(f32[8,2,8,128]{3,2,1,0:T(8,128)S(1)} %get-tuple-element.89), channel_id=1, replica_groups=mesh['asc'=8,'desc'=4] {'asc'}, dimensions={0} | all-to-all | bytes 131072 | tf_op jit(solution)/shard_map/all_to_all | solution.py:591
  97.8 3.8 %shard_map.103 = (f32[64,128]{1,0:T(8,128)}, f32[64,128]{1,0:T(8,128)}, f32[32,128]{1,0:T(8,128)S(1)}, f32[32,128]{1,0:T(8,128)S(1)}, f32[64,128]{1,0:T(8,128)}, /*index=5*/f32[8,2,8,128]{3,2,1,0:T(8,128)S(1)}) custom-call(f32[8,2,8,128]{3,2,1,0:T(8,128)S(1)} %all_to_all.57.got, f32[64,128]{1,0:T(8,128)S(1)} %get-tuple-element.90.value_0, ...), custom_call_target="tpu_custom_call" | custom-call | tf_op jit(solution)/shard_map/pallas_call | solution.py:546
  101.5 7.6 %all_to_all.58.got = f32[8,2,8,128]{3,2,1,0:T(8,128)S(1)} all-to-all(f32[8,2,8,128]{3,2,1,0:T(8,128)S(1)} %get-tuple-element.93), channel_id=1, replica_groups=mesh['asc'=8,'desc'=4] {'asc'}, dimensions={0} | all-to-all | bytes 131072 | tf_op jit(solution)/shard_map/all_to_all | solution.py:591
  109.2 3.0 %shard_map.104 = (f32[64,128]{1,0:T(8,128)}, f32[64,128]{1,0:T(8,128)}, f32[32,128]{1,0:T(8,128)S(1)}, f32[64,128]{1,0:T(8,128)}, f32[32,1,128]{2,1,0:T(1,128)S(1)}) custom-call(f32[8,2,8,128]{3,2,1,0:T(8,128)S(1)} %all_to_all.58.got, f32[64,128]{1,0:T(8,128)S(1)} %get-tuple-element.94.value_1, f32[2,72,128]{2,1,0:T(8,128)S(1)} %get-tuple-element.62.meta, ...), custom_call_target="tpu_custom_call" | custom-call | tf_op jit(solution)/shard_map/pallas_call | solution.py:546
  112.2 0.7 collective-permute-start
  112.9 11.5 %all_to_all.59.scalars = f32[32,1,128]{2,1,0:T(1,128)S(1)} all-to-all(f32[32,1,128]{2,1,0:T(1,128)S(1)} %get-tuple-element.101), channel_id=1, replica_groups=mesh['asc'=8,'desc'=4] {'asc','desc'}, dimensions={0} | all-to-all | bytes 32768 | tf_op jit(solution)/shard_map/all_to_all | solution.py:594
  124.4 0.0 collective-permute-done.desc
  124.4 0.8 shard_map.105
  (1 shorter events, 0.0 us)
Async XLA Ops:
  17.3 0.7 copy-start
  112.2 12.2 %collective-permute-start = (f32[4,32,128]{2,1,0:T(8,128)S(1)}, f32[4,32,128]{2,1,0:T(8,128)S(1)}, u32[]{:S(2)}, u32[]{:S(2)}) collective-permute-start(f32[4,32,128]{2,1,0:T(8,128)S(1)} %pad_maximum_fusion), channel_id=1, source_target_pairs={{0,0},{8,1},{16,2},{24,3},{1,4},{9,5},{17,6},{25,7},{2,8},{10,9},{... | collective-permute-start | bytes 196616 | tf_op jit(solution)/shard_map/ppermute | solution.py:655

commit v7 on v6

--- a/solution.py
+++ b/solution.py
@@ -245,12 +245,11 @@
     def __init__(self, sign, table, meta, phi, z_ref, value_ref):
         self.sign = sign
         self.table = table
-        self.ids = meta.at[0]
-        self.meta = meta
+        self.ids = meta
         self.phi = phi
         self.z_ref = z_ref
         self.value_ref = value_ref
-        self.count = meta.shape[1] - DUMMY_ROWS
+        self.count = meta.shape[0] - DUMMY_ROWS
 
     def cross(self, mine, other):
         return mine - other if self.sign > 0 else other - mine
@@ -298,9 +297,9 @@
         over_blocks(self.table, ahead, 0)
         return self.value_ref[: self.count]
 
-    def weigh(self, model):
-        live = self.meta[0, : self.count] >= 0.0
-        misfit = jnp.where(live, self.meta[1, : self.count] - model, 0.0)
+    def weigh(self, residual):
+        live = self.ids[: self.count] >= 0.0
+        misfit = jnp.where(live, residual, 0.0)
         weight = jnp.where(live, 1.0 / (1.0 + misfit * misfit / cauchy_square), 0.0)
         return weight, weight * misfit
 
@@ -324,47 +323,45 @@
 
 
 def setup_asc_kernel(
-    fold, rows, packed, coef, meta, phi, table, state, value, onward, times, value_ref
+    fold, rows, packed, coef, meta, phi, table, state, short, onward, times, value_ref
 ):
     state[...] = coef[...]
     chunks = packed.shape[0] * fold
     count = chunks * rows
-    meta[0, :count] = flat_first(packed, 0, fold, rows)
-    meta[0, count:] = jnp.full((DUMMY_ROWS, LANES), -1.0, F32)
-    fill_padded(meta.at[1], flat_first(packed, 4, fold, rows))
+    meta[:count] = flat_first(packed, 0, fold, rows)
+    meta[count:] = jnp.full((DUMMY_ROWS, LANES), -1.0, F32)
     fill_padded(times, flat_first(packed, 1, fold, rows))
-    used_rows(meta.at[0], chunks, rows, table)
-    basis_loop(table, meta.at[0], times, coef[...], phi, value_ref)
-    value[...] = value_ref[:count]
+    used_rows(meta, chunks, rows, table)
+    basis_loop(table, meta, times, coef[...], phi, value_ref)
+    short[...] = flat_first(packed, 4, fold, rows) - value_ref[:count]
     for j in range(chunks):
         base = j % fold * FIELDS
-        for f in range(3):
+        for f in range(2):
             start = (base + f + 2) * rows
             onward[j, f * rows : (f + 1) * rows] = packed[j // fold, start : start + rows]
-        onward[j, 3 * rows : 4 * rows] = value_ref[j * rows : (j + 1) * rows]
-        onward[j, 4 * rows :] = packed[j // fold, fold * FIELDS * rows :]
+        onward[j, 2 * rows : 3 * rows] = short[j * rows : (j + 1) * rows]
+        onward[j, 3 * rows :] = packed[j // fold, fold * FIELDS * rows :]
 
 
 def setup_desc_kernel(
-    fold, rows, packed, meta, phi, table, state, model, weights, basis_0, value_0, send,
+    fold, rows, packed, meta, phi, table, state, residual, weights, basis_0, value_0, send,
     times, z_ref, value_ref,
 ):
     chunks = packed.shape[0]
     count = chunks * rows
     home = lax.rem(lax.axis_index("asc"), fold) * (chunks // fold) + lax.axis_index("desc")
-    state[...] = packed[home, 4 * rows :]
-    meta[0, :count] = flat_second(packed, 0, rows)
-    meta[0, count:] = jnp.full((DUMMY_ROWS, LANES), -1.0, F32)
-    fill_padded(meta.at[1], flat_second(packed, 2, rows))
+    state[...] = packed[home, 3 * rows :]
+    meta[:count] = flat_second(packed, 0, rows)
+    meta[count:] = jnp.full((DUMMY_ROWS, LANES), -1.0, F32)
     fill_padded(times, flat_second(packed, 1, rows))
-    used_rows(meta.at[0], chunks, rows, table)
-    basis_loop(table, meta.at[0], times, state[...], phi, value_ref)
+    used_rows(meta, chunks, rows, table)
+    basis_loop(table, meta, times, state[...], phi, value_ref)
     role = Role(-1.0, table, meta, phi, z_ref, value_ref)
     own = value_ref[:count]
     write_chunks(send, 0, own)
-    modelled = role.cross(own, flat_second(packed, 3, rows))
-    model[...] = modelled
-    weights[...], z = role.weigh(modelled)
+    left = flat_second(packed, 2, rows) + own
+    residual[...] = left
+    weights[...], z = role.weigh(left)
     basis_0[...] = role.gradient(z, state[...])
     own = role.forward(basis_0[...])
     value_0[...] = own
@@ -372,13 +369,13 @@
 
 
 def first_asc_kernel(
-    chunks, got, value, meta, phi, table, state,
-    model, weights, crossed_0, basis_0, basis_1, value_1, send, z_ref, value_ref,
+    chunks, got, short, meta, phi, table, state,
+    residual, weights, crossed_0, basis_0, basis_1, value_1, send, z_ref, value_ref,
 ):
     role = Role(1.0, table, meta, phi, z_ref, value_ref)
-    modelled = role.cross(value[...], flat(got, 0, chunks))
-    model[...] = modelled
-    weights[...], z = role.weigh(modelled)
+    left = short[...] + flat(got, 0, chunks)
+    residual[...] = left
+    weights[...], z = role.weigh(left)
     basis_0[...] = role.gradient(z, state[...])
     own = role.forward(basis_0[...])
     write_chunks(send, 0, own)
@@ -440,8 +437,7 @@
         line = jnp.where(lane == place_in_line, curve, line)
         if i == 0:
             line = jnp.where(lane == len(PAIRS) + j, dots, line)
-    for d in range(scalars.shape[0]):
-        scalars[d] = line
+    scalars[0] = line
 
 
 def solve(scalars):
@@ -485,7 +481,7 @@
 
 
 def next_asc_kernel(
-    chunks, scalars, meta, phi, table, model, crossed_0, crossed_1, crossed_2,
+    chunks, scalars, meta, phi, table, residual, crossed_0, crossed_1, crossed_2,
     basis_a0, basis_a1, basis_a2, basis_d0, basis_d1, basis_d2, state_a, state_d, value_2,
     new_a, new_d, shares, weights, basis_0, value_0, send, z_ref, value_ref,
 ):
@@ -494,10 +490,10 @@
     y = solve(scalars)
     for i in range(3):
         shares[i : i + 1] = jnp.broadcast_to(y[i], (1, LANES))
-    modelled = model[...] + combine(y, [crossed_0[...], crossed_1[...], crossed_2[...]])
+    left = residual[...] - combine(y, [crossed_0[...], crossed_1[...], crossed_2[...]])
     new_a[...] = state_a[...] + combine(y, [basis_a0[...], basis_a1[...], basis_a2[...]])
     new_d[...] = state_d[...] + combine(y, [basis_d0[...], basis_d1[...], basis_d2[...]])
-    weights[...], z = role.weigh(modelled)
+    weights[...], z = role.weigh(left)
     basis_0[...] = role.gradient(z, new_a[...])
     own = role.forward(basis_0[...])
     value_0[...] = own
@@ -505,14 +501,14 @@
 
 
 def next_desc_kernel(
-    chunks, got, shares, meta, phi, table, model, crossed_0, crossed_1, value_2, state,
+    chunks, got, shares, meta, phi, table, residual, crossed_0, crossed_1, value_2, state,
     weights, new_crossed_0, basis_0, basis_1, value_1, send, z_ref, value_ref,
 ):
     role = Role(-1.0, table, meta, phi, z_ref, value_ref)
     y = [shares[i : i + 1] for i in range(3)]
     crossed_2 = role.cross(value_2[...], flat(got, 0, chunks))
-    modelled = model[...] + combine(y, [crossed_0[...], crossed_1[...], crossed_2])
-    weights[...], z = role.weigh(modelled)
+    left = residual[...] - combine(y, [crossed_0[...], crossed_1[...], crossed_2])
+    weights[...], z = role.weigh(left)
     basis_0[...] = role.gradient(z, state[...])
     own = role.forward(basis_0[...])
     write_chunks(send, 0, own)
@@ -575,7 +571,7 @@
     at_asc = lax.all_to_all(packed, "desc", split_axis=0, concat_axis=0, tiled=True)
 
     padded = all_rows + DUMMY_ROWS
-    meta_shape = shape((2, padded, LANES), F32)
+    meta_shape = shape((padded, LANES), F32)
     phi_shape = shape((all_blocks, 2 * terms, BLOCK_ROWS * LANES), BF16)
     table_shape = shape((all_rows + rows + BLOCK_ROWS + 1,), jnp.int32)
     role_shapes = [meta_shape, phi_shape, table_shape]
@@ -583,7 +579,7 @@
     send_shape = shape((na, 2, rows, LANES), F32)
     field_a = shape(coef_asc.shape, F32)
     field_d = shape(coef_desc.shape, F32)
-    line_shape = shape((na * nd, 1, LANES), F32)
+    line_shape = shape((1, 1, LANES), F32)
     times_scratch = pltpu.VMEM((padded, LANES), F32)
     scratch = [pltpu.VMEM((2, padded, LANES), F32), pltpu.VMEM((padded, LANES), F32)]
 
@@ -591,25 +587,25 @@
         return lax.all_to_all(x, "asc", split_axis=0, concat_axis=0, tiled=True)
 
     def share(x):
-        return lax.all_to_all(x, ("asc", "desc"), split_axis=0, concat_axis=0, tiled=True)
-
-    *asc, state_a, value, onward = call(
+        return lax.all_gather(x, ("asc", "desc"), axis=0, tiled=True)
+
+    *asc, state_a, short, onward = call(
         functools.partial(setup_asc_kernel, fold, rows),
-        role_shapes + [field_a, slot_shape, shape((na, 4 * rows + owned_desc, LANES), F32)],
+        role_shapes + [field_a, slot_shape, shape((na, 3 * rows + owned_desc, LANES), F32)],
         [times_scratch, scratch[1]],
         at_asc, coef_asc,
     )
-    *desc, state_d, model_d, weights_d, d0, own_d, send = call(
+    *desc, state_d, residual_d, weights_d, d0, own_d, send = call(
         functools.partial(setup_desc_kernel, fold, rows),
         role_shapes + [field_d, slot_shape, slot_shape, field_d, slot_shape, send_shape],
         [times_scratch] + scratch,
         exchange(onward),
     )
-    model_a, weights_a, crossed_a0, a0, a1, own_a, send = call(
+    residual_a, weights_a, crossed_a0, a0, a1, own_a, send = call(
         functools.partial(first_asc_kernel, na),
         [slot_shape, slot_shape, slot_shape, field_a, field_a, slot_shape, send_shape],
         scratch,
-        exchange(send), value, *asc, state_a,
+        exchange(send), short, *asc, state_a,
     )
     crossed_d0, crossed_d1, d1, d2, own_d, send = call(
         functools.partial(images_kernel, -1.0, na),
@@ -630,14 +626,14 @@
             slot_shape, field_a, slot_shape, send_shape,
         ],
         scratch,
-        share(scalars), *asc, model_a, crossed_a0, crossed_a1, crossed_a2,
+        share(scalars), *asc, residual_a, crossed_a0, crossed_a1, crossed_a2,
         a0, a1, a2, d0, d1, d2, state_a, state_d, own_a,
     )
     weights_d, crossed_d0, d0, d1, own_d, send = call(
         functools.partial(next_desc_kernel, na),
         [slot_shape, slot_shape, field_d, field_d, slot_shape, send_shape],
         scratch,
-        exchange(send), shares, *desc, model_d, crossed_d0, crossed_d1, own_d, state_d,
+        exchange(send), shares, *desc, residual_d, crossed_d0, crossed_d1, own_d, state_d,
     )
     _, _, a1, a2, _, send = call(
         functools.partial(images_kernel, 1.0, na),

time: 124 us -> 231 us (1.86)
  blocking collectives: 90.6 us -> 199 us
  Pallas kernels: 32.4 us -> 29 us
    all_gather x0 -> x2, blocking collectives: none -> 129 us  [share(): return lax.all_gather(x, ('asc', 'desc'), axis=0, tiled=True)]
    all_to_all x2 -> x0, blocking collectives: 20.8 us -> none  [share(): lax.all_to_all(x, ('asc', 'desc'), split_axis=0, concat_axis=0, tiled=True)]
    pallas_call x11, Pallas kernels: 32.4 us -> 29 us  [call(): pl.pallas_call(kernel, out_shape=outs, in_specs=[place(x) for x in args]...]
where the time goes in v7:
time: 231 us
  blocking collectives  199 us (86%)
  Pallas kernels  29 us (13%)
    all_gather x2, blocking collectives, share(): return lax.all_gather(x, ('asc', 'desc'), axis=0, tiled=True)  129 us
    all_to_all x7, blocking collectives, exchange(): return lax.all_to_all(x, 'asc', split_axis=0, concat_axis=0, tiled=True)  55.6 us
    pallas_call x11, Pallas kernels, call(): pl.pallas_call(kernel, out_shape=outs, in_specs=[place(x) for x in args]...  29 us
    all_to_all x1, blocking collectives, body(): lax.all_to_all(packed, 'desc', split_axis=0, concat_axis=0, tiled=True)  14.5 us
  transfers between devices with their start and end apart: 1, of which 0 were waited for; matrix products, arithmetic and copies ran while one was open for 0% of the time, Pallas kernels for 0%

profile of v7, /device:TPU:0, one launch (start us, length us, event | category | flops | bytes accessed | tf_op | source)
XLA Modules:
  0.0 230.5 jit_solution(14650901275742755465)
XLA Ops:
  0.6 2.2 shard_map.95
  2.8 14.5 %all_to_all.40.packed = f32[4,112,128]{2,1,0:T(8,128)S(1)} all-to-all(f32[4,112,128]{2,1,0:T(8,128)} %shard_map.95), channel_id=1, replica_groups=mesh['asc'=8,'desc'=4] {'desc'}, dimensions={0} | all-to-all | bytes 458752 | tf_op jit(solution)/shard_map/all_to_all | solution.py:571
  17.3 0.0 copy-start
  17.3 0.7 copy-done
  18.1 2.4 %shard_map.96 = (f32[72,128]{1,0:T(8,128)S(1)}, bf16[8,256,1024]{2,1,0:T(8,128)(2,1)S(1)}, s32[81]{0:T(128)S(1)}, f32[32,128]{1,0:T(8,128)S(1)}, f32[64,128]{1,0:T(8,128)S(1)}, /*index=5*/f32[8,56,128]{2,1,0:T(8,128)S(1)}) custom-call(f32[4,112,128]{2,1,0:T(8,128)S(1)} %all_to_all.40.packed, f32[32,128]{1,0:T(8,128)S(1)} %copy-done), custom_call_target="tpu_custom_call" | custom-call | tf_op jit(solution)/shard_map/pallas_call | solution.py:542
  20.5 10.5 %all_to_all.41.packed = f32[8,56,128]{2,1,0:T(8,128)S(1)} all-to-all(f32[8,56,128]{2,1,0:T(8,128)S(1)} %get-tuple-element.53), channel_id=1, replica_groups=mesh['asc'=8,'desc'=4] {'asc'}, dimensions={0} | all-to-all | bytes 458752 | tf_op jit(solution)/shard_map/all_to_all | solution.py:587
  31.0 3.7 %shard_map.97 = (f32[72,128]{1,0:T(8,128)S(1)}, bf16[8,256,1024]{2,1,0:T(8,128)(2,1)S(1)}, s32[81]{0:T(128)S(1)}, f32[32,128]{1,0:T(8,128)S(1)}, f32[64,128]{1,0...) custom-call(f32[8,56,128]{2,1,0:T(8,128)S(1)} %all_to_all.41.packed), custom_call_target="tpu_custom_call" | custom-call | tf_op jit(solution)/shard_map/pallas_call | solution.py:542
  34.8 7.4 %all_to_all.42.got = f32[8,2,8,128]{3,2,1,0:T(8,128)S(1)} all-to-all(f32[8,2,8,128]{3,2,1,0:T(8,128)S(1)} %get-tuple-element.54), channel_id=1, replica_groups=mesh['asc'=8,'desc'=4] {'asc'}, dimensions={0} | all-to-all | bytes 131072 | tf_op jit(solution)/shard_map/all_to_all | solution.py:587
  42.2 3.1 %shard_map.98 = (f32[64,128]{1,0:T(8,128)S(1)}, f32[64,128]{1,0:T(8,128)S(1)}, f32[64,128]{1,0:T(8,128)S(1)}, f32[32,128]{1,0:T(8,128)S(1)}, f32[32,128]{1,0:T(8...) custom-call(f32[8,2,8,128]{3,2,1,0:T(8,128)S(1)} %all_to_all.42.got, ...), custom_call_target="tpu_custom_call" | custom-call | tf_op jit(solution)/shard_map/pallas_call | solution.py:542
  45.3 7.7 %all_to_all.43.got = f32[8,2,8,128]{3,2,1,0:T(8,128)S(1)} all-to-all(f32[8,2,8,128]{3,2,1,0:T(8,128)S(1)} %get-tuple-element.60), channel_id=1, replica_groups=mesh['asc'=8,'desc'=4] {'asc'}, dimensions={0} | all-to-all | bytes 131072 | tf_op jit(solution)/shard_map/all_to_all | solution.py:587
  53.0 3.1 %shard_map.99 = (f32[64,128]{1,0:T(8,128)S(1)}, f32[64,128]{1,0:T(8,128)S(1)}, f32[32,128]{1,0:T(8,128)S(1)}, f32[32,128]{1,0:T(8,128)S(1)}, f32[64,128]{1,0:T(8,128)S(1)}, /*index=5*/f32[8,2,8,128]{3,2,1,0:T(8,128)S(1)}) custom-call(f32[8,2,8,128]{3,2,1,0:T(8,128)S(1)} %all_to_all.43.got, f32[64,128]{1,0:T(8,128)S(1)} %get-tuple-element.61.value_0, ...), custom_call_target="tpu_custom_call" | custom-call | tf_op jit(solution)/shard_map/pallas_call | solution.py:542
  56.1 7.4 %all_to_all.44.got = f32[8,2,8,128]{3,2,1,0:T(8,128)S(1)} all-to-all(f32[8,2,8,128]{3,2,1,0:T(8,128)S(1)} %get-tuple-element.67), channel_id=1, replica_groups=mesh['asc'=8,'desc'=4] {'asc'}, dimensions={0} | all-to-all | bytes 131072 | tf_op jit(solution)/shard_map/all_to_all | solution.py:587
  63.5 2.0 shard_map.100
  65.5 63.9 %all_gather.6.scalars = f32[32,1,128]{2,1,0:T(1,128)S(1)} all-gather(f32[1,1,128]{2,1,0:T(1,128)S(1)} %get-tuple-element.75), channel_id=1, replica_groups=mesh['asc'=8,'desc'=4] {'asc','desc'}, dimensions={0}, use_global_device_ids=true | all-gather | bytes 16896 | tf_op jit(solution)/shard_map/all_gather | solution.py:590
  129.4 2.2 shard_map.101
  131.6 7.6 %all_to_all.45.got = f32[8,2,8,128]{3,2,1,0:T(8,128)S(1)} all-to-all(f32[8,2,8,128]{3,2,1,0:T(8,128)S(1)} %get-tuple-element.82), channel_id=1, replica_groups=mesh['asc'=8,'desc'=4] {'asc'}, dimensions={0} | all-to-all | bytes 131072 | tf_op jit(solution)/shard_map/all_to_all | solution.py:587
  139.2 3.2 %shard_map.102 = (f32[64,128]{1,0:T(8,128)S(1)}, f32[64,128]{1,0:T(8,128)S(1)}, f32[32,128]{1,0:T(8,128)S(1)}, f32[32,128]{1,0:T(8,128)S(1)}, f32[64,128]{1,0:T(8,128)S(1)}, /*index=5*/f32[8,2,8,128]{3,2,1,0:T(8,128)S(1)}) custom-call(f32[8,2,8,128]{3,2,1,0:T(8,128)S(1)} %all_to_all.45.got, f32[8,128]{1,0:T(8,128)S(1)} %get-tuple-element.83.shares, ...), custom_call_target="tpu_custom_call" | custom-call | tf_op jit(solution)/shard_map/pallas_call | solution.py:542
  142.3 7.4 %all_to_all.46.got = f32[8,2,8,128]{3,2,1,0:T(8,128)S(1)} all-to-all(f32[8,2,8,128]{3,2,1,0:T(8,128)S(1)} %get-tuple-element.89), channel_id=1, replica_groups=mesh['asc'=8,'desc'=4] {'asc'}, dimensions={0} | all-to-all | bytes 131072 | tf_op jit(solution)/shard_map/all_to_all | solution.py:587
  149.7 3.8 %shard_map.103 = (f32[64,128]{1,0:T(8,128)}, f32[64,128]{1,0:T(8,128)}, f32[32,128]{1,0:T(8,128)S(1)}, f32[32,128]{1,0:T(8,128)S(1)}, f32[64,128]{1,0:T(8,128)}, /*index=5*/f32[8,2,8,128]{3,2,1,0:T(8,128)S(1)}) custom-call(f32[8,2,8,128]{3,2,1,0:T(8,128)S(1)} %all_to_all.46.got, f32[64,128]{1,0:T(8,128)S(1)} %get-tuple-element.90.value_0, ...), custom_call_target="tpu_custom_call" | custom-call | tf_op jit(solution)/shard_map/pallas_call | solution.py:542
  153.5 7.6 %all_to_all.47.got = f32[8,2,8,128]{3,2,1,0:T(8,128)S(1)} all-to-all(f32[8,2,8,128]{3,2,1,0:T(8,128)S(1)} %get-tuple-element.93), channel_id=1, replica_groups=mesh['asc'=8,'desc'=4] {'asc'}, dimensions={0} | all-to-all | bytes 131072 | tf_op jit(solution)/shard_map/all_to_all | solution.py:587
  161.1 2.5 %shard_map.104 = (f32[64,128]{1,0:T(8,128)}, f32[64,128]{1,0:T(8,128)}, f32[32,128]{1,0:T(8,128)S(1)}, f32[64,128]{1,0:T(8,128)}, f32[1,1,128]{2,1,0:T(1,128)S(1)}) custom-call(f32[8,2,8,128]{3,2,1,0:T(8,128)S(1)} %all_to_all.47.got, f32[64,128]{1,0:T(8,128)S(1)} %get-tuple-element.94.value_1, f32[72,128]{1,0:T(8,128)S(1)} %get-tuple-element.62.meta, ...), custom_call_target="tpu_custom_call" | custom-call | tf_op jit(solution)/shard_map/pallas_call | solution.py:542
  163.6 0.7 collective-permute-start
  164.3 65.5 %all_gather.7.scalars = f32[32,1,128]{2,1,0:T(1,128)S(1)} all-gather(f32[1,1,128]{2,1,0:T(1,128)S(1)} %get-tuple-element.101), channel_id=1, replica_groups=mesh['asc'=8,'desc'=4] {'asc','desc'}, dimensions={0}, use_global_device_ids=true | all-gather | bytes 16896 | tf_op jit(solution)/shard_map/all_gather | solution.py:590
  229.7 0.0 collective-permute-done.desc
  229.8 0.8 shard_map.105
  (1 shorter events, 0.0 us)
Async XLA Ops:
  17.3 0.7 copy-start
  163.6 66.1 %collective-permute-start = (f32[4,32,128]{2,1,0:T(8,128)S(1)}, f32[4,32,128]{2,1,0:T(8,128)S(1)}, u32[]{:S(2)}, u32[]{:S(2)}) collective-permute-start(f32[4,32,128]{2,1,0:T(8,128)S(1)} %pad_maximum_fusion), channel_id=1, source_target_pairs={{0,0},{8,1},{16,2},{24,3},{1,4},{9,5},{17,6},{25,7},{2,8},{10,9},{... | collective-permute-start | bytes 196616 | tf_op jit(solution)/shard_map/ppermute | solution.py:651

commit v8 on v7

--- a/solution.py
+++ b/solution.py
@@ -29,16 +29,12 @@
 SIN_TERMS = [(-1.0) ** i * math.pi ** (2 * i + 1) / math.factorial(2 * i + 1) for i in range(7)]
 
 
-def in_smem(x):
-    return x.dtype == jnp.int32 and len(x.shape) == 1
-
-
 def params(mebibytes):
     return pltpu.CompilerParams(vmem_limit_bytes=mebibytes * 1024 * 1024)
 
 
 def place(x):
-    return pl.BlockSpec(memory_space=pltpu.SMEM if in_smem(x) else pltpu.VMEM)
+    return pl.BlockSpec(memory_space=pltpu.VMEM)
 
 
 def split(x):
@@ -85,8 +81,7 @@
     ]
     for copy in copies:
         copy.start()
-    for copy in copies:
-        copy.wait()
+    copies[0].wait()
     owned_desc = coef.shape[0]
     blocks, width = ca.shape
     group = width // na
@@ -100,18 +95,20 @@
     lane = lax.broadcasted_iota(jnp.int32, (blocks, width), 1)
     live = lane.astype(F32) < fill_col
     fields = [
-        jnp.where(live, local_id(ca[...], owned_asc).astype(F32), -1.0),
-        ta[...],
-        jnp.where(live, local_id(cd[...], owned_desc).astype(F32), -1.0),
-        td[...],
-        height[...],
+        lambda: jnp.where(live, local_id(ca[...], owned_asc).astype(F32), -1.0),
+        lambda: ta[...],
+        lambda: jnp.where(live, local_id(cd[...], owned_desc).astype(F32), -1.0),
+        lambda: td[...],
+        lambda: height[...],
     ]
     source = lax.broadcasted_iota(jnp.int32, (width, width), 0)
     target = lax.broadcasted_iota(jnp.int32, (width, width), 1)
     owner = target // group
     place = target - owner * group
     order = (source == place * na + owner).astype(F32).astype(BF16)
-    for f, x in enumerate(fields):
+    for f, field in enumerate(fields):
+        copies[1 + f].wait()
+        x = field()
         high = x.astype(BF16)
         rest = x - high.astype(F32)
         middle = rest.astype(BF16)
@@ -132,6 +129,7 @@
         for r in range(na):
             start = (r // nd * FIELDS + f) * rows
             out[r % nd, start : start + rows] = parts[r]
+    copies[-1].wait()
     for q in range(nd):
         out[q, out.shape[1] - owned_desc :] = coef[...]
 
@@ -242,7 +240,10 @@
 
 
 class Role:
-    def __init__(self, sign, table, meta, phi, z_ref, value_ref):
+    def __init__(self, sign, send, meta, phi, table, z_ref, value_ref, listed=False):
+        if not listed:
+            rows = (meta.shape[0] - DUMMY_ROWS) // send.shape[0]
+            used_rows(meta, send.shape[0], rows, table)
         self.sign = sign
         self.table = table
         self.ids = meta
@@ -260,7 +261,6 @@
         self.z_ref[1, : self.count] = z - high
         self.z_ref[:, self.count :] = jnp.zeros((2, DUMMY_ROWS, LANES), F32)
         blocks, double, width = self.phi.shape
-        terms = double // 2
         row_iota = lax.broadcasted_iota(jnp.int32, (owned, width), 0).astype(F32)
 
         def gather(block, carry):
@@ -277,7 +277,10 @@
                 preferred_element_type=F32,
             )
 
-        g = over_blocks(self.table, gather, jnp.zeros((2 * owned, double), F32))
+        return self.gathered(over_blocks(self.table, gather, jnp.zeros((2 * owned, double), F32)))
+
+    def gathered(self, g):
+        owned, terms = g.shape[0] // 2, g.shape[1] // 2
         return self.sign * (g[:owned, :terms] + (g[:owned, terms:] + g[owned:, :terms]))
 
     def forward(self, field):
@@ -297,6 +300,46 @@
         over_blocks(self.table, ahead, 0)
         return self.value_ref[: self.count]
 
+    def forward_image(self, field, other, weight):
+        owned = field.shape[0]
+        stack = stacked(field)
+        blocks, double, width = self.phi.shape
+        row_iota = lax.broadcasted_iota(jnp.int32, (owned, width), 0).astype(F32)
+        fill_padded(self.z_ref.at[0], other)
+        fill_padded(self.z_ref.at[1], weight)
+        self.value_ref[...] = jnp.zeros(self.value_ref.shape, F32)
+
+        def both(block, carry):
+            rows = listed_rows(self.table, block * BLOCK_ROWS, BLOCK_ROWS)
+            phi = self.phi[block]
+            hit = row_iota == rows_pair(self.ids, rows)
+            values = []
+            for u in range(UNROLL):
+                part = slice(u * STEP_LANES, (u + 1) * STEP_LANES)
+                product = jnp.dot(stack, phi[:, part], preferred_element_type=F32)
+                value = product[:owned] + product[owned:]
+                values.append(
+                    jnp.sum(jnp.where(hit[:, part], value, 0.0), axis=0, keepdims=True)
+                )
+            value = jnp.concatenate(values, axis=1)
+            store_rows(self.value_ref, rows, value)
+            z = rows_pair(self.z_ref.at[1], rows) * self.cross(
+                value, rows_pair(self.z_ref.at[0], rows)
+            )
+            high = z.astype(BF16).astype(F32)
+            parts = [jnp.where(hit, x, 0.0).astype(BF16) for x in (high, z - high)]
+            return carry + lax.dot_general(
+                jnp.concatenate(parts, axis=0),
+                phi,
+                (((1,), (1,)), ((), ())),
+                preferred_element_type=F32,
+            )
+
+        image = self.gathered(
+            over_blocks(self.table, both, jnp.zeros((2 * owned, double), F32))
+        )
+        return self.value_ref[: self.count], SCALE * (image + damping * field)
+
     def weigh(self, residual):
         live = self.ids[: self.count] >= 0.0
         misfit = jnp.where(live, residual, 0.0)
@@ -323,7 +366,7 @@
 
 
 def setup_asc_kernel(
-    fold, rows, packed, coef, meta, phi, table, state, short, onward, times, value_ref
+    fold, rows, packed, coef, meta, phi, state, short, onward, times, table, value_ref
 ):
     state[...] = coef[...]
     chunks = packed.shape[0] * fold
@@ -344,8 +387,8 @@
 
 
 def setup_desc_kernel(
-    fold, rows, packed, meta, phi, table, state, residual, weights, basis_0, value_0, send,
-    times, z_ref, value_ref,
+    fold, rows, packed, meta, phi, state, residual, weights, basis_0, value_0, send,
+    times, table, z_ref, value_ref,
 ):
     chunks = packed.shape[0]
     count = chunks * rows
@@ -356,7 +399,7 @@
     fill_padded(times, flat_second(packed, 1, rows))
     used_rows(meta, chunks, rows, table)
     basis_loop(table, meta, times, state[...], phi, value_ref)
-    role = Role(-1.0, table, meta, phi, z_ref, value_ref)
+    role = Role(-1.0, send, meta, phi, table, z_ref, value_ref, listed=True)
     own = value_ref[:count]
     write_chunks(send, 0, own)
     left = flat_second(packed, 2, rows) + own
@@ -369,37 +412,35 @@
 
 
 def first_asc_kernel(
-    chunks, got, short, meta, phi, table, state,
-    residual, weights, crossed_0, basis_0, basis_1, value_1, send, z_ref, value_ref,
+    chunks, got, short, meta, phi, state,
+    residual, weights, crossed_0, basis_0, basis_1, value_1, send, table, z_ref, value_ref,
 ):
-    role = Role(1.0, table, meta, phi, z_ref, value_ref)
+    role = Role(1.0, send, meta, phi, table, z_ref, value_ref)
     left = short[...] + flat(got, 0, chunks)
     residual[...] = left
     weights[...], z = role.weigh(left)
     basis_0[...] = role.gradient(z, state[...])
-    own = role.forward(basis_0[...])
+    other = flat(got, 1, chunks)
+    own, basis_1[...] = role.forward_image(basis_0[...], other, weights[...])
     write_chunks(send, 0, own)
-    crossed = role.cross(own, flat(got, 1, chunks))
-    crossed_0[...] = crossed
-    basis_1[...] = role.image(weights[...] * crossed, basis_0[...])
+    crossed_0[...] = role.cross(own, other)
     own = role.forward(basis_1[...])
     value_1[...] = own
     write_chunks(send, 1, own)
 
 
 def images_kernel(
-    sign, chunks, got, value_0, meta, phi, table, weights, basis_0,
-    crossed_0, crossed_1, basis_1, basis_2, value_2, send, z_ref, value_ref,
+    sign, chunks, got, value_0, meta, phi, weights, basis_0,
+    crossed_0, crossed_1, basis_1, basis_2, value_2, send, table, z_ref, value_ref,
 ):
-    role = Role(sign, table, meta, phi, z_ref, value_ref)
+    role = Role(sign, send, meta, phi, table, z_ref, value_ref)
     crossed = role.cross(value_0[...], flat(got, 0, chunks))
     crossed_0[...] = crossed
     basis_1[...] = role.image(weights[...] * crossed, basis_0[...])
-    own = role.forward(basis_1[...])
+    other = flat(got, 1, chunks)
+    own, basis_2[...] = role.forward_image(basis_1[...], other, weights[...])
     write_chunks(send, 0, own)
-    crossed = role.cross(own, flat(got, 1, chunks))
-    crossed_1[...] = crossed
-    basis_2[...] = role.image(weights[...] * crossed, basis_1[...])
+    crossed_1[...] = role.cross(own, other)
     own = role.forward(basis_2[...])
     value_2[...] = own
     write_chunks(send, 1, own)
@@ -413,11 +454,11 @@
 
 
 def gram_kernel(
-    sign, chunks, got, value_1, meta, phi, table, weights, crossed_0, basis_0, basis_1,
+    sign, chunks, got, value_1, meta, phi, weights, crossed_0, basis_0, basis_1,
     other_0, other_1, other_2,
-    crossed_1, crossed_2, basis_2, value_2, scalars, z_ref, value_ref,
+    crossed_1, crossed_2, basis_2, value_2, scalars, table, z_ref, value_ref,
 ):
-    role = Role(sign, table, meta, phi, z_ref, value_ref)
+    role = Role(sign, got, meta, phi, table, z_ref, value_ref)
     weight = weights[...]
     crossed = role.cross(value_1[...], flat(got, 0, chunks))
     crossed_1[...] = crossed
@@ -437,7 +478,8 @@
         line = jnp.where(lane == place_in_line, curve, line)
         if i == 0:
             line = jnp.where(lane == len(PAIRS) + j, dots, line)
-    scalars[0] = line
+    for d in range(scalars.shape[0]):
+        scalars[d] = line
 
 
 def solve(scalars):
@@ -481,11 +523,11 @@
 
 
 def next_asc_kernel(
-    chunks, scalars, meta, phi, table, residual, crossed_0, crossed_1, crossed_2,
+    chunks, scalars, meta, phi, residual, crossed_0, crossed_1, crossed_2,
     basis_a0, basis_a1, basis_a2, basis_d0, basis_d1, basis_d2, state_a, state_d, value_2,
-    new_a, new_d, shares, weights, basis_0, value_0, send, z_ref, value_ref,
+    new_a, new_d, shares, weights, basis_0, value_0, send, table, z_ref, value_ref,
 ):
-    role = Role(1.0, table, meta, phi, z_ref, value_ref)
+    role = Role(1.0, send, meta, phi, table, z_ref, value_ref)
     write_chunks(send, 0, value_2[...])
     y = solve(scalars)
     for i in range(3):
@@ -501,20 +543,19 @@
 
 
 def next_desc_kernel(
-    chunks, got, shares, meta, phi, table, residual, crossed_0, crossed_1, value_2, state,
-    weights, new_crossed_0, basis_0, basis_1, value_1, send, z_ref, value_ref,
+    chunks, got, shares, meta, phi, residual, crossed_0, crossed_1, value_2, state,
+    weights, new_crossed_0, basis_0, basis_1, value_1, send, table, z_ref, value_ref,
 ):
-    role = Role(-1.0, table, meta, phi, z_ref, value_ref)
+    role = Role(-1.0, send, meta, phi, table, z_ref, value_ref)
     y = [shares[i : i + 1] for i in range(3)]
     crossed_2 = role.cross(value_2[...], flat(got, 0, chunks))
     left = residual[...] - combine(y, [crossed_0[...], crossed_1[...], crossed_2])
     weights[...], z = role.weigh(left)
     basis_0[...] = role.gradient(z, state[...])
-    own = role.forward(basis_0[...])
+    other = flat(got, 1, chunks)
+    own, basis_1[...] = role.forward_image(basis_0[...], other, weights[...])
     write_chunks(send, 0, own)
-    crossed = role.cross(own, flat(got, 1, chunks))
-    new_crossed_0[...] = crossed
-    basis_1[...] = role.image(weights[...] * crossed, basis_0[...])
+    new_crossed_0[...] = role.cross(own, other)
     own = role.forward(basis_1[...])
     value_1[...] = own
     write_chunks(send, 1, own)
@@ -573,26 +614,28 @@
     padded = all_rows + DUMMY_ROWS
     meta_shape = shape((padded, LANES), F32)
     phi_shape = shape((all_blocks, 2 * terms, BLOCK_ROWS * LANES), BF16)
-    table_shape = shape((all_rows + rows + BLOCK_ROWS + 1,), jnp.int32)
-    role_shapes = [meta_shape, phi_shape, table_shape]
+    role_shapes = [meta_shape, phi_shape]
+    table = pltpu.SMEM((all_rows + rows + BLOCK_ROWS + 1,), jnp.int32)
     slot_shape = shape((all_rows, LANES), F32)
     send_shape = shape((na, 2, rows, LANES), F32)
     field_a = shape(coef_asc.shape, F32)
     field_d = shape(coef_desc.shape, F32)
-    line_shape = shape((1, 1, LANES), F32)
+    line_shape = shape((na * nd, 1, LANES), F32)
     times_scratch = pltpu.VMEM((padded, LANES), F32)
-    scratch = [pltpu.VMEM((2, padded, LANES), F32), pltpu.VMEM((padded, LANES), F32)]
+    scratch = [
+        table, pltpu.VMEM((2, padded, LANES), F32), pltpu.VMEM((padded, LANES), F32),
+    ]
 
     def exchange(x):
         return lax.all_to_all(x, "asc", split_axis=0, concat_axis=0, tiled=True)
 
     def share(x):
-        return lax.all_gather(x, ("asc", "desc"), axis=0, tiled=True)
+        return lax.all_to_all(x, ("asc", "desc"), split_axis=0, concat_axis=0, tiled=True)
 
     *asc, state_a, short, onward = call(
         functools.partial(setup_asc_kernel, fold, rows),
         role_shapes + [field_a, slot_shape, shape((na, 3 * rows + owned_desc, LANES), F32)],
-        [times_scratch, scratch[1]],
+        [times_scratch, table, scratch[2]],
         at_asc, coef_asc,
     )
     *desc, state_d, residual_d, weights_d, d0, own_d, send = call(

time: 231 us -> 120 us (0.52)
  blocking collectives: 199 us -> 91.7 us
  Pallas kernels: 29 us -> 26.3 us
    all_gather x2 -> x0, blocking collectives: 129 us -> none  [share(): return lax.all_gather(x, ('asc', 'desc'), axis=0, tiled=True)]
    all_to_all x0 -> x2, blocking collectives: none -> 21.8 us  [share(): lax.all_to_all(x, ('asc', 'desc'), split_axis=0, concat_axis=0, tiled=True)]
    pallas_call x11, Pallas kernels: 29 us -> 26.3 us  [call(): pl.pallas_call(kernel, out_shape=outs, in_specs=[place(x) for x in args]...]
where the time goes in v8:
time: 120 us
  blocking collectives  91.7 us (76%)
  Pallas kernels  26.3 us (22%)
    all_to_all x7, blocking collectives, exchange(): return lax.all_to_all(x, 'asc', split_axis=0, concat_axis=0, tiled=True)  55.4 us
    pallas_call x11, Pallas kernels, call(): pl.pallas_call(kernel, out_shape=outs, in_specs=[place(x) for x in args]...  26.3 us
    all_to_all x2, blocking collectives, share(): lax.all_to_all(x, ('asc', 'desc'), split_axis=0, concat_axis=0, tiled=True)  21.8 us
    all_to_all x1, blocking collectives, body(): lax.all_to_all(packed, 'desc', split_axis=0, concat_axis=0, tiled=True)  14.5 us
  transfers between devices with their start and end apart: 1, of which 0 were waited for; matrix products, arithmetic and copies ran while one was open for 0% of the time, Pallas kernels for 0%

profile of v8, /device:TPU:0, one launch (start us, length us, event | category | flops | bytes accessed | tf_op | source)
XLA Modules:
  0.0 120.1 jit_solution(551480035376463921)
XLA Ops:
  0.6 2.6 %shard_map.95 = f32[4,112,128]{2,1,0:T(8,128)} custom-call(f32[32,128]{1,0:T(8,128)} %coef_in.1, s32[64,128]{1,0:T(8,128)} %ca_in.1, s32[64,128]{1,0:T(8,128)} %cd_in.1, f32[64,128]{1,0:T(8,128)} %ta_in.1, f32[64,128]{1,0:T(8,128)} %td_in.1, f32[64,128]{1,0:T(8,128)} %height_in.1, s32[1,64]{1,0:T(1,128)} %bitcast.9), custom_call_target="tpu_custom_call" | custom-call | tf_op jit(solution)/shard_map/pallas_call | solution.py:583
  3.2 14.5 %all_to_all.50.packed = f32[4,112,128]{2,1,0:T(8,128)S(1)} all-to-all(f32[4,112,128]{2,1,0:T(8,128)} %shard_map.95), channel_id=1, replica_groups=mesh['asc'=8,'desc'=4] {'desc'}, dimensions={0} | all-to-all | bytes 458752 | tf_op jit(solution)/shard_map/all_to_all | solution.py:612
  17.7 0.0 copy-start
  17.7 0.7 copy-done
  18.4 1.9 %shard_map.96 = (f32[72,128]{1,0:T(8,128)S(1)}, bf16[8,256,1024]{2,1,0:T(8,128)(2,1)S(1)}, f32[32,128]{1,0:T(8,128)S(1)}, f32[64,128]{1,0:T(8,128)S(1)}, f32[8,56,128]{2,1,0:T(8,128)S(1)}) custom-call(f32[4,112,128]{2,1,0:T(8,128)S(1)} %all_to_all.50.packed, f32[32,128]{1,0:T(8,128)S(1)} %copy-done), custom_call_target="tpu_custom_call" | custom-call | tf_op jit(solution)/shard_map/pallas_call | solution.py:583
  20.3 10.1 %all_to_all.51.packed = f32[8,56,128]{2,1,0:T(8,128)S(1)} all-to-all(f32[8,56,128]{2,1,0:T(8,128)S(1)} %get-tuple-element.51), channel_id=1, replica_groups=mesh['asc'=8,'desc'=4] {'asc'}, dimensions={0} | all-to-all | bytes 458752 | tf_op jit(solution)/shard_map/all_to_all | solution.py:630
  30.4 3.2 %shard_map.97 = (f32[72,128]{1,0:T(8,128)S(1)}, bf16[8,256,1024]{2,1,0:T(8,128)(2,1)S(1)}, f32[32,128]{1,0:T(8,128)S(1)}, f32[64,128]{1,0:T(8,128)S(1)}, f32[64,...) custom-call(f32[8,56,128]{2,1,0:T(8,128)S(1)} %all_to_all.51.packed), custom_call_target="tpu_custom_call" | custom-call | tf_op jit(solution)/shard_map/pallas_call | solution.py:583
  33.6 7.5 %all_to_all.52.got = f32[8,2,8,128]{3,2,1,0:T(8,128)S(1)} all-to-all(f32[8,2,8,128]{3,2,1,0:T(8,128)S(1)} %get-tuple-element.52), channel_id=1, replica_groups=mesh['asc'=8,'desc'=4] {'asc'}, dimensions={0} | all-to-all | bytes 131072 | tf_op jit(solution)/shard_map/all_to_all | solution.py:630
  41.1 3.0 %shard_map.98 = (f32[64,128]{1,0:T(8,128)S(1)}, f32[64,128]{1,0:T(8,128)S(1)}, f32[64,128]{1,0:T(8,128)S(1)}, f32[32,128]{1,0:T(8,128)S(1)}, f32[32,128]{1,0:T(8...) custom-call(f32[8,2,8,128]{3,2,1,0:T(8,128)S(1)} %all_to_all.52.got, ...), custom_call_target="tpu_custom_call" | custom-call | tf_op jit(solution)/shard_map/pallas_call | solution.py:583
  44.1 7.6 %all_to_all.53.got = f32[8,2,8,128]{3,2,1,0:T(8,128)S(1)} all-to-all(f32[8,2,8,128]{3,2,1,0:T(8,128)S(1)} %get-tuple-element.57), channel_id=1, replica_groups=mesh['asc'=8,'desc'=4] {'asc'}, dimensions={0} | all-to-all | bytes 131072 | tf_op jit(solution)/shard_map/all_to_all | solution.py:630
  51.7 3.0 %shard_map.99 = (f32[64,128]{1,0:T(8,128)S(1)}, f32[64,128]{1,0:T(8,128)S(1)}, f32[32,128]{1,0:T(8,128)S(1)}, f32[32,128]{1,0:T(8,128)S(1)}, f32[64,128]{1,0:T(8,128)S(1)}, /*index=5*/f32[8,2,8,128]{3,2,1,0:T(8,128)S(1)}) custom-call(f32[8,2,8,128]{3,2,1,0:T(8,128)S(1)} %all_to_all.53.got, f32[64,128]{1,0:T(8,128)S(1)} %get-tuple-element.58.value_0, ...), custom_call_target="tpu_custom_call" | custom-call | tf_op jit(solution)/shard_map/pallas_call | solution.py:583
  54.7 7.6 %all_to_all.54.got = f32[8,2,8,128]{3,2,1,0:T(8,128)S(1)} all-to-all(f32[8,2,8,128]{3,2,1,0:T(8,128)S(1)} %get-tuple-element.63), channel_id=1, replica_groups=mesh['asc'=8,'desc'=4] {'asc'}, dimensions={0} | all-to-all | bytes 131072 | tf_op jit(solution)/shard_map/all_to_all | solution.py:630
  62.3 1.6 %shard_map.100 = (f32[64,128]{1,0:T(8,128)S(1)}, f32[64,128]{1,0:T(8,128)S(1)}, f32[32,128]{1,0:T(8,128)S(1)}, f32[64,128]{1,0:T(8,128)S(1)}, f32[32,1,128]{2,1,0:T(1,128)S(1)}) custom-call(f32[8,2,8,128]{3,2,1,0:T(8,128)S(1)} %all_to_all.54.got, f32[64,128]{1,0:T(8,128)S(1)} %get-tuple-element.64.value_1, f32[72,128]{1,0:T(8,128)S(1)} %get-tuple-element.54.meta, ...), custom_call_target="tpu_custom_call" | custom-call | tf_op jit(solution)/shard_map/pallas_call | solution.py:583
  63.9 9.3 %all_to_all.55.scalars = f32[32,1,128]{2,1,0:T(1,128)S(1)} all-to-all(f32[32,1,128]{2,1,0:T(1,128)S(1)} %get-tuple-element.71), channel_id=1, replica_groups=mesh['asc'=8,'desc'=4] {'asc','desc'}, dimensions={0} | all-to-all | bytes 32768 | tf_op jit(solution)/shard_map/all_to_all | solution.py:633
  73.2 1.7 %shard_map.101 = (f32[32,128]{1,0:T(8,128)S(1)}, f32[32,128]{1,0:T(8,128)S(1)}, f32[8,128]{1,0:T(8,128)S(1)}, f32[64,128]{1,0:T(8,128)S(1)}, f32[32,128]{1,0:T(8...) custom-call(f32[32,1,128]{2,1,0:T(1,128)S(1)} %all_to_all.55.scalars, ...), custom_call_target="tpu_custom_call" | custom-call | tf_op jit(solution)/shard_map/pallas_call | solution.py:583
  74.9 7.4 %all_to_all.56.got = f32[8,2,8,128]{3,2,1,0:T(8,128)S(1)} all-to-all(f32[8,2,8,128]{3,2,1,0:T(8,128)S(1)} %get-tuple-element.78), channel_id=1, replica_groups=mesh['asc'=8,'desc'=4] {'asc'}, dimensions={0} | all-to-all | bytes 131072 | tf_op jit(solution)/shard_map/all_to_all | solution.py:630
  82.3 3.0 %shard_map.102 = (f32[64,128]{1,0:T(8,128)S(1)}, f32[64,128]{1,0:T(8,128)S(1)}, f32[32,128]{1,0:T(8,128)S(1)}, f32[32,128]{1,0:T(8,128)S(1)}, f32[64,128]{1,0:T(8,128)S(1)}, /*index=5*/f32[8,2,8,128]{3,2,1,0:T(8,128)S(1)}) custom-call(f32[8,2,8,128]{3,2,1,0:T(8,128)S(1)} %all_to_all.56.got, f32[8,128]{1,0:T(8,128)S(1)} %get-tuple-element.79.shares, ...), custom_call_target="tpu_custom_call" | custom-call | tf_op jit(solution)/shard_map/pallas_call | solution.py:583
  85.3 7.6 %all_to_all.57.got = f32[8,2,8,128]{3,2,1,0:T(8,128)S(1)} all-to-all(f32[8,2,8,128]{3,2,1,0:T(8,128)S(1)} %get-tuple-element.85), channel_id=1, replica_groups=mesh['asc'=8,'desc'=4] {'asc'}, dimensions={0} | all-to-all | bytes 131072 | tf_op jit(solution)/shard_map/all_to_all | solution.py:630
  92.8 3.6 %shard_map.103 = (f32[64,128]{1,0:T(8,128)}, f32[64,128]{1,0:T(8,128)}, f32[32,128]{1,0:T(8,128)S(1)}, f32[32,128]{1,0:T(8,128)S(1)}, f32[64,128]{1,0:T(8,128)}, /*index=5*/f32[8,2,8,128]{3,2,1,0:T(8,128)S(1)}) custom-call(f32[8,2,8,128]{3,2,1,0:T(8,128)S(1)} %all_to_all.57.got, f32[64,128]{1,0:T(8,128)S(1)} %get-tuple-element.86.value_0, ...), custom_call_target="tpu_custom_call" | custom-call | tf_op jit(solution)/shard_map/pallas_call | solution.py:583
  96.5 7.6 %all_to_all.58.got = f32[8,2,8,128]{3,2,1,0:T(8,128)S(1)} all-to-all(f32[8,2,8,128]{3,2,1,0:T(8,128)S(1)} %get-tuple-element.89), channel_id=1, replica_groups=mesh['asc'=8,'desc'=4] {'asc'}, dimensions={0} | all-to-all | bytes 131072 | tf_op jit(solution)/shard_map/all_to_all | solution.py:630
  104.1 2.1 %shard_map.104 = (f32[64,128]{1,0:T(8,128)}, f32[64,128]{1,0:T(8,128)}, f32[32,128]{1,0:T(8,128)S(1)}, f32[64,128]{1,0:T(8,128)}, f32[32,1,128]{2,1,0:T(1,128)S(1)}) custom-call(f32[8,2,8,128]{3,2,1,0:T(8,128)S(1)} %all_to_all.58.got, f32[64,128]{1,0:T(8,128)S(1)} %get-tuple-element.90.value_1, f32[72,128]{1,0:T(8,128)S(1)} %get-tuple-element.59.meta, ...), custom_call_target="tpu_custom_call" | custom-call | tf_op jit(solution)/shard_map/pallas_call | solution.py:583
  106.2 0.7 collective-permute-start
  106.8 12.5 %all_to_all.59.scalars = f32[32,1,128]{2,1,0:T(1,128)S(1)} all-to-all(f32[32,1,128]{2,1,0:T(1,128)S(1)} %get-tuple-element.97), channel_id=1, replica_groups=mesh['asc'=8,'desc'=4] {'asc','desc'}, dimensions={0} | all-to-all | bytes 32768 | tf_op jit(solution)/shard_map/all_to_all | solution.py:633
  119.3 0.0 collective-permute-done.desc
  119.3 0.8 shard_map.105
  (1 shorter events, 0.0 us)
Async XLA Ops:
  17.7 0.7 copy-start
  106.2 13.1 %collective-permute-start = (f32[4,32,128]{2,1,0:T(8,128)S(1)}, f32[4,32,128]{2,1,0:T(8,128)S(1)}, u32[]{:S(2)}, u32[]{:S(2)}) collective-permute-start(f32[4,32,128]{2,1,0:T(8,128)S(1)} %pad_maximum_fusion), channel_id=1, source_target_pairs={{0,0},{8,1},{16,2},{24,3},{1,4},{9,5},{17,6},{25,7},{2,8},{10,9},{... | collective-permute-start | bytes 196616 | tf_op jit(solution)/shard_map/ppermute | solution.py:694
